TPU v7x, 32 devices: a whole 2x2x4 slice. The times are simulated.
32 devices in a mesh: rep: 2 (over core), fsdp: 16 (over z, y, x).
Axes of the slice: x: 2, y: 2, z: 4, core: 2. Of those that a mesh axis runs over, the one named last changes fastest.
Arguments:
- tokens: bfloat16 [4096, 1024], P(('rep', 'fsdp')), may hold values from -6 to 6
- segment_ids: int32 [32, 128], P(('rep', 'fsdp')), may hold values from 0 to 3, never falling along the last dimension, each value on 1 to 64 neighbouring positions
- norm_gain: float32 [1024], replicated, may hold values from 0.5 to 1.5
- in_weight: bfloat16 [1024, 4384], P('fsdp'), may hold values from -0.1875 to 0.1875
- conv_weight: float32 [4, 2304], replicated, may hold values from -3 to 3
- conv_bias: float32 [2304], replicated, may hold values from -3 to 3
- dt_bias: float32 [32], replicated, may hold values from -7 to -2.5
- a_log: float32 [32], replicated, may hold values from 0 to 2.5
- skip_gain: float32 [32], replicated, may hold values from 0.5 to 1.5
- gate_gain: float32 [2048], replicated, may hold values from 0.5 to 1.5
- out_weight: bfloat16 [2048, 1024], P('fsdp'), may hold values from -0.125 to 0.125
- cotangent: bfloat16 [4096, 1024], P(('rep', 'fsdp')), may hold values from -6 to 6
Outputs:
- block_out: bfloat16 [4096, 1024], P(('rep', 'fsdp'))
- d_tokens: float32 [4096, 1024], P(('rep', 'fsdp'))
- d_norm_gain: float32 [1024], replicated
- d_in_weight: float32 [1024, 4384], P('fsdp')
- d_conv_weight: float32 [4, 2304], replicated
- d_conv_bias: float32 [2304], replicated
- d_dt_bias: float32 [32], replicated
- d_a_log: float32 [32], replicated
- d_skip_gain: float32 [32], replicated
- d_gate_gain: float32 [2048], replicated
- d_out_weight: float32 [2048, 1024], P('fsdp')
Inputs may be any that keep to these rules, and one draw needn't show every extreme that they name: `segment_ids`: each row is one packed sequence; its segment numbers start at 0, never fall, rise by at most one from a position to the next, and each segment has at most 64 tokens.
All inputs are finite; a program needn't handle non-finite values.
Results may differ from a plain program's by a relative error of at most 0.0071.
Values may be sent and summed in bfloat16 or wider, within the bound.
No kernel may reach another device: no remote copies, remote signals or barrier semaphores. Data moves between devices by JAX's collectives and lax.ppermute only.
A program may use at most 128 MiB of HBM per device.

v0:
```python
import jax
import jax.numpy as jnp
from jax import lax
from jax.sharding import PartitionSpec as P

BLOCK = 64


epsilon = 1e-05
highest = lax.Precision.HIGHEST


def rms_normed(hidden, gain):
    factor = lax.rsqrt(jnp.mean(hidden * hidden, axis=-1, keepdims=True) + epsilon)
    return hidden * factor * gain


def mixer(projected, segments, conv_weight, conv_bias, dt_bias, a_log, skip_gain, gate_gain):
    seq_count = projected.shape[0]
    seq_len = projected.shape[1]
    inner_dim = gate_gain.shape[0]
    head_count = dt_bias.shape[0]
    conv_dim = conv_bias.shape[0]
    state_dim = (conv_dim - inner_dim) // 2
    head_dim = inner_dim // head_count
    kernel_len = conv_weight.shape[0]
    gate_part = projected[:, :, :inner_dim]
    signal = projected[:, :, inner_dim : inner_dim + conv_dim]
    step_raw = projected[:, :, inner_dim + conv_dim :]
    mixed_conv = conv_bias + conv_weight[kernel_len - 1] * signal
    for offset in range(1, kernel_len):
        earlier = jnp.pad(signal, ((0, 0), (offset, 0), (0, 0)))[:, :seq_len]
        earlier_seg = jnp.pad(segments, ((0, 0), (offset, 0)), constant_values=-1)[:, :seq_len]
        same_doc = (earlier_seg == segments).astype(jnp.float32)[:, :, None]
        mixed_conv = mixed_conv + conv_weight[kernel_len - 1 - offset] * earlier * same_doc
    activated = jax.nn.silu(mixed_conv)
    values = activated[:, :, :inner_dim].reshape(seq_count, seq_len, head_count, head_dim)
    in_state = activated[:, :, inner_dim : inner_dim + state_dim]
    out_state = activated[:, :, inner_dim + state_dim :]
    step_size = jax.nn.softplus(step_raw + dt_bias)
    log_decay = -step_size * jnp.exp(a_log)
    scaled = values * step_size[..., None]
    blocks = seq_len // BLOCK
    total = seq_count * blocks
    seg_block = segments.reshape(total, BLOCK)
    entry_seg = jnp.pad(segments, ((0, 0), (1, 0)), constant_values=-1)[:, :seq_len].reshape(
        total, BLOCK
    )[:, 0]
    cumul = jnp.cumsum(log_decay.reshape(total, BLOCK, head_count), axis=1)
    keys_blk = in_state.reshape(total, BLOCK, state_dim)
    query_blk = out_state.reshape(total, BLOCK, state_dim)
    value_blk = scaled.reshape(total, BLOCK, head_count, head_dim)
    scores = jnp.einsum("ktn,ksn->kts", query_blk, keys_blk, precision=highest)
    places = jnp.arange(BLOCK)
    visible = (places[:, None] >= places[None, :])[None] & (
        seg_block[:, :, None] == seg_block[:, None, :]
    )
    cumul_heads = jnp.swapaxes(cumul, 1, 2)
    spread = cumul_heads[:, :, :, None] - cumul_heads[:, :, None, :]
    visible_heads = visible[:, None]
    weights = (
        jnp.exp(jnp.where(visible_heads, spread, 0.0))
        * visible_heads.astype(jnp.float32)
        * scores[:, None]
    )
    inside = jnp.einsum("khts,kshp->kthp", weights, value_blk, precision=highest)
    same_last = (seg_block == seg_block[:, -1:]).astype(jnp.float32)
    tail_weight = jnp.exp(cumul[:, -1:, :] - cumul) * same_last[:, :, None]
    contrib = jnp.einsum(
        "kshp,ksn->khpn", value_blk * tail_weight[..., None], keys_blk, precision=highest
    )
    carry_keep = (
        jnp.exp(cumul[:, -1, :]) * (entry_seg == seg_block[:, -1]).astype(jnp.float32)[:, None]
    )
    contrib_seq = jnp.swapaxes(
        contrib.reshape(seq_count, blocks, head_count, head_dim, state_dim), 0, 1
    )
    keep_seq = jnp.swapaxes(carry_keep.reshape(seq_count, blocks, head_count), 0, 1)

    def advance(carried, scanned):
        added, factor = scanned
        return (factor[:, :, None, None] * carried + added, carried)

    start_state = jnp.zeros((seq_count, head_count, head_dim, state_dim), jnp.float32)
    final_state, entering = lax.scan(advance, start_state, (contrib_seq, keep_seq))
    entering = jnp.swapaxes(entering, 0, 1).reshape(total, head_count, head_dim, state_dim)
    reach = jnp.exp(cumul) * (seg_block == entry_seg[:, None]).astype(jnp.float32)[:, :, None]
    carried_out = (
        jnp.einsum("ktn,khpn->kthp", query_blk, entering, precision=highest) * reach[..., None]
    )
    result = (inside + carried_out).reshape(seq_count, seq_len, head_count, head_dim) + skip_gain[
        :, None
    ] * values
    result = result.reshape(seq_count, seq_len, inner_dim) * jax.nn.silu(gate_part)
    return rms_normed(result, gate_gain)


def per_device(
    tokens,
    segment_ids,
    norm_gain,
    in_weight,
    conv_weight,
    conv_bias,
    dt_bias,
    a_log,
    skip_gain,
    gate_gain,
    out_weight,
    cotangent,
):
    in_full, out_full = (
        lax.all_gather(in_weight, "fsdp", axis=0, tiled=True),
        lax.all_gather(out_weight, "fsdp", axis=0, tiled=True),
    )
    seq_count = segment_ids.shape[0]
    seq_len = segment_ids.shape[1]
    hidden = tokens.astype(jnp.float32)
    normed, norm_pullback = jax.vjp(rms_normed, hidden, norm_gain)
    normed_low = normed.astype(jnp.bfloat16)
    projected = jnp.dot(normed_low, in_full, preferred_element_type=jnp.float32)

    def middle(proj_rows, conv_w, conv_b, step_bias, decay_log, skip_w, gate_w):
        mixed = mixer(
            proj_rows.reshape(seq_count, seq_len, -1),
            segment_ids,
            conv_w,
            conv_b,
            step_bias,
            decay_log,
            skip_w,
            gate_w,
        )
        return mixed.reshape(seq_count * seq_len, -1)

    gated, mix_pullback = jax.vjp(
        middle, projected, conv_weight, conv_bias, dt_bias, a_log, skip_gain, gate_gain
    )
    gated_low = gated.astype(jnp.bfloat16)
    block_out = (hidden + jnp.dot(gated_low, out_full, preferred_element_type=jnp.float32)).astype(
        jnp.bfloat16
    )
    in_back, out_back = (in_full, out_full)
    d_gated = jnp.einsum("td,id->ti", cotangent, out_back, preferred_element_type=jnp.float32)
    d_out_full = jnp.einsum("ti,td->id", gated_low, cotangent, preferred_element_type=jnp.float32)
    d_projected, d_conv_weight, d_conv_bias, d_dt_bias, d_a_log, d_skip_gain, d_gate_gain = (
        mix_pullback(d_gated)
    )
    d_proj_low = d_projected.astype(jnp.bfloat16)
    d_normed = jnp.einsum("tj,dj->td", d_proj_low, in_back, preferred_element_type=jnp.float32)
    d_in_full = jnp.einsum("td,tj->dj", normed_low, d_proj_low, preferred_element_type=jnp.float32)
    d_hidden, d_norm_gain = norm_pullback(d_normed)
    d_tokens = cotangent.astype(jnp.float32) + d_hidden
    shard_in, shard_out = (
        lax.psum_scatter(d_in_full, "fsdp", scatter_dimension=0, tiled=True),
        lax.psum_scatter(d_out_full, "fsdp", scatter_dimension=0, tiled=True),
    )
    d_in_weight, d_out_weight = lax.psum((shard_in, shard_out), "rep")
    d_norm_gain, d_conv_weight, d_conv_bias, d_dt_bias, d_a_log, d_skip_gain, d_gate_gain = (
        lax.psum(
            (d_norm_gain, d_conv_weight, d_conv_bias, d_dt_bias, d_a_log, d_skip_gain, d_gate_gain),
            ("rep", "fsdp"),
        )
    )
    return (
        block_out,
        d_tokens,
        d_norm_gain,
        d_in_weight,
        d_conv_weight,
        d_conv_bias,
        d_dt_bias,
        d_a_log,
        d_skip_gain,
        d_gate_gain,
        d_out_weight,
    )


def solution(mesh):
    in_specs = (
        P(("rep", "fsdp"), None),
        P(("rep", "fsdp"), None),
        P(),
        P("fsdp", None),
        P(),
        P(),
        P(),
        P(),
        P(),
        P(),
        P("fsdp", None),
        P(("rep", "fsdp"), None),
    )
    out_specs = (
        P(("rep", "fsdp"), None),
        P(("rep", "fsdp"), None),
        P(),
        P("fsdp", None),
        P(),
        P(),
        P(),
        P(),
        P(),
        P(),
        P("fsdp", None),
    )
    return jax.shard_map(
        per_device, mesh=mesh, in_specs=in_specs, out_specs=out_specs, check_vma=False
    )
```

profile of v0, /device:TPU:0, one launch (start us, length us, event | category | flops | bytes accessed | tf_op | source)
XLA Modules:
  0.0 840.0 jit_solution(2882744091389612828)
XLA Ops:
  9.9 1.5 fusion.105
  14.4 1.1 fusion.83
  17.2 116.2 %all-gather.3.cloned.1.call-done = bf16[1024,4384]{1,0:T(8,128)(2,1)} async-done(((bf16[64,4384]{1,0:T(8,128)(2,1)}), bf16[1024,4384]{1,0:T(8,128)(2,1)}) %all-gather.3.cloned.1.call-update) | async-done | bytes 8978448 | tf_op jit(solution)/shard_map/all_gather | solution.py:113
  133.4 7.4 convolution_bitcast_fusion
  141.0 1.3 copy-done.9
  144.2 3.8 fusion.42
  148.0 1.1 slice.89
  149.6 2.5 reshape.478
  153.0 3.4 fusion.25
  157.1 3.6 while.34
  160.7 1.8 fusion.13
  162.6 3.9 bitcast_add_fusion.3
  166.5 3.0 copy.192
  169.6 3.8 reshape.484
  173.4 2.0 multiply_reduce_fusion.9
  176.4 4.6 fusion.110
  181.1 29.1 %all-gather.5.cloned.1.call-done = bf16[2048,1024]{1,0:T(8,128)(2,1)} async-done(((bf16[128,1024]{1,0:T(8,128)(2,1)}), bf16[2048,1024]{1,0:T(8,128)(2,1)}) %all-gather.5.cloned.1.call-update) | async-done | bytes 4194320 | tf_op jit(solution)/shard_map/all_gather | solution.py:114
  210.2 4.6 fusion.54
  214.8 3.7 multiply_reduce_fusion.7
  218.6 3.4 reshape.486
  222.0 4.2 copy.224
  226.2 5.0 fusion.24
  231.7 1.6 broadcast.249
  233.3 6.4 while.35
  237.2 1.1 bitcast_dynamic-update-slice_fusion.5
  239.8 5.1 multiply_reduce_fusion.1
  244.9 4.1 bitcast_add_fusion.2
  249.0 3.0 copy.198
  252.0 2.6 reshape.493
  254.6 3.4 reshape.488
  258.0 1.4 copy.200
  259.4 5.3 fusion.44
  264.8 5.3 fusion.35
  270.9 1.6 copy.206
  272.5 5.3 fusion.47
  281.3 2.7 multiply_reduce_fusion.2
  287.0 1.2 fusion.55
  288.3 1.6 multiply_reduce_fusion.8
  290.2 2.6 multiply_reduce_fusion.6
  292.8 1.5 multiply_multiply_fusion
  294.4 1.3 fusion.41
  295.7 7.8 fusion.88
  304.5 84.4 %reduce-scatter.5.cloned.1.call-done = f32[128,1024]{1,0:T(8,128)} async-done(((f32[2048,1024]{1,0:T(8,128)}), f32[128,1024]{1,0:T(8,128)}) %reduce-scatter.5.cloned.1.call-update) | async-done | bytes 524304 | tf_op jit(solution)/shard_map/reduce_scatter | solution.py:156
  389.0 382.7 %reduce-scatter.3.cloned.1.call-done = f32[64,4384]{1,0:T(8,128)} async-done(((f32[1024,4384]{1,0:T(8,128)}), f32[64,4384]{1,0:T(8,128)}) %reduce-scatter.3.cloned.1.call-update) | async-done | bytes 1122320 | tf_op jit(solution)/shard_map/reduce_scatter | solution.py:155
  771.7 6.8 fusion.81
  778.5 46.1 %all-reduce.21 = (f32[1024]{0:T(1024)}, f32[4,2304]{1,0:T(4,128)}, f32[2304]{0:T(1024)}, f32[32]{0:T(128)}, f32[32]{0:T(128)}, /*index=5*/f32[32]{0:T(128)}, f32[2048]{0:T(1024)}) all-reduce(f32[1024]{0:T(1024)S(1)} %get-tuple-element.323, f32[4,2304]{1,0:T(4,128)S(1)} %pad_add_fusion, ...), channel_id=1, replica_groups=mesh['rep'=2,'fsdp'=16] {'rep','fsdp'}, use_global_device_ids=true, to_apply=%region_19.20 | all-reduce | flops 14688 | bytes 117504 | tf_op jit(solution)/shard_map/psum | solution.py:160
  825.6 4.1 fusion.36
  829.8 2.4 copy.280
  (291 shorter events, 31.8 us)
Async XLA Ops:
  7.2 126.2 %all-gather.3.cloned.1.call-start = ((), (), s32[]{:S(2)}) async-start(), calls=%async_computation.2 | async-start | bytes 9748480 | tf_op jit(solution)/shard_map/all_gather | solution.py:113
  7.9 202.3 %all-gather.5.cloned.1.call-start = ((), (), s32[]{:S(2)}) async-start(), calls=%async_computation.3 | async-start | bytes 4456448 | tf_op jit(solution)/shard_map/all_gather | solution.py:114
  8.7 380.3 %reduce-scatter.5.cloned.1.call-start = ((), (), s32[]{:S(2)}) async-start(), calls=%async_computation.5 | async-start | bytes 8912896 | tf_op jit(solution)/shard_map/reduce_scatter | solution.py:156
  9.4 131.6 %copy-start.90 = (f32[32]{0:T(128)}, f32[32]{0:T(128)S(1)}, u32[]{:S(2)}) copy-start(f32[32]{0:T(128)S(1)} %exp.43) | copy-start | bytes 388
  13.1 129.7 %copy-start.87 = (f32[2]{0:T(128)}, f32[2]{0:T(128)S(1)}, u32[]{:S(2)}) copy-start(f32[2]{0:T(128)S(1)} %fusion.97) | copy-start | bytes 28
  14.3 129.9 %copy-start.60 = (f32[2304]{0:T(1024)}, f32[2304]{0:T(1024)S(1)}, u32[]{:S(2)}) copy-start(f32[2304]{0:T(1024)S(1)} %get-tuple-element.325) | copy-start | bytes 27652
  14.4 129.8 %copy-start.62 = (f32[2304]{0:T(1024)}, f32[2304]{0:T(1024)S(1)}, u32[]{:S(2)}) copy-start(f32[2304]{0:T(1024)S(1)} %get-tuple-element.326) | copy-start | bytes 27652
  14.4 129.8 %copy-start.64 = (f32[2304]{0:T(1024)}, f32[2304]{0:T(1024)S(1)}, u32[]{:S(2)}) copy-start(f32[2304]{0:T(1024)S(1)} %get-tuple-element.327) | copy-start | bytes 27652
  14.4 129.8 %copy-start.66 = (f32[2304]{0:T(1024)}, f32[2304]{0:T(1024)S(1)}, u32[]{:S(2)}) copy-start(f32[2304]{0:T(1024)S(1)} %get-tuple-element.328) | copy-start | bytes 27652
  15.5 125.4 %copy-start.95 = (f32[128]{0:T(128)}, f32[128]{0:T(128)S(1)}, u32[]{:S(2)}) copy-start(f32[128]{0:T(128)S(1)} %fusion.83) | copy-start | bytes 1540
  15.5 125.4 %copy-start.79 = (f32[128]{0:T(128)}, f32[128]{0:T(128)S(1)}, u32[]{:S(2)}) copy-start(f32[128]{0:T(128)S(1)} %fusion.101) | copy-start | bytes 1540
  16.4 127.8 %copy-start.81 = (f32[128]{0:T(128)}, f32[128]{0:T(128)S(1)}, u32[]{:S(2)}) copy-start(f32[128]{0:T(128)S(1)} %get-tuple-element.394) | copy-start | bytes 1540
  16.4 127.8 %copy-start.83 = (f32[128]{0:T(128)}, f32[128]{0:T(128)S(1)}, u32[]{:S(2)}) copy-start(f32[128]{0:T(128)S(1)} %get-tuple-element.395) | copy-start | bytes 1540
  16.4 127.8 %copy-start.85 = (f32[128]{0:T(128)}, f32[128]{0:T(128)S(1)}, u32[]{:S(2)}) copy-start(f32[128]{0:T(128)S(1)} %get-tuple-element.396) | copy-start | bytes 1540
  17.1 145.4 %copy-start.39 = (f32[2,64,64]{2,1,0:T(8,128)}, f32[2,64,64]{2,1,0:T(8,128)S(1)}, u32[]{:S(2)}) copy-start(f32[2,64,64]{2,1,0:T(8,128)S(1)} %get-tuple-element.391) | copy-start | bytes 98308
  17.1 145.4 %copy-start.55 = (pred[2,64,64]{2,1,0:T(8,128)(4,1)}, pred[2,64,64]{2,1,0:T(8,128)(4,1)S(1)}, u32[]{:S(2)}) copy-start(pred[2,64,64]{2,1,0:T(8,128)(4,1)S(1)} %get-tuple-element.390) | copy-start | bytes 24580
  142.3 5.8 copy-start.15
  142.4 5.7 copy-start.50
  142.5 20.1 %copy-start.32 = (f32[2,64,32]{1,2,0:T(8,128)}, f32[2,64,32]{1,2,0:T(8,128)S(1)}, u32[]{:S(2)}) copy-start(f32[2,64,32]{1,2,0:T(8,128)S(1)} %copy.180) | copy-start | bytes 49156
  142.8 9.4 %copy-start.30 = (f32[2,64,32]{1,2,0:T(8,128)}, f32[2,64,32]{1,2,0:T(8,128)S(1)}, u32[]{:S(2)}) copy-start(f32[2,64,32]{1,2,0:T(8,128)S(1)} %copy.187) | copy-start | bytes 49156
  142.8 19.7 %copy-start.34 = (f32[2,32,64]{2,1,0:T(8,128)}, f32[2,32,64]{2,1,0:T(8,128)S(1)}, u32[]{:S(2)}) copy-start(f32[2,32,64]{2,1,0:T(8,128)S(1)} %copy.183) | copy-start | bytes 49156
  149.5 6.9 copy-start.28
  149.6 11.1 %copy-start.26 = (f32[1,128,128]{2,1,0:T(8,128)}, f32[1,128,128]{2,1,0:T(8,128)S(1)}, u32[]{:S(2)}) copy-start(f32[1,128,128]{2,1,0:T(8,128)S(1)} %copy.185) | copy-start | bytes 196612
  153.0 9.6 %copy-start.43 = (f32[2,64,32]{1,2,0:T(8,128)}, f32[2,64,32]{1,2,0:T(8,128)S(1)}, u32[]{:S(2)}) copy-start(f32[2,64,32]{1,2,0:T(8,128)S(1)} %get-tuple-element.386) | copy-start | bytes 49156
  156.6 5.9 copy-start.37
  175.9 38.9 %copy-start.75 = (f32[128]{0:T(128)}, f32[128]{0:T(128)S(1)}, u32[]{:S(2)}) copy-start(f32[128]{0:T(128)S(1)} %fusion.102) | copy-start | bytes 1540
  181.0 590.6 %reduce-scatter.3.cloned.1.call-start = ((), (), s32[]{:S(2)}) async-start(), calls=%async_computation.4 | async-start | bytes 19496960 | tf_op jit(solution)/shard_map/reduce_scatter | solution.py:155
  181.0 33.7 %copy-start.98 = (f32[128]{0:T(128)S(1)}, f32[128]{0:T(128)}, u32[]{:S(2)}) copy-start(f32[128]{0:T(128)} %copy-done.97) | copy-start | bytes 1540
  231.7 8.0 copy-start.29
  239.7 5.2 copy-start.20
  239.7 5.2 copy-start.35
  239.7 5.1 copy-start.38
  259.3 5.4 copy-start.2
  259.3 5.4 copy-start.21
  259.3 5.4 copy-start.33
  259.3 5.4 copy-start.36
  259.3 5.4 copy-start.57
  264.7 7.7 copy-start.3
  272.5 5.3 copy-start.53
  272.5 6.3 copy-start.31
  272.5 6.3 copy-start.47
  281.3 5.7 copy-start.17
  303.5 468.1 %copy-start.99 = (f32[32]{0:T(128)S(1)}, f32[32]{0:T(128)}, u32[]{:S(2)}) copy-start(f32[32]{0:T(128)} %param.23) | copy-start | bytes 388
  303.6 526.2 %all-reduce.25.cloned.1.call-start = ((), (), s32[]{:S(2)}) async-start(), calls=%async_computation.6 | async-start | bytes 3342336 | tf_op jit(solution)/shard_map/psum | solution.py:158
  771.7 6.8 copy-start.69
  771.7 53.0 %copy-start.96 = (f32[128]{0:T(128)S(1)}, f32[128]{0:T(128)}, u32[]{:S(2)}) copy-start(f32[128]{0:T(128)} %copy-done.95) | copy-start | bytes 1540
  771.7 53.9 %copy-start.76 = (f32[128]{0:T(128)S(1)}, f32[128]{0:T(128)}, u32[]{:S(2)}) copy-start(f32[128]{0:T(128)} %copy-done.75) | copy-start | bytes 1540
  778.5 47.1 %copy-start.6 = (f32[1,128,2048]{1,2,0:T(8,128)S(1)}, f32[1,128,2048]{1,2,0:T(8,128)}, u32[]{:S(2)}) copy-start(f32[1,128,2048]{1,2,0:T(8,128)} %copy-done.4) | copy-start | bytes 3145732
  (61 other events, 160.7 us)
Sparse Core Ops, SparseCore 0:
  10.8 122.5 all-gather.2
  136.2 73.9 all-gather.4
  212.5 176.4 reduce-scatter.4
  391.1 380.4 reduce-scatter.2
  773.9 26.5 all-reduce.24
where the time goes:
time: 845 us; the launch traced here: 840 us
  waiting for transfers between devices  614 us (73%)
  matrix products  76 us (9%)
  local copies, waits for them, and re-layouts  55 us (7%)
  blocking collectives  46.1 us (5%)
  other arithmetic  32.8 us (4%)
  between operations  15.5 us (2%)
    reduce_scatter x1, waiting for transfers between devices, per_device(): lax.psum_scatter(d_in_full, 'fsdp', scatter_dimension=0, tiled=True)  383 us
    all_gather x1, waiting for transfers between devices, per_device(): lax.all_gather(in_weight, 'fsdp', axis=0, tiled=True)  116 us
    reduce_scatter x1, waiting for transfers between devices, per_device(): lax.psum_scatter(d_out_full, 'fsdp', scatter_dimension=0, tiled=True)  84.4 us
    psum x1, blocking collectives, per_device(): lax.psum((d_norm_gain, d_conv_weight, d_conv_bias, d_dt_bias, d_a_log, d_...  46.1 us
    all_gather x1, waiting for transfers between devices, per_device(): lax.all_gather(out_weight, 'fsdp', axis=0, tiled=True)  29.1 us
  transfers between devices with their start and end apart: 5, of which 4 were waited for; matrix products, arithmetic and copies ran while one was open for 18% of the time, Pallas kernels for 0%

commit v1 on v0

v1 whole, which is shorter than its diff:
```python
import functools

import jax
import jax.numpy as jnp
from jax import lax
from jax.experimental import pallas as pl
from jax.experimental.pallas import tpu as pltpu
from jax.sharding import PartitionSpec as P

epsilon = 1e-05
highest = lax.Precision.HIGHEST
f32 = jnp.float32
bf16 = jnp.bfloat16
LANES = 128
VMEM_LIMIT = 50 * 1024 * 1024
BOTH = ("rep", "fsdp")


def exact_dot(a, b, dims=((1,), (0,))):
    return lax.dot_general(a, b, (dims, ((), ())), precision=highest, preferred_element_type=f32)


def low_dot(a, b, dims=((1,), (0,))):
    return lax.dot_general(
        a.astype(bf16), b.astype(bf16), (dims, ((), ())), preferred_element_type=f32
    )


def iota(shape, dim):
    return lax.broadcasted_iota(jnp.int32, shape, dim)


def params(**kw):
    return pltpu.CompilerParams(vmem_limit_bytes=VMEM_LIMIT, **kw)


def in_vmem(n):
    return [pl.BlockSpec(memory_space=pltpu.VMEM)] * n


def in_smem(n):
    return [pl.BlockSpec(memory_space=pltpu.SMEM)] * n


def anywhere(n):
    return [pl.BlockSpec(memory_space=pl.ANY)] * n


def chunk_copies(pos_ref, chunks, whole, sems, inward):
    copies = []
    for at, chunk in enumerate(chunks):
        rows = chunk.shape[0]
        start = pl.multiple_of(pos_ref[at], 16)
        part = whole.at[pl.ds(start, rows)]
        source, target = (chunk, part) if inward else (part, chunk)
        copies.append(pltpu.make_async_copy(source, target, sems.at[at]))
    return copies


def silu_parts(v):
    sig = 1.0 / (1.0 + jnp.exp(-v))
    return sig, v * sig


def conv_block(proj_ref, masks_ref, cw_ref, cb_ref, inner, at):
    signal = proj_ref[:, pl.ds(pl.multiple_of(inner + at * LANES, LANES), LANES)]
    lanes = pl.ds(pl.multiple_of(at * LANES, LANES), LANES)
    taps = cw_ref.shape[0]
    mixed = cb_ref[:, lanes] + cw_ref[taps - 1 : taps, lanes] * signal
    for offset in range(1, taps):
        earlier = pltpu.roll(signal, offset, 0) * masks_ref[offset - 1]
        mixed = mixed + cw_ref[taps - 1 - offset : taps - offset, lanes] * earlier
    return signal, mixed


def decay_prep(proj_ref, heads_ref, inner, head_dim, stepe_ref, cume_ref, cumt_ref):
    tokens, width = proj_ref.shape
    raw = proj_ref[:, width - LANES :] + heads_ref[0:1, :]
    step = jnp.maximum(raw, 0.0) + jnp.log1p(jnp.exp(-jnp.abs(raw)))
    decay = -step * jnp.exp(heads_ref[1:2, :])
    lower = (iota((LANES, LANES), 0) >= iota((LANES, LANES), 1)).astype(f32)
    spread = (
        iota((LANES, inner), 1) // head_dim == iota((LANES, inner), 0)
    ).astype(f32)
    stepe_ref[...] = exact_dot(step, spread)
    for seq in range(tokens // LANES):
        rows = slice(seq * LANES, (seq + 1) * LANES)
        cumul = exact_dot(lower, decay[rows])
        cume_ref[rows, :] = exact_dot(cumul, spread)
        turned = cumul.T
        for pair in range(inner // LANES):
            cumt_ref[pair, 0:2, rows] = turned[2 * pair : 2 * pair + 2]
    return raw, step, decay


def pair_weights(cume_ref, cumt_ref, vis_ref, rows, lanes, pair, half):
    cols = cume_ref[rows, lanes]
    seen = vis_ref[rows, :] > 0.5
    first, second = cumt_ref[pair, 0:1, rows], cumt_ref[pair, 1:2, rows]
    fade_a = jnp.exp(jnp.where(seen, cols[:, 0:1] - first, -1e30))
    fade_b = jnp.exp(jnp.where(seen, cols[:, half : half + 1] - second, -1e30))
    return fade_a, fade_b


def split_heads(block, half):
    lane = iota(block.shape, 1)
    return jnp.concatenate(
        [jnp.where(lane < half, block, 0.0), jnp.where(lane >= half, block, 0.0)], axis=0
    )


def forward_kernel(
    chunk_count, inner, head_dim,
    pos_ref, tok_ref, gain_ref, masks_ref, vis_ref, cw_ref, cb_ref, heads_ref, skip_ref, *rest,
):
    chunks = rest[:chunk_count]
    normed_ref, proj_ref, mixer_ref, sq_ref, w_ref, act_ref, stepe_ref, cume_ref, cumt_ref, score_ref, sems = (
        rest[chunk_count:]
    )
    copies = chunk_copies(pos_ref, chunks, w_ref, sems, True)
    for copy in copies:
        copy.start()
    hidden = tok_ref[...].astype(f32)
    factor = lax.rsqrt(jnp.mean(hidden * hidden, axis=-1, keepdims=True) + epsilon)
    normed_ref[...] = (hidden * factor * gain_ref[...]).astype(bf16)
    for copy in copies:
        copy.wait()
    tokens, width = proj_ref.shape
    for start in range(0, width, 512):
        end = min(start + 512, width)
        proj_ref[:, start:end] = jnp.dot(
            normed_ref[...], w_ref[:, start:end], preferred_element_type=f32
        )
    decay_prep(proj_ref, heads_ref, inner, head_dim, stepe_ref, cume_ref, cumt_ref)

    def convolve(at, _):
        signal, mixed = conv_block(proj_ref, masks_ref, cw_ref, cb_ref, inner, at)
        act_ref[:, pl.ds(pl.multiple_of(at * LANES, LANES), LANES)] = silu_parts(mixed)[1]
        return 0

    lax.fori_loop(0, act_ref.shape[1] // LANES, convolve, 0)
    seqs = tokens // LANES
    for seq in range(seqs):
        rows = slice(seq * LANES, (seq + 1) * LANES)
        keys = act_ref[rows, inner : inner + LANES]
        queries = act_ref[rows, inner + LANES :]
        score_ref[rows, :] = exact_dot(queries, keys, ((1,), (1,)))
    sq_ref[...] = jnp.zeros_like(sq_ref)

    def scan(pair, _):
        lanes = pl.ds(pl.multiple_of(pair * LANES, LANES), LANES)
        skip = skip_ref[:, lanes]
        for seq in range(seqs):
            rows = slice(seq * LANES, (seq + 1) * LANES)
            fade_a, fade_b = pair_weights(cume_ref, cumt_ref, vis_ref, rows, lanes, pair, head_dim)
            score = score_ref[rows, :]
            weights = jnp.concatenate([fade_a * score, fade_b * score], axis=1)
            values = act_ref[rows, lanes]
            scaled = split_heads(values * stepe_ref[rows, lanes], head_dim)
            mixed = low_dot(weights, scaled) + skip * values
            mixer_ref[rows, lanes] = mixed
            product = mixed * silu_parts(proj_ref[rows, lanes])[1]
            sq_ref[rows, :] += product * product
        return 0

    lax.fori_loop(0, inner // LANES, scan, 0)
    total = jnp.sum(sq_ref[...], axis=1, keepdims=True)
    sq_ref[...] = jnp.broadcast_to(total, sq_ref.shape)


def gated_kernel(
    chunk_count, inner, full_inner,
    pos_ref, proj_ref, mixer_ref, sq_ref, gain_ref, cot_ref, *rest,
):
    gated_ref = rest[0]
    chunks = rest[1 : 1 + chunk_count]
    grad_ref, sems = rest[1 + chunk_count :]
    factor = lax.rsqrt(sq_ref[...][:, 0:1] / full_inner + epsilon)
    for start in range(0, inner, LANES):
        lanes = slice(start, start + LANES)
        product = mixer_ref[:, lanes] * silu_parts(proj_ref[:, lanes])[1]
        gated_ref[:, lanes] = (product * factor * gain_ref[:, lanes]).astype(bf16)
    for start in range(0, inner, 256):
        lanes = slice(start, start + 256)
        grad_ref[lanes, :] = low_dot(gated_ref[:, lanes], cot_ref[...], ((0,), (0,))).astype(bf16)
    copies = chunk_copies(pos_ref, chunks, grad_ref, sems, False)
    for copy in copies:
        copy.start()
    for copy in copies:
        copy.wait()


def out_kernel(
    chunk_count, inner,
    pos_ref, proj_ref, mixer_ref, gain_ref, cot_ref, gated_ref, *rest,
):
    chunks = rest[:chunk_count]
    dgated_ref, cross_ref, block_ref, w_ref, sems = rest[chunk_count:]
    copies = chunk_copies(pos_ref, chunks, w_ref, sems, True)
    for copy in copies:
        copy.start()
    for copy in copies:
        copy.wait()
    cross = jnp.zeros(cross_ref.shape, f32)
    for start in range(0, inner, 256):
        lanes = slice(start, start + 256)
        dgated_ref[:, lanes] = low_dot(cot_ref[...], w_ref[lanes, :], ((1,), (1,)))
    for start in range(0, inner, LANES):
        lanes = slice(start, start + LANES)
        product = mixer_ref[:, lanes] * silu_parts(proj_ref[:, lanes])[1]
        cross = cross + product * gain_ref[:, lanes] * dgated_ref[:, lanes]
    cross_ref[...] = jnp.broadcast_to(jnp.sum(cross, axis=1, keepdims=True), cross.shape)
    block_ref[...] = jnp.dot(gated_ref[...], w_ref[...], preferred_element_type=f32)


def backward_kernel(
    chunk_count, inner, head_dim, full_inner,
    pos_ref, normed_ref, proj_ref, mixer_ref, dgated_ref, sq_ref, cross_ref, gain_ref,
    masks_ref, vis_ref, cw_ref, cb_ref, heads_ref, skip_ref, *rest,
):
    dproj_ref, small_ref = rest[:2]
    chunks = rest[2 : 2 + chunk_count]
    (act_ref, stepe_ref, cume_ref, cumt_ref, score_ref, dscore_ref, dact_ref, dstep_ref,
     rowsum_ref, colsum_ref, turned_ref, dskip_ref, grad_ref, sems) = rest[2 + chunk_count :]
    tokens, width = proj_ref.shape
    seqs = tokens // LANES
    raw, step, decay = decay_prep(
        proj_ref, heads_ref, inner, head_dim, stepe_ref, cume_ref, cumt_ref
    )
    small_ref[...] = jnp.zeros_like(small_ref)

    def convolve(at, _):
        signal, mixed = conv_block(proj_ref, masks_ref, cw_ref, cb_ref, inner, at)
        act_ref[:, pl.ds(pl.multiple_of(at * LANES, LANES), LANES)] = silu_parts(mixed)[1]
        return 0

    lax.fori_loop(0, act_ref.shape[1] // LANES, convolve, 0)
    for seq in range(seqs):
        rows = slice(seq * LANES, (seq + 1) * LANES)
        keys = act_ref[rows, inner : inner + LANES]
        queries = act_ref[rows, inner + LANES :]
        score_ref[rows, :] = exact_dot(queries, keys, ((1,), (1,)))
    dscore_ref[...] = jnp.zeros_like(dscore_ref)
    dstep_ref[...] = jnp.zeros_like(dstep_ref)
    rowsum_ref[...] = jnp.zeros_like(rowsum_ref)
    turned_ref[...] = jnp.zeros_like(turned_ref)
    dskip_ref[...] = jnp.zeros_like(dskip_ref)
    factor = lax.rsqrt(sq_ref[...] / full_inner + epsilon)
    pull = factor * factor * factor * cross_ref[...] / full_inner

    def scan(pair, _):
        lanes = pl.ds(pl.multiple_of(pair * LANES, LANES), LANES)
        skip = skip_ref[:, lanes]
        gain = gain_ref[:, lanes]
        collect = (
            iota((LANES, LANES), 0) // head_dim + 2 * pair == iota((LANES, LANES), 1)
        ).astype(f32)
        dgain = jnp.zeros((1, LANES), f32)
        dskip = jnp.zeros((1, LANES), f32)
        for seq in range(seqs):
            rows = slice(seq * LANES, (seq + 1) * LANES)
            gate = proj_ref[rows, lanes]
            sig, gate_act = silu_parts(gate)
            mixed = mixer_ref[rows, lanes]
            product = mixed * gate_act
            dgated = dgated_ref[rows, lanes]
            dproduct = factor[rows] * gain * dgated - product * pull[rows]
            dgain = dgain + jnp.sum(dgated * product * factor[rows], axis=0, keepdims=True)
            dgate = dproduct * mixed * (sig * (1.0 + gate * (1.0 - sig)))
            dproj_ref[rows, lanes] = dgate.astype(bf16)
            dmixed = dproduct * gate_act
            values = act_ref[rows, lanes]
            stepe = stepe_ref[rows, lanes]
            dskip = dskip + jnp.sum(dmixed * values, axis=0, keepdims=True)
            fade_a, fade_b = pair_weights(cume_ref, cumt_ref, vis_ref, rows, lanes, pair, head_dim)
            score = score_ref[rows, :]
            weights_a, weights_b = fade_a * score, fade_b * score
            dsplit = split_heads(dmixed, head_dim)
            dweights = low_dot(dsplit, values * stepe, ((1,), (1,)))
            dweights_a, dweights_b = dweights[:LANES], dweights[LANES:]
            dscore_ref[rows, :] += dweights_a * fade_a + dweights_b * fade_b
            spread_a, spread_b = dweights_a * weights_a, dweights_b * weights_b
            lane = iota((LANES, LANES), 1)
            rowsum_ref[rows, :] += jnp.where(
                lane == 2 * pair,
                jnp.sum(spread_a, axis=1, keepdims=True),
                jnp.where(lane == 2 * pair + 1, jnp.sum(spread_b, axis=1, keepdims=True), 0.0),
            )
            colsum_ref[pair, 0:1, rows] = jnp.sum(spread_a, axis=0, keepdims=True)
            colsum_ref[pair, 1:2, rows] = jnp.sum(spread_b, axis=0, keepdims=True)
            weights = jnp.concatenate([weights_a, weights_b], axis=0)
            dscaled = low_dot(weights, dsplit, ((0,), (0,)))
            dact_ref[rows, lanes] = dscaled * stepe + skip * dmixed
            dstep_ref[rows, :] += exact_dot(dscaled * values, collect)
        small_ref[5:6, lanes] = dgain
        dskip_ref[0:1, lanes] = dskip
        return 0

    lax.fori_loop(0, inner // LANES, scan, 0)
    for pair in range(inner // LANES):
        turned_ref[2 * pair : 2 * pair + 2, :] = colsum_ref[pair, 0:2, :]
    upper = (iota((LANES, LANES), 0) <= iota((LANES, LANES), 1)).astype(f32)
    rate = jnp.exp(heads_ref[1:2, :])
    ddt = jnp.zeros((1, LANES), f32)
    dalog = jnp.zeros((1, LANES), f32)
    for seq in range(seqs):
        rows = slice(seq * LANES, (seq + 1) * LANES)
        keys = act_ref[rows, inner : inner + LANES]
        queries = act_ref[rows, inner + LANES :]
        dscore = dscore_ref[rows, :]
        dact_ref[rows, inner : inner + LANES] = exact_dot(dscore, queries, ((0,), (0,)))
        dact_ref[rows, inner + LANES :] = exact_dot(dscore, keys)
        dcumul = rowsum_ref[rows, :] - turned_ref[:, rows].T
        ddecay = exact_dot(upper, dcumul)
        dalog = dalog + jnp.sum(ddecay * decay[rows], axis=0, keepdims=True)
        dstep = dstep_ref[rows, :] - ddecay * rate
        draw = dstep / (1.0 + jnp.exp(-raw[rows]))
        ddt = ddt + jnp.sum(draw, axis=0, keepdims=True)
        dproj_ref[rows, width - LANES :] = draw.astype(bf16)
    gather = (
        iota((inner, LANES), 0) // head_dim == iota((inner, LANES), 1)
    ).astype(f32)
    dskip_heads = exact_dot(dskip_ref[...], gather)
    small_ref[6:7, 0:LANES] = ddt
    small_ref[6:7, LANES : 2 * LANES] = dalog
    small_ref[6:7, 2 * LANES : 3 * LANES] = dskip_heads[0:1]

    def convolve_back(at, _):
        lanes = pl.ds(pl.multiple_of(at * LANES, LANES), LANES)
        signal, mixed = conv_block(proj_ref, masks_ref, cw_ref, cb_ref, inner, at)
        sig, _unused = silu_parts(mixed)
        dmixed = dact_ref[:, lanes] * (sig * (1.0 + mixed * (1.0 - sig)))
        taps = cw_ref.shape[0]
        small_ref[taps : taps + 1, lanes] = jnp.sum(dmixed, axis=0, keepdims=True)
        small_ref[taps - 1 : taps, lanes] = jnp.sum(dmixed * signal, axis=0, keepdims=True)
        dsignal = cw_ref[taps - 1 : taps, lanes] * dmixed
        for offset in range(1, taps):
            masked = dmixed * masks_ref[offset - 1]
            place = taps - 1 - offset
            small_ref[place : place + 1, lanes] = jnp.sum(
                masked * pltpu.roll(signal, offset, 0), axis=0, keepdims=True
            )
            dsignal = dsignal + cw_ref[place : place + 1, lanes] * pltpu.roll(
                masked, tokens - offset, 0
            )
        dproj_ref[:, pl.ds(pl.multiple_of(inner + at * LANES, LANES), LANES)] = dsignal.astype(bf16)
        return 0

    lax.fori_loop(0, act_ref.shape[1] // LANES, convolve_back, 0)
    for start in range(0, width, 512):
        lanes = slice(start, min(start + 512, width))
        grad_ref[:, lanes] = low_dot(normed_ref[...], dproj_ref[:, lanes], ((0,), (0,))).astype(bf16)
    copies = chunk_copies(pos_ref, chunks, grad_ref, sems, False)
    for copy in copies:
        copy.start()
    for copy in copies:
        copy.wait()


def dnormed_kernel(chunk_count, pos_ref, dproj_ref, *rest):
    chunks = rest[:chunk_count]
    dnormed_ref, w_ref, sems = rest[chunk_count:]
    copies = chunk_copies(pos_ref, chunks, w_ref, sems, True)
    for copy in copies:
        copy.start()
    for copy in copies:
        copy.wait()
    for start in range(0, w_ref.shape[0], 256):
        lanes = slice(start, start + 256)
        dnormed_ref[:, lanes] = low_dot(dproj_ref[...], w_ref[lanes, :], ((1,), (1,)))


def tail_kernel(tok_ref, cot_ref, gain_ref, mine_ref, other_ref, dtok_ref, dgain_ref):
    hidden = tok_ref[...].astype(f32)
    factor = lax.rsqrt(jnp.mean(hidden * hidden, axis=-1, keepdims=True) + epsilon)
    dnormed = mine_ref[...] + other_ref[...]
    dgain_ref[...] = jnp.broadcast_to(
        jnp.sum(dnormed * hidden * factor, axis=0, keepdims=True), dgain_ref.shape
    )
    scaled = dnormed * gain_ref[...]
    pull = jnp.mean(scaled * hidden, axis=-1, keepdims=True) * factor * factor * factor
    dtok_ref[...] = cot_ref[...].astype(f32) + scaled * factor - hidden * pull


class Links:
    first, second = (1, 2), (2, 1)

    def __init__(self, reps, chips):
        self.reps, self.chips = reps, chips
        self.paired = reps == 2 and chips == 16
        self.rep = lax.axis_index("rep")
        self.chip = lax.axis_index("fsdp")

    def exchange(self, x, masks):
        pairs = [
            (core * self.chips + chip, core * self.chips + (chip ^ masks[core]))
            for core in range(self.reps)
            for chip in range(self.chips)
        ]
        return lax.ppermute(x, BOTH, pairs)

    def sources(self):
        if not self.paired:
            return None
        one = jnp.where(self.rep == 0, self.first[0], self.first[1])
        two = jnp.where(self.rep == 0, self.second[0], self.second[1])
        places = [0 * one, one, two, 0 * one + 3]
        return jnp.stack([self.chip ^ (4 * slot) ^ place for slot in range(4) for place in places])

    def gather_rows(self, x):
        if not self.paired:
            return [lax.all_gather(x, "fsdp", axis=0, tiled=True)]
        chunks = []
        for slot in range(4):
            block = self.exchange(x, (4 * slot, 4 * slot)) if slot else x
            near = self.exchange(block, self.first)
            side = self.exchange(block, self.second)
            far = self.exchange(near, self.second)
            chunks += [block, near, side, far]
        return chunks

    def grad_shapes(self, rows, width):
        if not self.paired:
            return [jax.ShapeDtypeStruct((rows, width), bf16)]
        return [jax.ShapeDtypeStruct((rows // self.chips, width), bf16)] * self.chips

    def scatter_rows(self, chunks):
        if not self.paired:
            return lax.psum_scatter(chunks[0], "fsdp", scatter_dimension=0, tiled=True).astype(f32)
        total = None
        for slot in (3, 2, 1, 0):
            own, near, side, far = chunks[4 * slot : 4 * slot + 4]
            near = near.astype(f32) + self.exchange(far, self.second).astype(f32)
            own = own.astype(f32) + self.exchange(side, self.second).astype(f32)
            own = own + self.exchange(near.astype(bf16), self.first).astype(f32)
            if slot:
                own = self.exchange(own.astype(bf16), (4 * slot, 4 * slot)).astype(f32)
            total = own if total is None else total + own
        return total

    def swap(self, x):
        return lax.ppermute(x, "rep", [(0, 1), (1, 0)])

    def from_reps(self, x):
        if self.reps == 2:
            other = self.swap(x)
            return [jnp.where(self.rep == 0, x, other), jnp.where(self.rep == 0, other, x)]
        whole = lax.all_gather(x, "rep", axis=0)
        return [whole[at] for at in range(self.reps)]

    def sum_reps(self, x):
        return x + self.swap(x) if self.reps == 2 else lax.psum(x, "rep")

    def own_rows(self, x):
        rows = x.shape[0] // self.reps
        if self.reps == 2:
            mine = lax.dynamic_slice_in_dim(x, self.rep * rows, rows, 0)
            theirs = lax.dynamic_slice_in_dim(x, (1 - self.rep) * rows, rows, 0)
            return mine, self.swap(theirs)
        mine = lax.psum_scatter(x, "rep", scatter_dimension=0, tiled=True)
        return mine, jnp.zeros_like(mine)

    def sum_chips(self, x):
        if not self.paired:
            return lax.psum(x, "fsdp")
        for step in (1, 4):
            one, two, three = (self.exchange(x, (at * step, at * step)) for at in (1, 2, 3))
            x = (x + one) + (two + three)
        return x


def per_device(
    reps, chips,
    tokens, segment_ids, norm_gain, in_weight, conv_weight, conv_bias, dt_bias, a_log, skip_gain,
    gate_gain, out_weight, cotangent,
):
    links = Links(reps, chips)
    rep, chip = links.rep, links.chip
    full_inner, full_heads = gate_gain.shape[0], dt_bias.shape[0]
    conv_dim, taps = conv_bias.shape[0], conv_weight.shape[0]
    model = norm_gain.shape[0]
    state = (conv_dim - full_inner) // 2
    inner, heads = full_inner // reps, full_heads // reps
    head_dim = full_inner // full_heads
    rows_in, rows_out = in_weight.shape[0], out_weight.shape[0]
    conv_local = inner + 2 * state
    width = inner + conv_local + LANES
    own_tokens = tokens.shape[0]
    total = own_tokens * reps

    def columns(x, start, size):
        return lax.dynamic_slice_in_dim(x, start, size, x.ndim - 1)

    own_in = jnp.concatenate(
        [
            columns(in_weight, rep * inner, inner),
            columns(in_weight, full_inner + rep * inner, inner),
            in_weight[:, 2 * full_inner : full_inner + conv_dim],
            columns(in_weight, full_inner + conv_dim + rep * heads, heads),
            jnp.zeros((rows_in, LANES - heads), bf16),
        ],
        axis=1,
    )
    in_chunks = links.gather_rows(own_in)
    sources = links.sources()
    if links.paired:
        half = rows_out // 2
        away = lax.dynamic_slice_in_dim(out_weight, (1 - rep) * half, half, 0)
        kept = lax.dynamic_slice_in_dim(out_weight, rep * half, half, 0)
        moves = [(at, at + 8) for at in range(8)] + [(chips + at + 8, chips + at) for at in range(8)]
        came = lax.ppermute(away, BOTH, moves)
        holds = (rep == 0) == (chip < 8)
        own_out = jnp.where(holds, kept, came)
        in_pos = (sources * rows_in).astype(jnp.int32)
        out_pos = ((2 * (sources % 8) + sources // 8) * half).astype(jnp.int32)
        out_chunks = links.gather_rows(own_out)
    else:
        in_pos = out_pos = jnp.zeros((1,), jnp.int32)
        out_full = lax.all_gather(out_weight, "fsdp", axis=0, tiled=True)
        out_chunks = [lax.dynamic_slice_in_dim(out_full, rep * inner, inner, 0)]
    count = len(in_chunks)

    chip_tokens = jnp.concatenate(links.from_reps(tokens), axis=0)
    chip_cot = jnp.concatenate(links.from_reps(cotangent), axis=0)
    segments = jnp.concatenate(links.from_reps(segment_ids), axis=0)
    seq_count, seq_len = segments.shape
    masks = []
    for offset in range(1, taps):
        earlier = jnp.pad(segments, ((0, 0), (offset, 0)), constant_values=-1)[:, :seq_len]
        same = (earlier == segments).astype(f32).reshape(total, 1)
        masks.append(jnp.broadcast_to(same, (total, LANES)))
    masks = jnp.stack(masks)
    places = jnp.arange(seq_len)
    visible = (
        (places[:, None] >= places[None, :])[None] & (segments[:, :, None] == segments[:, None, :])
    ).astype(f32).reshape(total, seq_len)

    def local_conv(x):
        return jnp.concatenate([columns(x, rep * inner, inner), x[..., full_inner:]], axis=-1)

    conv_w, conv_b = local_conv(conv_weight), local_conv(conv_bias[None])

    def lane_row(x):
        return jnp.pad(columns(x, rep * heads, heads), (0, LANES - heads))

    head_rows = jnp.pad(jnp.stack([lane_row(dt_bias), lane_row(a_log)]), ((0, 6), (0, 0)))
    skip = jnp.repeat(columns(skip_gain, rep * heads, heads), head_dim)[None]
    gate_g = columns(gate_gain, rep * inner, inner)[None]
    norm_g = norm_gain[None]

    def arr(*shape, dtype=f32):
        return jax.ShapeDtypeStruct(shape, dtype)

    def vmem(*shape, dtype=f32):
        return pltpu.VMEM(shape, dtype)

    sems = pltpu.SemaphoreType.DMA((count,))
    normed, projected, mixed, squares = pl.pallas_call(
        functools.partial(forward_kernel, count, inner, head_dim),
        out_shape=[arr(total, model, dtype=bf16), arr(total, width), arr(total, inner), arr(total, LANES)],
        in_specs=in_smem(1) + in_vmem(8) + anywhere(count),
        out_specs=in_vmem(4),
        scratch_shapes=[
            vmem(model, width, dtype=bf16), vmem(total, conv_local), vmem(total, inner),
            vmem(total, inner), vmem(inner // LANES, 8, total), vmem(total, LANES), sems,
        ],
        compiler_params=params(),
        name="forward",
    )(in_pos, chip_tokens, norm_g, masks, visible, conv_w, conv_b, head_rows, skip, *in_chunks)
    squares = links.sum_reps(squares)
    out_shapes = links.grad_shapes(inner, model)
    gated, *out_grads = pl.pallas_call(
        functools.partial(gated_kernel, count, inner, full_inner),
        out_shape=[arr(total, inner, dtype=bf16)] + out_shapes,
        in_specs=in_smem(1) + in_vmem(5),
        out_specs=in_vmem(1) + anywhere(count),
        scratch_shapes=[vmem(inner, model, dtype=bf16), sems],
        compiler_params=params(),
        name="gated",
    )(out_pos, projected, mixed, squares, gate_g, chip_cot)
    d_gated, cross, block_part = pl.pallas_call(
        functools.partial(out_kernel, count, inner),
        out_shape=[arr(total, inner), arr(total, LANES), arr(total, model)],
        in_specs=in_smem(1) + in_vmem(5) + anywhere(count),
        out_specs=in_vmem(3),
        scratch_shapes=[vmem(inner, model, dtype=bf16), sems],
        compiler_params=params(),
        name="out",
    )(out_pos, projected, mixed, gate_g, chip_cot, gated, *out_chunks)
    cross = links.sum_reps(cross)
    in_shapes = links.grad_shapes(model, width)
    d_proj, small, *in_grads = pl.pallas_call(
        functools.partial(backward_kernel, count, inner, head_dim, full_inner),
        out_shape=[arr(total, width, dtype=bf16), arr(8, conv_local)] + in_shapes,
        in_specs=in_smem(1) + in_vmem(13),
        out_specs=in_vmem(2) + anywhere(count),
        scratch_shapes=[
            vmem(total, conv_local), vmem(total, inner), vmem(total, inner), vmem(inner // LANES, 8, total),
            vmem(total, LANES), vmem(total, LANES), vmem(total, conv_local), vmem(total, LANES),
            vmem(total, LANES), vmem(inner // LANES, 8, total), vmem(LANES, total), vmem(8, inner), vmem(model, width, dtype=bf16), sems,
        ],
        compiler_params=params(),
        name="backward",
    )(in_pos, normed, projected, mixed, d_gated, squares, cross, gate_g, masks, visible, conv_w, conv_b,
      head_rows, skip)

    out_sum = links.scatter_rows(out_grads)
    in_sum = links.scatter_rows(in_grads)
    d_normed = pl.pallas_call(
        functools.partial(dnormed_kernel, count),
        out_shape=arr(total, model),
        in_specs=in_smem(1) + in_vmem(1) + anywhere(count),
        out_specs=in_vmem(1)[0],
        scratch_shapes=[vmem(model, width, dtype=bf16), sems],
        compiler_params=params(),
        name="dnormed",
    )(in_pos, d_proj, *in_chunks)
    d_normed_a, d_normed_b = links.own_rows(d_normed)
    d_tokens, d_gain = pl.pallas_call(
        tail_kernel,
        out_shape=[arr(own_tokens, model), arr(8, model)],
        in_specs=in_vmem(5),
        out_specs=in_vmem(2),
        compiler_params=params(),
        name="tail",
    )(tokens, cotangent, norm_g, d_normed_a, d_normed_b)
    block_a, block_b = links.own_rows(block_part)
    block_out = (tokens.astype(f32) + (block_a + block_b)).astype(bf16)

    small = links.sum_chips(small)
    d_norm_gain = links.sum_chips(links.sum_reps(d_gain))[0]
    smalls = links.from_reps(small)

    def join(start, end, row=slice(None)):
        return jnp.concatenate([part[row, start:end] for part in smalls], axis=1)

    shared = sum(part[:, inner:] for part in smalls[1:]) + smalls[0][:, inner:]
    d_conv = jnp.concatenate([join(0, inner), shared], axis=1)
    d_conv_weight, d_conv_bias = d_conv[:taps], d_conv[taps]
    d_gate_gain = join(0, inner)[5]
    d_dt_bias = join(0, heads)[6]
    d_a_log = join(LANES, LANES + heads)[6]
    d_skip_gain = join(2 * LANES, 2 * LANES + heads)[6]

    in_parts = links.from_reps(in_sum)
    mid = inner + inner
    d_in_weight = jnp.concatenate(
        [part[:, :inner] for part in in_parts]
        + [part[:, inner:mid] for part in in_parts]
        + [sum(part[:, mid : mid + 2 * state] for part in in_parts[1:]) + in_parts[0][:, mid : mid + 2 * state]]
        + [part[:, mid + 2 * state : mid + 2 * state + heads] for part in in_parts],
        axis=1,
    )
    if links.paired:
        back = lax.ppermute(out_sum, BOTH, [(target, source) for source, target in moves])
        halves = jnp.where(rep == 0, jnp.concatenate([out_sum, back]), jnp.concatenate([back, out_sum]))
        other = links.swap(halves)
        d_out_weight = jnp.where(holds, halves, other)
    else:
        held = lax.all_gather(out_sum, "fsdp", axis=0, tiled=True)
        whole = lax.all_gather(held, "rep", axis=0, tiled=True)
        d_out_weight = lax.dynamic_slice_in_dim(whole, chip * rows_out, rows_out, 0)
    return (
        block_out, d_tokens, d_norm_gain, d_in_weight, d_conv_weight, d_conv_bias, d_dt_bias, d_a_log,
        d_skip_gain, d_gate_gain, d_out_weight,
    )


def solution(mesh):
    rows = P(("rep", "fsdp"), None)
    in_specs = (
        rows, rows, P(), P("fsdp", None), P(), P(), P(), P(), P(), P(), P("fsdp", None), rows,
    )
    out_specs = (
        rows, rows, P(), P("fsdp", None), P(), P(), P(), P(), P(), P(), P("fsdp", None),
    )
    reps, chips = mesh.shape["rep"], mesh.shape["fsdp"]
    return jax.shard_map(
        functools.partial(per_device, reps, chips),
        mesh=mesh, in_specs=in_specs, out_specs=out_specs, check_vma=False,
    )
```

time: 845 us -> 294 us (0.35)
  waiting for transfers between devices: 614 us -> 83.4 us
  starting transfers between devices: 0.45 us -> 122 us
  matrix products: 76 us -> 0 us
  Pallas kernels: 0 us -> 55 us
  blocking collectives: 46.1 us -> 0 us
  local copies, waits for them, and re-layouts: 55 us -> 18.5 us
  other arithmetic: 32.8 us -> 12.9 us
  between operations: 15.5 us -> 1.86 us
    reduce_scatter x2 -> x0, waiting for transfers between devices: 467 us -> none  [the longest x1 383 us: per_device(): lax.psum_scatter(d_in_full, 'fsdp', scatter_dimension=0, tiled=True)]
    all_gather x2 -> x0, waiting for transfers between devices: 145 us -> none  [the longest x1 116 us: per_device(): lax.all_gather(in_weight, 'fsdp', axis=0, tiled=True)]
    ppermute x0 -> x85, starting transfers between devices: none -> 122 us  [the longest x72 118 us: exchange(): return lax.ppermute(x, BOTH, pairs)]
    ppermute x0 -> x85, waiting for transfers between devices: none -> 83.4 us  [the longest x72 75.3 us: exchange(): return lax.ppermute(x, BOTH, pairs)]
    dot_general x18 -> x0, matrix products: 76 us -> none  [the longest x3 13.8 us: mixer(): jnp.einsum('kshp,ksn->khpn', value_blk * tail_weight[..., None], keys_blk...]
    pallas_call x0 -> x6, Pallas kernels: none -> 55 us  [the longest x1 20.6 us: per_device(): pl.pallas_call(functools.partial(backward_kernel, count, inner, head_dim,...]
    psum x1 -> x0, blocking collectives: 46.1 us -> none  [per_device(): lax.psum((d_norm_gain, d_conv_weight, d_conv_bias, d_dt_bias, d_a_log, d_...]
    reshape x11 -> x0, local copies, waits for them, and re-layouts: 19.5 us -> none  [the longest x2 7.19 us: mixer(): (inside + carried_out).reshape(seq_count, seq_len, head_count, head_dim)]
  transfers between devices with their start and end apart: 5 -> 85, of which waited for: 4 -> 29; matrix products, arithmetic and copies ran while one was open for 18% -> 6% of each run, Pallas kernels for 0% -> 16%
where the time goes in v1:
time: 294 us; the launch traced here: 293 us
  starting transfers between devices  122 us (41%)
  waiting for transfers between devices  83.4 us (28%)
  Pallas kernels  55 us (19%)
  local copies, waits for them, and re-layouts  18.5 us (6%)
  other arithmetic  12.9 us (4%)
    ppermute x72, starting transfers between devices, exchange(): return lax.ppermute(x, BOTH, pairs)  118 us
    ppermute x72, waiting for transfers between devices, exchange(): return lax.ppermute(x, BOTH, pairs)  75.3 us
    pallas_call x1, Pallas kernels, per_device(): pl.pallas_call(functools.partial(backward_kernel, count, inner, head_dim,...  20.6 us
    pallas_call x1, Pallas kernels, per_device(): pl.pallas_call(functools.partial(forward_kernel, count, inner, head_dim),...  13.5 us
    unnamed x138, local copies, waits for them, and re-layouts  8.87 us
    pallas_call x1, Pallas kernels, per_device(): pl.pallas_call(functools.partial(gated_kernel, count, inner, full_inner),...  6.83 us
    pallas_call x1, Pallas kernels, per_device(): pl.pallas_call(functools.partial(out_kernel, count, inner), out_shape=[ar...  6.6 us
    pallas_call x1, Pallas kernels, per_device(): pl.pallas_call(functools.partial(dnormed_kernel, count), out_shape=arr(to...  6.35 us
  transfers between devices with their start and end apart: 85, of which 29 were waited for; matrix products, arithmetic and copies ran while one was open for 6% of the time, Pallas kernels for 16%

profile of v1, /device:TPU:0, one launch (start us, length us, event | category | flops | bytes accessed | tf_op | source)
XLA Modules:
  0.0 293.4 jit_solution(9923906368514310941)
XLA Ops:
  3.6 4.1 %collective-permute-start.9 = (bf16[64,2432]{1,0:T(8,128)(2,1)S(1)}, bf16[64,2432]{1,0:T(8,128)(2,1)S(1)}, u32[]{:S(2)}, u32[]{:S(2)}) collective-permute-start(bf16[64,2432]{1,0:T(8,128)(2,1)S(1)} %concatenate.46.rest_0_), channel_id=1, source_target_pairs={{0,8},{1,9},{2,10},{3,11},{4,12},{5,13},{6,14},{7,15},{8,0},{9,1},... | collective-permute-start | bytes 933896 | tf_op jit(solution)/shard_map/ppermute | solution.py:400
  8.3 2.0 collective-permute-start.19
  10.7 5.1 %collective-permute-done.19 = bf16[64,1024]{1,0:T(8,128)(2,1)S(1)} collective-permute-done((bf16[64,1024]{1,0:T(8,128)(2,1)S(1)}, bf16[64,1024]{1,0:T(8,128)(2,1)S(1)}, u32[]{:S(2)}, u32[]{:S(2)}) %collective-permute-start.19) | collective-permute-done | bytes 131104 | tf_op jit(solution)/shard_map/ppermute | solution.py:511
  15.8 9.6 %collective-permute-start.23 = (bf16[64,1024]{1,0:T(8,128)(2,1)S(1)}, bf16[64,1024]{1,0:T(8,128)(2,1)S(1)}, u32[]{:S(2)}, u32[]{:S(2)}) collective-permute-start(bf16[64,1024]{1,0:T(8,128)(2,1)S(1)} %dynamic-slice_select_fusion.rest_0_), channel_id=1, source_target_pairs={{0,4},{1,5},{2,6},{3,7},{4,0},{5,1},{6,2},{7,3},{8,12},{9,13},{10,... | collective-permute-start | bytes 393224 | tf_op jit(solution)/shard_map/ppermute | solution.py:400
  25.6 2.9 %collective-permute-start.13 = (bf16[64,2432]{1,0:T(8,128)(2,1)S(1)}, bf16[64,2432]{1,0:T(8,128)(2,1)S(1)}, u32[]{:S(2)}, u32[]{:S(2)}) collective-permute-start(bf16[64,2432]{1,0:T(8,128)(2,1)S(1)} %concatenate.46.rest_0_), channel_id=1, source_target_pairs={{0,12},{1,13},{2,14},{3,15},{4,8},{5,9},{6,10},{7,11},{8,4},{9,5},... | collective-permute-start | bytes 933896 | tf_op jit(solution)/shard_map/ppermute | solution.py:400
  30.8 9.7 %collective-permute-start.31 = (bf16[64,1024]{1,0:T(8,128)(2,1)S(1)}, bf16[64,1024]{1,0:T(8,128)(2,1)}, u32[]{:S(2)}, u32[]{:S(2)}) collective-permute-start(bf16[64,1024]{1,0:T(8,128)(2,1)S(1)} %dynamic-slice_select_fusion.rest_0_), channel_id=1, source_target_pairs={{0,12},{1,13},{2,14},{3,15},{4,8},{5,9},{6,10},{7,11},{8,4},{9,5},... | collective-permute-start | bytes 393224 | tf_op jit(solution)/shard_map/ppermute | solution.py:400
  40.8 10.6 %collective-permute-done.27.rest_8_ = bf16[64,1024]{1,0:T(8,128)(2,1)} collective-permute-done((bf16[64,1024]{1,0:T(8,128)(2,1)S(1)}, bf16[64,1024]{1,0:T(8,128)(2,1)}, u32[]{:S(2)}, u32[]{:S(2)}) %collective-permute-start.27) | collective-permute-done | bytes 131104 | tf_op jit(solution)/shard_map/ppermute | solution.py:400
  51.4 1.6 collective-permute-start.2
  53.0 1.6 collective-permute-start.3
  57.3 4.3 %collective-permute-done.2.rest_1_ = bf16[64,2432]{1,0:T(8,128)(2,1)S(1)} collective-permute-done((bf16[64,2432]{1,0:T(8,128)(2,1)S(1)}, bf16[64,2432]{1,0:T(8,128)(2,1)S(1)}, u32[]{:S(2)}, u32[]{:S(2)}) %collective-permute-start.2) | collective-permute-done | bytes 311328 | tf_op jit(solution)/shard_map/ppermute | solution.py:400
  61.6 1.6 collective-permute-start.11
  64.9 3.4 %collective-permute-done.10.rest_9_ = bf16[64,2432]{1,0:T(8,128)(2,1)S(1)} collective-permute-done((bf16[64,2432]{1,0:T(8,128)(2,1)S(1)}, bf16[64,2432]{1,0:T(8,128)(2,1)S(1)}, u32[]{:S(2)}, u32[]{:S(2)}) %collective-permute-start.10) | collective-permute-done | bytes 311328 | tf_op jit(solution)/shard_map/ppermute | solution.py:400
  68.3 1.6 collective-permute-start.7
  69.9 5.1 %collective-permute-done.14.rest_13_ = bf16[64,2432]{1,0:T(8,128)(2,1)S(1)} collective-permute-done((bf16[64,2432]{1,0:T(8,128)(2,1)S(1)}, bf16[64,2432]{1,0:T(8,128)(2,1)S(1)}, u32[]{:S(2)}, u32[]{:S(2)}) %collective-permute-start.14) | collective-permute-done | bytes 311328 | tf_op jit(solution)/shard_map/ppermute | solution.py:400
  75.0 1.6 collective-permute-start.4
  76.6 5.1 %collective-permute-done.6.rest_5_ = bf16[64,2432]{1,0:T(8,128)(2,1)S(1)} collective-permute-done((bf16[64,2432]{1,0:T(8,128)(2,1)S(1)}, bf16[64,2432]{1,0:T(8,128)(2,1)S(1)}, u32[]{:S(2)}, u32[]{:S(2)}) %collective-permute-start.6) | collective-permute-done | bytes 311328 | tf_op jit(solution)/shard_map/ppermute | solution.py:400
  81.6 1.6 collective-permute-start.12
  84.4 1.6 collective-permute-start.20
  87.0 1.6 collective-permute-start.16
  88.6 1.6 collective-permute-start.8
  90.1 1.9 broadcast_select_fusion.4
  92.9 2.2 collective-permute-done.16.rest_15_
  95.7 4.2 %collective-permute-done.8.rest_7_ = bf16[64,2432]{1,0:T(8,128)(2,1)S(1)} collective-permute-done((bf16[64,2432]{1,0:T(8,128)(2,1)S(1)}, bf16[64,2432]{1,0:T(8,128)(2,1)S(1)}, u32[]{:S(2)}, u32[]{:S(2)}) %collective-permute-start.8) | collective-permute-done | bytes 311328 | tf_op jit(solution)/shard_map/ppermute | solution.py:400
  100.8 13.5 %forward.1 = (bf16[256,1024]{1,0:T(8,128)(2,1)}, f32[256,2432]{1,0:T(8,128)}, f32[256,1024]{1,0:T(8,128)}, f32[256,128]{1,0:T(8,128)}) custom-call(s32[16]{0:T(128)S(1)} %get-tuple-element.128.pos_ref, bf16[256,1024]{1,0:T(8,128)(2,1)} %pad_maximum_fusion.tok_ref, f32[1,1024]{1,0:T(1,128)S(1)} %bitcast.50, f32[3,256,128]{2,1,0:T(8,128)} %pad_maximum_fusion.2.masks_ref, ...), custom_call_target="tpu_custom_call" | custom-call | tf_op jit(solution)/shard_map/forward/pallas_call | solution.py:558
  114.3 1.6 collective-permute-start.25
  117.0 1.6 collective-permute-start.33
  125.9 6.8 %gated.1 = (bf16[256,1024]{1,0:T(8,128)(2,1)S(1)}, bf16[64,1024]{1,0:T(8,128)(2,1)S(1)}, bf16[64,1024]{1,0:T(8,128)(2,1)S(1)}, bf16[64,1024]{1,0:T(8,128)(2,1)S(...) custom-call(s32[16]{0:T(128)S(1)} %get-tuple-element.129.pos_ref, ...), custom_call_target="tpu_custom_call" | custom-call | tf_op jit(solution)/shard_map/gated/pallas_call | solution.py:572
  139.3 6.6 %out.1 = (f32[256,1024]{1,0:T(8,128)}, f32[256,128]{1,0:T(8,128)}, f32[256,1024]{1,0:T(8,128)}) custom-call(s32[16]{0:T(128)S(1)} %get-tuple-element.129.pos_ref, f32[256,2432]{1,0:T(8,128)} %get-tuple-element.55.proj_ref, f32[256,1024]{1,0:T(8,128)} %get-tuple-element.56.mixer_ref, f32[1,1024]{1,0:T(1,128)S(1)} %bitcast.48, ...), custom_call_target="tpu_custom_call" | custom-call | tf_op jit(solution)/shard_map/out/pallas_call | solution.py:581
  152.8 20.6 %backward.1 = (bf16[256,2432]{1,0:T(8,128)(2,1)}, f32[8,1280]{1,0:T(8,128)S(1)}, bf16[64,2432]{1,0:T(8,128)(2,1)S(1)}, bf16[64,2432]{1,0:T(8,128)(2,1)S(1)}, bf1...) custom-call(s32[16]{0:T(128)S(1)} %get-tuple-element.128.pos_ref, ...), custom_call_target="tpu_custom_call" | custom-call | tf_op jit(solution)/shard_map/backward/pallas_call | solution.py:592
  176.6 1.5 collective-permute-start.63
  178.2 1.6 collective-permute-start.81
  179.8 1.8 collective-permute-done.63
  181.7 2.9 collective-permute-start.65
  186.2 6.4 %dnormed.1 = f32[256,1024]{1,0:T(8,128)} custom-call(s32[16]{0:T(128)S(1)} %get-tuple-element.128.pos_ref, bf16[256,2432]{1,0:T(8,128)(2,1)} %get-tuple-element.63.dproj_ref, bf16[64,2432]{1,0:T(8,128)(2,1)S(1)} %concatenate.46.rest_0_, bf16[64,2432]{1,0:T(8,128)(2,1)S(1)} %collective-permute-done.2.rest_1_, ...), custom_call_target="tpu_custom_call" | custom-call | tf_op jit(solution)/shard_map/dnormed/pallas_call | solution.py:609
  196.2 1.6 collective-permute-start.70
  205.6 2.4 collective-permute-start.71
  208.0 2.1 collective-permute-start.79
  215.2 2.5 collective-permute-done.75
  223.5 5.3 %collective-permute-done.54 = bf16[64,2432]{1,0:T(8,128)(2,1)S(1)} collective-permute-done((bf16[64,2432]{1,0:T(8,128)(2,1)S(1)}, bf16[64,2432]{1,0:T(8,128)(2,1)S(1)}, u32[]{:S(2)}, u32[]{:S(2)}) %collective-permute-start.54) | collective-permute-done | bytes 311328 | tf_op jit(solution)/shard_map/ppermute | solution.py:400
  228.9 1.8 collective-permute-done.37.other_ref
  233.1 4.4 %collective-permute-done.58 = bf16[64,2432]{1,0:T(8,128)(2,1)S(1)} collective-permute-done((bf16[64,2432]{1,0:T(8,128)(2,1)S(1)}, bf16[64,2432]{1,0:T(8,128)(2,1)S(1)}, u32[]{:S(2)}, u32[]{:S(2)}) %collective-permute-start.58) | collective-permute-done | bytes 311328 | tf_op jit(solution)/shard_map/ppermute | solution.py:400
  242.0 1.6 collective-permute-start.55
  243.6 4.7 %collective-permute-done.51 = bf16[64,2432]{1,0:T(8,128)(2,1)S(1)} collective-permute-done((bf16[64,2432]{1,0:T(8,128)(2,1)S(1)}, bf16[64,2432]{1,0:T(8,128)(2,1)S(1)}, u32[]{:S(2)}, u32[]{:S(2)}) %collective-permute-start.51) | collective-permute-done | bytes 311328 | tf_op jit(solution)/shard_map/ppermute | solution.py:400
  254.4 2.6 collective-permute-start.48
  260.2 6.3 %collective-permute-done.48 = bf16[64,2432]{1,0:T(8,128)(2,1)S(1)} collective-permute-done((bf16[64,2432]{1,0:T(8,128)(2,1)S(1)}, bf16[64,2432]{1,0:T(8,128)(2,1)S(1)}, u32[]{:S(2)}, u32[]{:S(2)}) %collective-permute-start.48) | collective-permute-done | bytes 311328 | tf_op jit(solution)/shard_map/ppermute | solution.py:400
  266.5 13.3 %collective-permute-start.42 = (f32[8,1024]{1,0:T(8,128)S(1)}, f32[8,1024]{1,0:T(8,128)S(1)}, u32[]{:S(2)}, u32[]{:S(2)}) collective-permute-start(f32[8,1024]{1,0:T(8,128)S(1)} %add_add_fusion.4), channel_id=1, source_target_pairs={{0,4},{1,5},{2,6},{3,7},{4,0},{5,1},{6,2},{7,3},{8,12},{9,13},{10,... | collective-permute-start | bytes 98312 | tf_op jit(solution)/shard_map/ppermute | solution.py:400
  279.8 5.0 %collective-permute-done.52 = bf16[64,2432]{1,0:T(8,128)(2,1)S(1)} collective-permute-done((bf16[64,2432]{1,0:T(8,128)(2,1)S(1)}, bf16[64,2432]{1,0:T(8,128)(2,1)S(1)}, u32[]{:S(2)}, u32[]{:S(2)}) %collective-permute-start.52) | collective-permute-done | bytes 311328 | tf_op jit(solution)/shard_map/ppermute | solution.py:400
  288.1 1.6 collective-permute-done.43
  (354 shorter events, 86.9 us)
Async XLA Ops:
  3.6 51.0 %collective-permute-start.9 = (bf16[64,2432]{1,0:T(8,128)(2,1)S(1)}, bf16[64,2432]{1,0:T(8,128)(2,1)S(1)}, u32[]{:S(2)}, u32[]{:S(2)}) collective-permute-start(bf16[64,2432]{1,0:T(8,128)(2,1)S(1)} %concatenate.46.rest_0_), channel_id=1, source_target_pairs={{0,8},{1,9},{2,10},{3,11},{4,12},{5,13},{6,14},{7,15},{8,0},{9,1},... | collective-permute-start | bytes 933896 | tf_op jit(solution)/shard_map/ppermute | solution.py:400
  7.7 17.9 %collective-permute-start.1 = (s32[1,128]{1,0:T(1,128)S(1)}, s32[1,128]{1,0:T(1,128)S(1)}, u32[]{:S(2)}, u32[]{:S(2)}) collective-permute-start(s32[1,128]{1,0:T(1,128)S(1)} %copy-done.62), channel_id=1, source_target_pairs={{0,16},{16,0},{1,17},{17,1},{2,18},{18,2},{3,19},{19,3},{4,20},{20... | collective-permute-start | bytes 1544 | tf_op jit(solution)/shard_map/ppermute | solution.py:442
  7.7 20.8 %collective-permute-start = (bf16[128,1024]{1,0:T(8,128)(2,1)S(1)}, bf16[128,1024]{1,0:T(8,128)(2,1)}, u32[]{:S(2)}, u32[]{:S(2)}) collective-permute-start(bf16[128,1024]{1,0:T(8,128)(2,1)S(1)} %copy-done), channel_id=1, source_target_pairs={{0,16},{16,0},{1,17},{17,1},{2,18},{18,2},{3,19},{19,3},{4,20},{20... | collective-permute-start | bytes 786440 | tf_op jit(solution)/shard_map/ppermute | solution.py:442
  8.2 21.4 %collective-permute-start.17 = (bf16[128,1024]{1,0:T(8,128)(2,1)S(1)}, bf16[128,1024]{1,0:T(8,128)(2,1)S(1)}, u32[]{:S(2)}, u32[]{:S(2)}) collective-permute-start(bf16[128,1024]{1,0:T(8,128)(2,1)S(1)} %copy-done.9), channel_id=1, source_target_pairs={{0,16},{16,0},{1,17},{17,1},{2,18},{18,2},{3,19},{19,3},{4,20},{20... | collective-permute-start | bytes 786440 | tf_op jit(solution)/shard_map/ppermute | solution.py:442
  15.8 15.0 %collective-permute-start.23 = (bf16[64,1024]{1,0:T(8,128)(2,1)S(1)}, bf16[64,1024]{1,0:T(8,128)(2,1)S(1)}, u32[]{:S(2)}, u32[]{:S(2)}) collective-permute-start(bf16[64,1024]{1,0:T(8,128)(2,1)S(1)} %dynamic-slice_select_fusion.rest_0_), channel_id=1, source_target_pairs={{0,4},{1,5},{2,6},{3,7},{4,0},{5,1},{6,2},{7,3},{8,12},{9,13},{10,... | collective-permute-start | bytes 393224 | tf_op jit(solution)/shard_map/ppermute | solution.py:400
  25.6 29.5 %collective-permute-start.13 = (bf16[64,2432]{1,0:T(8,128)(2,1)S(1)}, bf16[64,2432]{1,0:T(8,128)(2,1)S(1)}, u32[]{:S(2)}, u32[]{:S(2)}) collective-permute-start(bf16[64,2432]{1,0:T(8,128)(2,1)S(1)} %concatenate.46.rest_0_), channel_id=1, source_target_pairs={{0,12},{1,13},{2,14},{3,15},{4,8},{5,9},{6,10},{7,11},{8,4},{9,5},... | collective-permute-start | bytes 933896 | tf_op jit(solution)/shard_map/ppermute | solution.py:400
  28.5 28.1 %collective-permute-start.5 = (bf16[64,2432]{1,0:T(8,128)(2,1)S(1)}, bf16[64,2432]{1,0:T(8,128)(2,1)S(1)}, u32[]{:S(2)}, u32[]{:S(2)}) collective-permute-start(bf16[64,2432]{1,0:T(8,128)(2,1)S(1)} %concatenate.46.rest_0_), channel_id=1, source_target_pairs={{0,4},{1,5},{2,6},{3,7},{4,0},{5,1},{6,2},{7,3},{8,12},{9,13},{10,... | collective-permute-start | bytes 933896 | tf_op jit(solution)/shard_map/ppermute | solution.py:400
  29.6 21.8 %collective-permute-start.27 = (bf16[64,1024]{1,0:T(8,128)(2,1)S(1)}, bf16[64,1024]{1,0:T(8,128)(2,1)}, u32[]{:S(2)}, u32[]{:S(2)}) collective-permute-start(bf16[64,1024]{1,0:T(8,128)(2,1)S(1)} %dynamic-slice_select_fusion.rest_0_), channel_id=1, source_target_pairs={{0,8},{1,9},{2,10},{3,11},{4,12},{5,13},{6,14},{7,15},{8,0},{9,1},... | collective-permute-start | bytes 393224 | tf_op jit(solution)/shard_map/ppermute | solution.py:400
  30.8 22.2 %collective-permute-start.31 = (bf16[64,1024]{1,0:T(8,128)(2,1)S(1)}, bf16[64,1024]{1,0:T(8,128)(2,1)}, u32[]{:S(2)}, u32[]{:S(2)}) collective-permute-start(bf16[64,1024]{1,0:T(8,128)(2,1)S(1)} %dynamic-slice_select_fusion.rest_0_), channel_id=1, source_target_pairs={{0,12},{1,13},{2,14},{3,15},{4,8},{5,9},{6,10},{7,11},{8,4},{9,5},... | collective-permute-start | bytes 393224 | tf_op jit(solution)/shard_map/ppermute | solution.py:400
  54.6 13.7 %collective-permute-start.10 = (bf16[64,2432]{1,0:T(8,128)(2,1)S(1)}, bf16[64,2432]{1,0:T(8,128)(2,1)S(1)}, u32[]{:S(2)}, u32[]{:S(2)}) collective-permute-start(bf16[64,2432]{1,0:T(8,128)(2,1)S(1)} %collective-permute-done.9.rest_8_), channel_id=1, source_target_pairs={{0,1},{1,0},{2,3},{3,2},{4,5},{5,4},{6,7},{7,6},{8,9},{9,8},{10,11... | collective-permute-start | bytes 933896 | tf_op jit(solution)/shard_map/ppermute | solution.py:400
  55.1 19.8 %collective-permute-start.14 = (bf16[64,2432]{1,0:T(8,128)(2,1)S(1)}, bf16[64,2432]{1,0:T(8,128)(2,1)S(1)}, u32[]{:S(2)}, u32[]{:S(2)}) collective-permute-start(bf16[64,2432]{1,0:T(8,128)(2,1)S(1)} %collective-permute-done.13.rest_12_), channel_id=1, source_target_pairs={{0,1},{1,0},{2,3},{3,2},{4,5},{5,4},{6,7},{7,6},{8,9},{9,8},{10,11... | collective-permute-start | bytes 933896 | tf_op jit(solution)/shard_map/ppermute | solution.py:400
  56.6 25.0 %collective-permute-start.6 = (bf16[64,2432]{1,0:T(8,128)(2,1)S(1)}, bf16[64,2432]{1,0:T(8,128)(2,1)S(1)}, u32[]{:S(2)}, u32[]{:S(2)}) collective-permute-start(bf16[64,2432]{1,0:T(8,128)(2,1)S(1)} %collective-permute-done.5.rest_4_), channel_id=1, source_target_pairs={{0,1},{1,0},{2,3},{3,2},{4,5},{5,4},{6,7},{7,6},{8,9},{9,8},{10,11... | collective-permute-start | bytes 933896 | tf_op jit(solution)/shard_map/ppermute | solution.py:400
  61.6 22.8 %collective-permute-start.11 = (bf16[64,2432]{1,0:T(8,128)(2,1)S(1)}, bf16[64,2432]{1,0:T(8,128)(2,1)S(1)}, u32[]{:S(2)}, u32[]{:S(2)}) collective-permute-start(bf16[64,2432]{1,0:T(8,128)(2,1)S(1)} %collective-permute-done.9.rest_8_), channel_id=1, source_target_pairs={{0,2},{1,3},{2,0},{3,1},{4,6},{5,7},{6,4},{7,5},{8,10},{9,11},{10,... | collective-permute-start | bytes 933896 | tf_op jit(solution)/shard_map/ppermute | solution.py:400
  63.4 22.6 %collective-permute-start.15 = (bf16[64,2432]{1,0:T(8,128)(2,1)S(1)}, bf16[64,2432]{1,0:T(8,128)(2,1)S(1)}, u32[]{:S(2)}, u32[]{:S(2)}) collective-permute-start(bf16[64,2432]{1,0:T(8,128)(2,1)S(1)} %collective-permute-done.13.rest_12_), channel_id=1, source_target_pairs={{0,2},{1,3},{2,0},{3,1},{4,6},{5,7},{6,4},{7,5},{8,10},{9,11},{10,... | collective-permute-start | bytes 933896 | tf_op jit(solution)/shard_map/ppermute | solution.py:400
  68.3 18.2 %collective-permute-start.7 = (bf16[64,2432]{1,0:T(8,128)(2,1)S(1)}, bf16[64,2432]{1,0:T(8,128)(2,1)S(1)}, u32[]{:S(2)}, u32[]{:S(2)}) collective-permute-start(bf16[64,2432]{1,0:T(8,128)(2,1)S(1)} %collective-permute-done.5.rest_4_), channel_id=1, source_target_pairs={{0,2},{1,3},{2,0},{3,1},{4,6},{5,7},{6,4},{7,5},{8,10},{9,11},{10,... | collective-permute-start | bytes 933896 | tf_op jit(solution)/shard_map/ppermute | solution.py:400
  75.0 12.0 %collective-permute-start.4 = (bf16[64,2432]{1,0:T(8,128)(2,1)S(1)}, bf16[64,2432]{1,0:T(8,128)(2,1)S(1)}, u32[]{:S(2)}, u32[]{:S(2)}) collective-permute-start(bf16[64,2432]{1,0:T(8,128)(2,1)S(1)} %collective-permute-done.2.rest_1_), channel_id=1, source_target_pairs={{0,2},{1,3},{2,0},{3,1},{4,6},{5,7},{6,4},{7,5},{8,10},{9,11},{10,... | collective-permute-start | bytes 933896 | tf_op jit(solution)/shard_map/ppermute | solution.py:400
  84.4 29.8 %collective-permute-start.20 = (bf16[64,1024]{1,0:T(8,128)(2,1)S(1)}, bf16[64,1024]{1,0:T(8,128)(2,1)}, u32[]{:S(2)}, u32[]{:S(2)}) collective-permute-start(bf16[64,1024]{1,0:T(8,128)(2,1)S(1)} %copy-done.12), channel_id=1, source_target_pairs={{0,1},{1,0},{2,3},{3,2},{4,5},{5,4},{6,7},{7,6},{8,9},{9,8},{10,11... | collective-permute-start | bytes 393224 | tf_op jit(solution)/shard_map/ppermute | solution.py:400
  86.0 29.9 %collective-permute-start.21 = (bf16[64,1024]{1,0:T(8,128)(2,1)S(1)}, bf16[64,1024]{1,0:T(8,128)(2,1)S(1)}, u32[]{:S(2)}, u32[]{:S(2)}) collective-permute-start(bf16[64,1024]{1,0:T(8,128)(2,1)S(1)} %copy-done.12), channel_id=1, source_target_pairs={{0,2},{1,3},{2,0},{3,1},{4,6},{5,7},{6,4},{7,5},{8,10},{9,11},{10,... | collective-permute-start | bytes 393224 | tf_op jit(solution)/shard_map/ppermute | solution.py:400
  86.5 30.5 %collective-permute-start.24 = (bf16[64,1024]{1,0:T(8,128)(2,1)S(1)}, bf16[64,1024]{1,0:T(8,128)(2,1)}, u32[]{:S(2)}, u32[]{:S(2)}) collective-permute-start(bf16[64,1024]{1,0:T(8,128)(2,1)S(1)} %copy-done.15), channel_id=1, source_target_pairs={{0,1},{1,0},{2,3},{3,2},{4,5},{5,4},{6,7},{7,6},{8,9},{9,8},{10,11... | collective-permute-start | bytes 393224 | tf_op jit(solution)/shard_map/ppermute | solution.py:400
  88.6 11.4 %collective-permute-start.8 = (bf16[64,2432]{1,0:T(8,128)(2,1)S(1)}, bf16[64,2432]{1,0:T(8,128)(2,1)S(1)}, u32[]{:S(2)}, u32[]{:S(2)}) collective-permute-start(bf16[64,2432]{1,0:T(8,128)(2,1)S(1)} %collective-permute-done.6.rest_5_), channel_id=1, source_target_pairs={{0,2},{1,3},{2,0},{3,1},{4,6},{5,7},{6,4},{7,5},{8,10},{9,11},{10,... | collective-permute-start | bytes 933896 | tf_op jit(solution)/shard_map/ppermute | solution.py:400
  95.1 21.9 %collective-permute-start.28 = (bf16[64,1024]{1,0:T(8,128)(2,1)}, bf16[64,1024]{1,0:T(8,128)(2,1)}, u32[]{:S(2)}, u32[]{:S(2)}) collective-permute-start(bf16[64,1024]{1,0:T(8,128)(2,1)} %collective-permute-done.27.rest_8_), channel_id=1, source_target_pairs={{0,1},{1,0},{2,3},{3,2},{4,5},{5,4},{6,7},{7,6},{8,9},{9,8},{10,11... | collective-permute-start | bytes 393224 | tf_op jit(solution)/shard_map/ppermute | solution.py:400
  99.9 18.7 %collective-permute-start.32 = (bf16[64,1024]{1,0:T(8,128)(2,1)}, bf16[64,1024]{1,0:T(8,128)(2,1)}, u32[]{:S(2)}, u32[]{:S(2)}) collective-permute-start(bf16[64,1024]{1,0:T(8,128)(2,1)} %collective-permute-done.31.rest_12_), channel_id=1, source_target_pairs={{0,1},{1,0},{2,3},{3,2},{4,5},{5,4},{6,7},{7,6},{8,9},{9,8},{10,11... | collective-permute-start | bytes 393224 | tf_op jit(solution)/shard_map/ppermute | solution.py:400
  117.0 21.5 %collective-permute-start.33 = (bf16[64,1024]{1,0:T(8,128)(2,1)}, bf16[64,1024]{1,0:T(8,128)(2,1)}, u32[]{:S(2)}, u32[]{:S(2)}) collective-permute-start(bf16[64,1024]{1,0:T(8,128)(2,1)} %collective-permute-done.31.rest_12_), channel_id=1, source_target_pairs={{0,2},{1,3},{2,0},{3,1},{4,6},{5,7},{6,4},{7,5},{8,10},{9,11},{10,... | collective-permute-start | bytes 393224 | tf_op jit(solution)/shard_map/ppermute | solution.py:400
  118.6 20.6 %collective-permute-start.22 = (bf16[64,1024]{1,0:T(8,128)(2,1)}, bf16[64,1024]{1,0:T(8,128)(2,1)}, u32[]{:S(2)}, u32[]{:S(2)}) collective-permute-start(bf16[64,1024]{1,0:T(8,128)(2,1)} %collective-permute-done.20.rest_1_), channel_id=1, source_target_pairs={{0,2},{1,3},{2,0},{3,1},{4,6},{5,7},{6,4},{7,5},{8,10},{9,11},{10,... | collective-permute-start | bytes 393224 | tf_op jit(solution)/shard_map/ppermute | solution.py:400
  120.0 19.2 %collective-permute-start.26 = (bf16[64,1024]{1,0:T(8,128)(2,1)}, bf16[64,1024]{1,0:T(8,128)(2,1)}, u32[]{:S(2)}, u32[]{:S(2)}) collective-permute-start(bf16[64,1024]{1,0:T(8,128)(2,1)} %collective-permute-done.24.rest_5_), channel_id=1, source_target_pairs={{0,2},{1,3},{2,0},{3,1},{4,6},{5,7},{6,4},{7,5},{8,10},{9,11},{10,... | collective-permute-start | bytes 393224 | tf_op jit(solution)/shard_map/ppermute | solution.py:400
  121.7 17.5 %collective-permute-start.30 = (bf16[64,1024]{1,0:T(8,128)(2,1)}, bf16[64,1024]{1,0:T(8,128)(2,1)}, u32[]{:S(2)}, u32[]{:S(2)}) collective-permute-start(bf16[64,1024]{1,0:T(8,128)(2,1)} %collective-permute-done.28.rest_9_), channel_id=1, source_target_pairs={{0,2},{1,3},{2,0},{3,1},{4,6},{5,7},{6,4},{7,5},{8,10},{9,11},{10,... | collective-permute-start | bytes 393224 | tf_op jit(solution)/shard_map/ppermute | solution.py:400
  122.2 17.0 %collective-permute-start.34 = (bf16[64,1024]{1,0:T(8,128)(2,1)}, bf16[64,1024]{1,0:T(8,128)(2,1)}, u32[]{:S(2)}, u32[]{:S(2)}) collective-permute-start(bf16[64,1024]{1,0:T(8,128)(2,1)} %collective-permute-done.32.rest_13_), channel_id=1, source_target_pairs={{0,2},{1,3},{2,0},{3,1},{4,6},{5,7},{6,4},{7,5},{8,10},{9,11},{10,... | collective-permute-start | bytes 393224 | tf_op jit(solution)/shard_map/ppermute | solution.py:400
  146.0 27.5 %collective-permute-start.69 = (bf16[64,1024]{1,0:T(8,128)(2,1)}, bf16[64,1024]{1,0:T(8,128)(2,1)}, u32[]{:S(2)}, u32[]{:S(2)}) collective-permute-start(bf16[64,1024]{1,0:T(8,128)(2,1)} %get-tuple-element.86), channel_id=1, source_target_pairs={{0,2},{1,3},{2,0},{3,1},{4,6},{5,7},{6,4},{7,5},{8,10},{9,11},{10,... | collective-permute-start | bytes 393224 | tf_op jit(solution)/shard_map/ppermute | solution.py:400
  146.6 53.2 %collective-permute-start.68 = (bf16[64,1024]{1,0:T(8,128)(2,1)}, bf16[64,1024]{1,0:T(8,128)(2,1)S(1)}, u32[]{:S(2)}, u32[]{:S(2)}) collective-permute-start(bf16[64,1024]{1,0:T(8,128)(2,1)} %copy-done.45), channel_id=1, source_target_pairs={{0,2},{1,3},{2,0},{3,1},{4,6},{5,7},{6,4},{7,5},{8,10},{9,11},{10,... | collective-permute-start | bytes 393224 | tf_op jit(solution)/shard_map/ppermute | solution.py:400
  148.1 27.6 %collective-permute-start.73 = (bf16[64,1024]{1,0:T(8,128)(2,1)}, bf16[64,1024]{1,0:T(8,128)(2,1)S(1)}, u32[]{:S(2)}, u32[]{:S(2)}) collective-permute-start(bf16[64,1024]{1,0:T(8,128)(2,1)} %copy-done.49), channel_id=1, source_target_pairs={{0,2},{1,3},{2,0},{3,1},{4,6},{5,7},{6,4},{7,5},{8,10},{9,11},{10,... | collective-permute-start | bytes 393224 | tf_op jit(solution)/shard_map/ppermute | solution.py:400
  148.6 54.2 %collective-permute-start.72 = (bf16[64,1024]{1,0:T(8,128)(2,1)}, bf16[64,1024]{1,0:T(8,128)(2,1)S(1)}, u32[]{:S(2)}, u32[]{:S(2)}) collective-permute-start(bf16[64,1024]{1,0:T(8,128)(2,1)} %copy-done.44), channel_id=1, source_target_pairs={{0,2},{1,3},{2,0},{3,1},{4,6},{5,7},{6,4},{7,5},{8,10},{9,11},{10,... | collective-permute-start | bytes 393224 | tf_op jit(solution)/shard_map/ppermute | solution.py:400
  151.2 25.4 %collective-permute-start.77 = (bf16[64,1024]{1,0:T(8,128)(2,1)}, bf16[64,1024]{1,0:T(8,128)(2,1)S(1)}, u32[]{:S(2)}, u32[]{:S(2)}) collective-permute-start(bf16[64,1024]{1,0:T(8,128)(2,1)} %copy-done.48), channel_id=1, source_target_pairs={{0,2},{1,3},{2,0},{3,1},{4,6},{5,7},{6,4},{7,5},{8,10},{9,11},{10,... | collective-permute-start | bytes 393224 | tf_op jit(solution)/shard_map/ppermute | solution.py:400
  181.7 12.1 %collective-permute-start.65 = (f32[8,1280]{1,0:T(8,128)S(1)}, f32[8,1280]{1,0:T(8,128)S(1)}, u32[]{:S(2)}, u32[]{:S(2)}) collective-permute-start(f32[8,1280]{1,0:T(8,128)S(1)} %add_add_fusion.3), channel_id=1, source_target_pairs={{0,8},{1,9},{2,10},{3,11},{4,12},{5,13},{6,14},{7,15},{8,0},{9,1},... | collective-permute-start | bytes 122888 | tf_op jit(solution)/shard_map/ppermute | solution.py:400
  192.6 13.0 %collective-permute-start.76 = (bf16[64,1024]{1,0:T(8,128)(2,1)S(1)}, bf16[64,1024]{1,0:T(8,128)(2,1)S(1)}, u32[]{:S(2)}, u32[]{:S(2)}) collective-permute-start(bf16[64,1024]{1,0:T(8,128)(2,1)S(1)} %copy-done.43), channel_id=1, source_target_pairs={{0,2},{1,3},{2,0},{3,1},{4,6},{5,7},{6,4},{7,5},{8,10},{9,11},{10,... | collective-permute-start | bytes 393224 | tf_op jit(solution)/shard_map/ppermute | solution.py:400
  193.8 14.2 %collective-permute-start.80 = (bf16[64,1024]{1,0:T(8,128)(2,1)S(1)}, bf16[64,1024]{1,0:T(8,128)(2,1)S(1)}, u32[]{:S(2)}, u32[]{:S(2)}) collective-permute-start(bf16[64,1024]{1,0:T(8,128)(2,1)S(1)} %copy-done.41), channel_id=1, source_target_pairs={{0,2},{1,3},{2,0},{3,1},{4,6},{5,7},{6,4},{7,5},{8,10},{9,11},{10,... | collective-permute-start | bytes 393224 | tf_op jit(solution)/shard_map/ppermute | solution.py:400
  204.7 15.1 %collective-permute-start.46 = (bf16[64,2432]{1,0:T(8,128)(2,1)S(1)}, bf16[64,2432]{1,0:T(8,128)(2,1)S(1)}, u32[]{:S(2)}, u32[]{:S(2)}) collective-permute-start(bf16[64,2432]{1,0:T(8,128)(2,1)S(1)} %copy-done.65), channel_id=1, source_target_pairs={{0,2},{1,3},{2,0},{3,1},{4,6},{5,7},{6,4},{7,5},{8,10},{9,11},{10,... | collective-permute-start | bytes 933896 | tf_op jit(solution)/shard_map/ppermute | solution.py:400
  211.9 28.0 %collective-permute-start.45 = (bf16[64,2432]{1,0:T(8,128)(2,1)S(1)}, bf16[64,2432]{1,0:T(8,128)(2,1)S(1)}, u32[]{:S(2)}, u32[]{:S(2)}) collective-permute-start(bf16[64,2432]{1,0:T(8,128)(2,1)S(1)} %copy-done.63), channel_id=1, source_target_pairs={{0,2},{1,3},{2,0},{3,1},{4,6},{5,7},{6,4},{7,5},{8,10},{9,11},{10,... | collective-permute-start | bytes 933896 | tf_op jit(solution)/shard_map/ppermute | solution.py:400
  217.6 24.3 %collective-permute-start.49 = (bf16[64,2432]{1,0:T(8,128)(2,1)S(1)}, bf16[64,2432]{1,0:T(8,128)(2,1)S(1)}, u32[]{:S(2)}, u32[]{:S(2)}) collective-permute-start(bf16[64,2432]{1,0:T(8,128)(2,1)S(1)} %get-tuple-element.71), channel_id=1, source_target_pairs={{0,2},{1,3},{2,0},{3,1},{4,6},{5,7},{6,4},{7,5},{8,10},{9,11},{10,... | collective-permute-start | bytes 933896 | tf_op jit(solution)/shard_map/ppermute | solution.py:400
  219.8 29.6 %collective-permute-start.53 = (bf16[64,2432]{1,0:T(8,128)(2,1)S(1)}, bf16[64,2432]{1,0:T(8,128)(2,1)S(1)}, u32[]{:S(2)}, u32[]{:S(2)}) collective-permute-start(bf16[64,2432]{1,0:T(8,128)(2,1)S(1)} %get-tuple-element.75), channel_id=1, source_target_pairs={{0,2},{1,3},{2,0},{3,1},{4,6},{5,7},{6,4},{7,5},{8,10},{9,11},{10,... | collective-permute-start | bytes 933896 | tf_op jit(solution)/shard_map/ppermute | solution.py:400
  222.2 15.3 %collective-permute-start.58 = (bf16[64,2432]{1,0:T(8,128)(2,1)S(1)}, bf16[64,2432]{1,0:T(8,128)(2,1)S(1)}, u32[]{:S(2)}, u32[]{:S(2)}) collective-permute-start(bf16[64,2432]{1,0:T(8,128)(2,1)S(1)} %get-tuple-element.81), channel_id=1, source_target_pairs={{0,2},{1,3},{2,0},{3,1},{4,6},{5,7},{6,4},{7,5},{8,10},{9,11},{10,... | collective-permute-start | bytes 933896 | tf_op jit(solution)/shard_map/ppermute | solution.py:400
  238.7 20.2 %collective-permute-start.57 = (bf16[64,2432]{1,0:T(8,128)(2,1)S(1)}, bf16[64,2432]{1,0:T(8,128)(2,1)S(1)}, u32[]{:S(2)}, u32[]{:S(2)}) collective-permute-start(bf16[64,2432]{1,0:T(8,128)(2,1)S(1)} %get-tuple-element.79), channel_id=1, source_target_pairs={{0,2},{1,3},{2,0},{3,1},{4,6},{5,7},{6,4},{7,5},{8,10},{9,11},{10,... | collective-permute-start | bytes 933896 | tf_op jit(solution)/shard_map/ppermute | solution.py:400
  239.9 13.2 %collective-permute-start.83 = (f32[64,1024]{1,0:T(8,128)S(1)}, f32[64,1024]{1,0:T(8,128)S(1)}, u32[]{:S(2)}, u32[]{:S(2)}) collective-permute-start(f32[64,1024]{1,0:T(8,128)S(1)} %add_add_fusion.1), channel_id=1, source_target_pairs={{8,0},{9,1},{10,2},{11,3},{12,4},{13,5},{14,6},{15,7},{16,24},{17,... | collective-permute-start | bytes 786440 | tf_op jit(solution)/shard_map/ppermute | solution.py:655
  254.4 12.1 %collective-permute-start.48 = (bf16[64,2432]{1,0:T(8,128)(2,1)S(1)}, bf16[64,2432]{1,0:T(8,128)(2,1)S(1)}, u32[]{:S(2)}, u32[]{:S(2)}) collective-permute-start(bf16[64,2432]{1,0:T(8,128)(2,1)S(1)} %add_convert_fusion.5), channel_id=1, source_target_pairs={{0,12},{1,13},{2,14},{3,15},{4,8},{5,9},{6,10},{7,11},{8,4},{9,5},... | collective-permute-start | bytes 933896 | tf_op jit(solution)/shard_map/ppermute | solution.py:400
  257.0 27.8 %collective-permute-start.52 = (bf16[64,2432]{1,0:T(8,128)(2,1)S(1)}, bf16[64,2432]{1,0:T(8,128)(2,1)S(1)}, u32[]{:S(2)}, u32[]{:S(2)}) collective-permute-start(bf16[64,2432]{1,0:T(8,128)(2,1)S(1)} %add_convert_fusion.3), channel_id=1, source_target_pairs={{0,8},{1,9},{2,10},{3,11},{4,12},{5,13},{6,14},{7,15},{8,0},{9,1},... | collective-permute-start | bytes 933896 | tf_op jit(solution)/shard_map/ppermute | solution.py:400
  258.0 26.9 %collective-permute-start.56 = (bf16[64,2432]{1,0:T(8,128)(2,1)S(1)}, bf16[64,2432]{1,0:T(8,128)(2,1)S(1)}, u32[]{:S(2)}, u32[]{:S(2)}) collective-permute-start(bf16[64,2432]{1,0:T(8,128)(2,1)S(1)} %add_convert_fusion.1), channel_id=1, source_target_pairs={{0,4},{1,5},{2,6},{3,7},{4,0},{5,1},{6,2},{7,3},{8,12},{9,13},{10,... | collective-permute-start | bytes 933896 | tf_op jit(solution)/shard_map/ppermute | solution.py:400
  258.8 27.4 %collective-permute-start.35 = (f32[128,1024]{1,0:T(8,128)S(1)}, f32[128,1024]{1,0:T(8,128)S(1)}, u32[]{:S(2)}, u32[]{:S(2)}) collective-permute-start(f32[128,1024]{1,0:T(8,128)S(1)} %constant_dynamic-slice_fusion.2), channel_id=1, source_target_pairs={{0,16},{16,0},{1,17},{17,1},{2,18},{18,2},{3,19},{19,3},{4,20},{20... | collective-permute-start | bytes 1572872 | tf_op jit(solution)/shard_map/ppermute | solution.py:442
  260.2 31.0 %collective-permute-start.84 = (f32[128,1024]{1,0:T(8,128)S(1)}, f32[128,1024]{1,0:T(8,128)S(1)}, u32[]{:S(2)}, u32[]{:S(2)}) collective-permute-start(f32[128,1024]{1,0:T(8,128)S(1)} %maximum_select_fusion), channel_id=1, source_target_pairs={{0,16},{16,0},{1,17},{17,1},{2,18},{18,2},{3,19},{19,3},{4,20},{20... | collective-permute-start | bytes 1572872 | tf_op jit(solution)/shard_map/ppermute | solution.py:442
  266.5 21.6 %collective-permute-start.42 = (f32[8,1024]{1,0:T(8,128)S(1)}, f32[8,1024]{1,0:T(8,128)S(1)}, u32[]{:S(2)}, u32[]{:S(2)}) collective-permute-start(f32[8,1024]{1,0:T(8,128)S(1)} %add_add_fusion.4), channel_id=1, source_target_pairs={{0,4},{1,5},{2,6},{3,7},{4,0},{5,1},{6,2},{7,3},{8,12},{9,13},{10,... | collective-permute-start | bytes 98312 | tf_op jit(solution)/shard_map/ppermute | solution.py:400
  (107 other events, 1148.8 us)

commit v2 on v1

v2 whole, which is shorter than its diff:
```python
import functools

import jax
import jax.numpy as jnp
from jax import lax
from jax.experimental import pallas as pl
from jax.experimental.pallas import tpu as pltpu
from jax.sharding import PartitionSpec as P

epsilon = 1e-05
highest = lax.Precision.HIGHEST
f32 = jnp.float32
bf16 = jnp.bfloat16
LANES = 128
MIB = 1024 * 1024
BOTH = ("rep", "fsdp")


def exact_dot(a, b, dims=((1,), (0,))):
    return lax.dot_general(a, b, (dims, ((), ())), precision=highest, preferred_element_type=f32)


def low_dot(a, b, dims=((1,), (0,))):
    return lax.dot_general(
        a.astype(bf16), b.astype(bf16), (dims, ((), ())), preferred_element_type=f32
    )


def iota(shape, dim):
    return lax.broadcasted_iota(jnp.int32, shape, dim)


def cost(microseconds):
    return pl.CostEstimate(flops=0, transcendentals=0, bytes_accessed=microseconds * 3500000)


def params():
    return pltpu.CompilerParams(vmem_limit_bytes=56 * MIB)


def in_vmem(n):
    return [pl.BlockSpec(memory_space=pltpu.VMEM)] * n


def in_smem(n):
    return [pl.BlockSpec(memory_space=pltpu.SMEM)] * n


def in_hbm(n):
    return [pl.BlockSpec(memory_space=pltpu.HBM)] * n


def source_chip(rank_ref, slot, place):
    first = jnp.where(rank_ref[1] == 0, 1, 2)
    step = (0, first, 3 - first, 3)[place]
    return rank_ref[2] ^ (4 * slot) ^ step


def in_rows(rank_ref, slot, place, rows):
    return pl.ds(pl.multiple_of(source_chip(rank_ref, slot, place) * rows, 16), rows)


def out_rows(rank_ref, slot, place, rows):
    chip = source_chip(rank_ref, slot, place)
    return pl.ds(pl.multiple_of((4 * (chip // 8) + chip % 4) * rows, 16), rows)


def in_copies(rank_ref, chunks, whole, sems):
    copies = []
    for at, chunk in enumerate(chunks):
        part = chunk.at[:, pl.ds(0, whole.shape[1])]
        if len(chunks) > 1:
            target = whole.at[in_rows(rank_ref, at // 4, at % 4, chunk.shape[0])]
        else:
            target = whole
        copies.append(pltpu.make_async_copy(part, target, sems.at[at]))
    return copies


def out_copies(rank_ref, chunks, whole, sems):
    copies = []
    width = whole.shape[1]
    for at, chunk in enumerate(chunks):
        part = chunk.at[:, pl.ds(chunk.shape[1] - width, width)]
        if len(chunks) > 1:
            target = whole.at[out_rows(rank_ref, at // 4 * 2, at % 4, chunk.shape[0])]
        else:
            target = whole
        copies.append(pltpu.make_async_copy(part, target, sems.at[at]))
    return copies


def in_grad_copies(rank_ref, chunks, whole, sems):
    if len(chunks) == 1:
        return [pltpu.make_async_copy(whole, chunks[0], sems.at[0])]
    copies = []
    width = whole.shape[1]
    rows = chunks[0].shape[0]
    for group, first_slot in enumerate((2, 0)):
        for side in range(2):
            for place in range(4):
                chunk = chunks[3 * group + min(place, 2)]
                held = chunk.at[pl.ds(rows * (place == 3), rows), pl.ds(side * width, width)]
                part = whole.at[in_rows(rank_ref, first_slot + side, place, rows)]
                copies.append(pltpu.make_async_copy(part, held, sems.at[len(copies)]))
    return copies


def out_grad_copies(rank_ref, chunks, whole, sems):
    if len(chunks) == 1:
        return [pltpu.make_async_copy(whole, chunks[0], sems.at[0])]
    copies = []
    rows = chunks[0].shape[0] // 2
    for place, chunk in enumerate(chunks):
        for at in range(2):
            part = whole.at[out_rows(rank_ref, 2 * at, place, rows)]
            copies.append(pltpu.make_async_copy(part, chunk.at[pl.ds(at * rows, rows)], sems.at[len(copies)]))
    return copies


def started(source, target, sem):
    copy = pltpu.make_async_copy(source, target, sem)
    copy.start()
    return copy


def token_copies(places, refs, target, start, rows, sems, first=0):
    width = target.shape[1]
    return [
        started(
            refs[ref].at[pl.ds(row + start, rows), pl.ds(0, width)],
            target.at[pl.ds(at * rows, rows)],
            sems.at[first + at],
        )
        for at, (ref, row) in enumerate(places)
    ]


def spread_marks(seg_ref, masks_ref, vis_ref):
    row, col = iota((LANES, LANES), 0), iota((LANES, LANES), 1)
    for seq in range(seg_ref.shape[0] // 16):
        rows = slice(seq * LANES, (seq + 1) * LANES)
        across = jnp.broadcast_to(seg_ref[16 * seq : 16 * seq + 1, :].astype(f32), (LANES, LANES))
        down = across.T
        vis_ref[rows, :] = ((across == down) & (row >= col)).astype(f32)
        for offset in range(1, masks_ref.shape[0] + 1):
            same = (pltpu.roll(down, offset, 0) == down) & (row >= offset)
            masks_ref[offset - 1, rows, :] = same.astype(f32)


def halves(core, even, odd):
    lane = iota(even.shape, 1)
    low = jnp.where(lane < LANES // 2, even, pltpu.roll(odd, LANES // 2, 1))
    high = jnp.where(lane < LANES // 2, pltpu.roll(even, LANES // 2, 1), odd)
    return jnp.where(core == 0, low, high)


def head_blocks(inner, group, at, side):
    start = 4 * inner * group + LANES * (8 * (at // 2) + 2 * (at % 2))
    first = pl.multiple_of(start + 4 * LANES * side, LANES)
    return pl.ds(first, LANES), pl.ds(pl.multiple_of(first + LANES, LANES), LANES)


def head_number(local, side, core):
    return 16 * (local // 4) + 8 * side + 2 * (local % 4) + core


def pack_kernel(inner, state, heads, rank_ref, in_ref, out_ref, keep_ref, give_ref):
    side, core = rank_ref[0], rank_ref[1]
    shared = 2 * state
    for target, of_side in ((keep_ref, side), (give_ref, 1 - side)):
        for group in range(2):
            for at in range(inner // LANES):
                even, odd = head_blocks(inner, group, at, of_side)
                lanes = slice(inner * group + LANES * at, inner * group + LANES * (at + 1))
                target[:, lanes] = halves(
                    core, in_ref[:, even].astype(f32), in_ref[:, odd].astype(f32)
                ).astype(bf16)
        target[:, 2 * inner : 2 * inner + shared] = in_ref[:, 8 * inner : 8 * inner + shared]
        shape = (4 * heads, LANES)
        local = iota(shape, 1)
        pick = (local < heads) & (iota(shape, 0) == head_number(local, of_side, core))
        steps = low_dot(in_ref[:, 8 * inner + shared :], pick.astype(f32))
        target[:, 2 * inner + shared : 2 * inner + shared + LANES] = steps.astype(bf16)
    rows = keep_ref.shape[0]
    lower, upper = out_ref[:rows].astype(f32), out_ref[rows:].astype(f32)
    keep_ref[:, 2 * inner + shared + LANES :] = jnp.where(core == 0, lower, upper).astype(bf16)


def prepare_kernel(
    inner, state, heads, head_dim,
    rank_ref, cw_in, cb_in, gate_in, norm_in, dt_in, alog_in, skip_in,
    cw_ref, cb_ref, gate_ref, norm_ref, heads_ref, skip_ref,
):
    side, core = rank_ref[0], rank_ref[1]

    def chosen(get):
        low, high = (halves(core, get(4 * of_side), get(4 * of_side + 1)) for of_side in range(2))
        return jnp.where(side == 0, low, high)

    for at in range(inner // LANES):
        first = 8 * (at // 2) + 2 * (at % 2)
        lanes = slice(LANES * at, LANES * (at + 1))
        cw_ref[:, lanes] = chosen(lambda b: cw_in[:, LANES * (first + b) : LANES * (first + b + 1)])
        cb_ref[:, lanes] = chosen(lambda b: cb_in[first + b : first + b + 1, :])
        gate_ref[:, lanes] = chosen(lambda b: gate_in[first + b : first + b + 1, :])
    cw_ref[:, inner:] = cw_in[:, 4 * inner :]
    for at in range(2 * state // LANES):
        row = 4 * inner // LANES + at
        cb_ref[:, inner + LANES * at : inner + LANES * (at + 1)] = cb_in[row : row + 1, :]
    for row in range(norm_in.shape[0]):
        norm_ref[:, LANES * row : LANES * (row + 1)] = norm_in[row : row + 1, :]
    shape = (4 * heads, LANES)
    local = iota(shape, 1)
    pick = ((local < heads) & (iota(shape, 0) == head_number(local, side, core))).astype(f32)
    rows = jnp.concatenate([dt_in[...], alog_in[...], skip_in[...], jnp.zeros((5, 4 * heads), f32)], axis=0)
    own = exact_dot(rows, pick)
    heads_ref[...] = own
    spread = (iota((LANES, inner), 1) // head_dim == iota((LANES, inner), 0)).astype(f32)
    skip_ref[...] = exact_dot(own, spread)[2:3]


def unpack_kernel(
    inner, state, heads, model, taps,
    rank_ref, mine_ref, other_ref, small_mine_ref, small_other_ref,
    in_ref, out_ref, conv_ref, bias_ref, gate_ref, gain_ref, *head_refs,
):
    side, core = rank_ref[0], rank_ref[1]
    width = 2 * inner + 2 * state + LANES
    shared = 2 * state

    def both(start, end):
        mine, other = mine_ref[:, start:end], other_ref[:, start:end]
        return jnp.where(core == 0, mine, other), jnp.where(core == 0, other, mine)

    tails = [None, None]
    for offset, of_side in ((0, side), (width + model, 1 - side)):
        for group in range(2):
            for at in range(inner // LANES):
                start = offset + inner * group + LANES * at
                first, second = both(start, start + LANES)
                even, odd = head_blocks(inner, group, at, of_side)
                in_ref[:, even] = halves(0, first, second)
                in_ref[:, odd] = halves(1, first, second)
        start = offset + 2 * inner
        first, second = both(start, start + shared)
        keys = first + second
        start += shared
        first, second = both(start, start + LANES)
        row, col = iota((LANES, LANES), 0), iota((LANES, LANES), 1)
        steps = exact_dot(
            first, ((row < heads) & (col == head_number(row, of_side, 0))).astype(f32)
        ) + exact_dot(second, ((row < heads) & (col == head_number(row, of_side, 1))).astype(f32))
        tails[0 if offset == 0 else 1] = (keys, steps)
    in_ref[:, 8 * inner : 8 * inner + shared] = tails[0][0] + tails[1][0]
    in_ref[:, 8 * inner + shared :] = (tails[0][1] + tails[1][1])[:, : 4 * heads]
    rows = mine_ref.shape[0]
    first, second = both(width, width + model)
    out_ref[:rows, :] = first
    out_ref[rows:, :] = second

    def small_both(start, end):
        mine, other = small_mine_ref[:, start:end], small_other_ref[:, start:end]
        return jnp.where(core == 0, mine, other), jnp.where(core == 0, other, mine)

    row, col = iota((LANES, LANES), 0), iota((LANES, LANES), 1)
    small_width = small_mine_ref.shape[1] // 2
    for of_side in range(2):
        offset = small_width * jnp.where(side == of_side, 0, 1)
        for at in range(inner // LANES):
            lanes = pl.ds(pl.multiple_of(offset + LANES * at, LANES), LANES)
            mine, other = small_mine_ref[:, lanes], small_other_ref[:, lanes]
            first, second = jnp.where(core == 0, mine, other), jnp.where(core == 0, other, mine)
            place = 8 * (at // 2) + 4 * of_side + 2 * (at % 2)
            for step in range(2):
                block = halves(step, first, second)
                conv_ref[:, LANES * (place + step) : LANES * (place + step + 1)] = block[:taps]
                bias_ref[place + step : place + step + 1, :] = block[taps : taps + 1]
                gate_ref[place + step : place + step + 1, :] = block[taps + 1 : taps + 2]
    shared_blocks = []
    for at in range(inner // LANES, small_width // LANES):
        sides = []
        for of_side in range(2):
            start = small_width * of_side + LANES * at
            first, second = small_both(start, start + LANES)
            sides.append(first + second)
        shared_blocks.append(sides[0] + sides[1])
    for at, block in enumerate(shared_blocks[: shared // LANES]):
        place = 4 * inner // LANES + at
        conv_ref[:, LANES * place : LANES * (place + 1)] = block[:taps]
        bias_ref[place : place + 1, :] = block[taps : taps + 1]
    gain_ref[...] = shared_blocks[shared // LANES]
    scatter_sides = (side, 1 - side)
    for kind in range(3):
        total = jnp.zeros((8, LANES), f32)
        for at, of_side in enumerate(scatter_sides):
            start = small_width * at + LANES * kind
            first, second = small_both(start, start + LANES)
            for of_core, part in enumerate((first, second)):
                pick = (row < heads) & (col == head_number(row, of_side, of_core))
                total = total + exact_dot(part, pick.astype(f32))
        head_refs[kind][...] = total[taps + 2 : taps + 3, : 4 * heads]


def silu_parts(v):
    sig = 1.0 / (1.0 + jnp.exp(-v))
    return sig, v * sig


def conv_block(proj_ref, masks_ref, cw_ref, cb_ref, inner, at):
    signal = proj_ref[:, pl.ds(pl.multiple_of(inner + at * LANES, LANES), LANES)]
    lanes = pl.ds(pl.multiple_of(at * LANES, LANES), LANES)
    taps = cw_ref.shape[0]
    mixed = cb_ref[:, lanes] + cw_ref[taps - 1 : taps, lanes] * signal
    for offset in range(1, taps):
        earlier = pltpu.roll(signal, offset, 0) * masks_ref[offset - 1]
        mixed = mixed + cw_ref[taps - 1 - offset : taps - offset, lanes] * earlier
    return signal, mixed


def decay_prep(proj_ref, heads_ref, inner, head_dim, stepe_ref, cume_ref, cumt_ref):
    tokens, width = proj_ref.shape
    raw = proj_ref[:, width - LANES :] + heads_ref[0:1, :]
    step = jnp.maximum(raw, 0.0) + jnp.log1p(jnp.exp(-jnp.abs(raw)))
    decay = -step * jnp.exp(heads_ref[1:2, :])
    lower = (iota((LANES, LANES), 0) >= iota((LANES, LANES), 1)).astype(f32)
    spread = (
        iota((LANES, inner), 1) // head_dim == iota((LANES, inner), 0)
    ).astype(f32)
    stepe_ref[...] = exact_dot(step, spread)
    for seq in range(tokens // LANES):
        rows = slice(seq * LANES, (seq + 1) * LANES)
        cumul = exact_dot(lower, decay[rows])
        cume_ref[rows, :] = exact_dot(cumul, spread)
        turned = cumul.T
        for pair in range(inner // LANES):
            cumt_ref[pair, 0:2, rows] = turned[2 * pair : 2 * pair + 2]
    return raw, step, decay


def pair_weights(cume_ref, cumt_ref, vis_ref, rows, lanes, pair, half):
    cols = cume_ref[rows, lanes]
    seen = vis_ref[rows, :] > 0.5
    first, second = cumt_ref[pair, 0:1, rows], cumt_ref[pair, 1:2, rows]
    fade_a = jnp.exp(jnp.where(seen, cols[:, 0:1] - first, -1e30))
    fade_b = jnp.exp(jnp.where(seen, cols[:, half : half + 1] - second, -1e30))
    return fade_a, fade_b


def split_heads(block, half):
    lane = iota(block.shape, 1)
    return jnp.concatenate(
        [jnp.where(lane < half, block, 0.0), jnp.where(lane >= half, block, 0.0)], axis=0
    )


def forward_kernel(
    places, in_count, out_count, inner, head_dim,
    rank_ref, gain_ref, gate_gain_ref, cw_ref, cb_ref, heads_ref, skip_ref, *rest,
):
    token_count = 1 + max(ref for ref, _ in places)
    token_rows, rest = rest[:token_count], rest[token_count:]
    in_chunks, out_chunks = rest[:in_count], rest[in_count : in_count + out_count]
    (sums_ref, normed_out, proj_out, mixer_out, dgated_out,
     normed_ref, proj_ref, mixer_ref, dgated_ref, w_ref, w_out_ref, act_ref, stepe_ref, cume_ref,
     cumt_ref, score_ref, sq_ref, cross_ref, masks_ref, vis_ref, tok_ref, cot_ref, seg_ref,
     in_sems, out_sems, store_sems, token_sems) = (
        rest[in_count + out_count :]
    )
    count = len(places)
    tokens_in = token_copies(places, token_rows, tok_ref, 0, LANES, token_sems)
    tokens_in += token_copies(places, token_rows, seg_ref, 2 * LANES, 16, token_sems, count)
    cot_in = token_copies(places, token_rows, cot_ref, LANES, LANES, token_sems, 2 * count)
    copies = in_copies(rank_ref, in_chunks, w_ref, in_sems)
    copies += out_copies(rank_ref, out_chunks, w_out_ref, out_sems)
    for copy in copies:
        copy.start()
    for copy in tokens_in:
        copy.wait()
    hidden = tok_ref[...].astype(f32)
    factor = lax.rsqrt(jnp.mean(hidden * hidden, axis=-1, keepdims=True) + epsilon)
    normed_ref[...] = (hidden * factor * gain_ref[...]).astype(bf16)
    stores = [started(normed_ref, normed_out, store_sems.at[0])]
    spread_marks(seg_ref, masks_ref, vis_ref)
    for copy in copies + cot_in:
        copy.wait()
    tokens, width = proj_ref.shape
    for start in range(0, width, 512):
        end = min(start + 512, width)
        proj_ref[:, start:end] = jnp.dot(
            normed_ref[...], w_ref[:, start:end], preferred_element_type=f32
        )
    for start in range(0, inner, 256):
        lanes = slice(start, start + 256)
        dgated_ref[:, lanes] = low_dot(cot_ref[...], w_out_ref[lanes, :], ((1,), (1,)))
    stores.append(started(proj_ref, proj_out, store_sems.at[1]))
    stores.append(started(dgated_ref, dgated_out, store_sems.at[2]))
    decay_prep(proj_ref, heads_ref, inner, head_dim, stepe_ref, cume_ref, cumt_ref)

    def convolve(at, _):
        signal, mixed = conv_block(proj_ref, masks_ref, cw_ref, cb_ref, inner, at)
        act_ref[:, pl.ds(pl.multiple_of(at * LANES, LANES), LANES)] = silu_parts(mixed)[1]
        return 0

    lax.fori_loop(0, act_ref.shape[1] // LANES, convolve, 0)
    seqs = tokens // LANES
    for seq in range(seqs):
        rows = slice(seq * LANES, (seq + 1) * LANES)
        keys = act_ref[rows, inner : inner + LANES]
        queries = act_ref[rows, inner + LANES :]
        score_ref[rows, :] = exact_dot(queries, keys, ((1,), (1,)))
    sq_ref[...] = jnp.zeros_like(sq_ref)
    cross_ref[...] = jnp.zeros_like(cross_ref)

    def scan(pair, _):
        lanes = pl.ds(pl.multiple_of(pair * LANES, LANES), LANES)
        skip = skip_ref[:, lanes]
        for seq in range(seqs):
            rows = slice(seq * LANES, (seq + 1) * LANES)
            fade_a, fade_b = pair_weights(cume_ref, cumt_ref, vis_ref, rows, lanes, pair, head_dim)
            score = score_ref[rows, :]
            weights = jnp.concatenate([fade_a * score, fade_b * score], axis=1)
            values = act_ref[rows, lanes]
            scaled = split_heads(values * stepe_ref[rows, lanes], head_dim)
            mixed = low_dot(weights, scaled) + skip * values
            mixer_ref[rows, lanes] = mixed
            product = mixed * silu_parts(proj_ref[rows, lanes])[1]
            sq_ref[rows, :] += product * product
            cross_ref[rows, :] += product * gate_gain_ref[:, lanes] * dgated_ref[rows, lanes]
        return 0

    lax.fori_loop(0, inner // LANES, scan, 0)
    stores.append(started(mixer_ref, mixer_out, store_sems.at[3]))
    for seq in range(seqs):
        rows = slice(seq * LANES, (seq + 1) * LANES)
        sums_ref[seq : seq + 1, :] = jnp.sum(sq_ref[rows, :].T, axis=0, keepdims=True)
        at = seqs + seq
        sums_ref[at : at + 1, :] = jnp.sum(cross_ref[rows, :].T, axis=0, keepdims=True)
    for copy in stores:
        copy.wait()


def gated_kernel(
    places, chunk_count, grad_count, inner, full_inner,
    rank_ref, sums_ref, gain_ref, proj_in, mixer_in, *rest,
):
    token_count = 1 + max(ref for ref, _ in places)
    token_rows, rest = rest[:token_count], rest[token_count:]
    chunks = rest[:chunk_count]
    block_ref = rest[chunk_count]
    grads = rest[chunk_count + 1 : chunk_count + 1 + grad_count]
    (proj_ref, mixer_ref, gated_ref, factor_ref, w_out_ref, grad_ref, cot_ref, sems, grad_sems, load_sems,
     token_sems) = (
        rest[chunk_count + 1 + grad_count :]
    )
    loads = [
        started(proj_in.at[:, pl.ds(0, inner)], proj_ref, load_sems.at[0]),
        started(mixer_in, mixer_ref, load_sems.at[1]),
    ]
    loads += token_copies(places, token_rows, cot_ref, LANES, LANES, token_sems)
    weights = out_copies(rank_ref, chunks, w_out_ref, sems)
    for copy in weights:
        copy.start()
    tokens = proj_ref.shape[0]
    seqs = tokens // LANES
    for seq in range(seqs):
        row = lax.rsqrt(sums_ref[seq : seq + 1, :] / full_inner + epsilon)
        factor_ref[seq * LANES : (seq + 1) * LANES, :] = jnp.broadcast_to(row, (LANES, LANES)).T
    for copy in loads:
        copy.wait()
    for start in range(0, inner, LANES):
        lanes = slice(start, start + LANES)
        product = mixer_ref[:, lanes] * silu_parts(proj_ref[:, lanes])[1]
        gated_ref[:, lanes] = (product * factor_ref[...] * gain_ref[:, lanes]).astype(bf16)
    for start in range(0, inner, 256):
        lanes = slice(start, start + 256)
        grad_ref[lanes, :] = low_dot(gated_ref[:, lanes], cot_ref[...], ((0,), (0,))).astype(bf16)
    copies = out_grad_copies(rank_ref, grads, grad_ref, grad_sems)
    for copy in copies:
        copy.start()
    for copy in weights:
        copy.wait()
    block_ref[...] = jnp.dot(gated_ref[...], w_out_ref[...], preferred_element_type=f32)
    for copy in copies:
        copy.wait()


def backward_kernel(
    places, weight_count, chunk_count, inner, head_dim, full_inner,
    rank_ref, sums_ref, gain_ref, cw_ref, cb_ref, heads_ref, skip_ref,
    normed_in, proj_in, mixer_in, dgated_in, *rest,
):
    token_count = 1 + max(ref for ref, _ in places)
    token_rows, rest = rest[:token_count], rest[token_count:]
    weight_chunks = rest[:weight_count]
    rest = rest[weight_count:]
    dnormed_ref, small_ref = rest[:2]
    chunks = rest[2 : 2 + chunk_count]
    (normed_ref, proj_ref, mixer_ref, dgated_ref, masks_ref, vis_ref, dact_ref,
     act_ref, stepe_ref, cume_ref, cumt_ref, score_ref, dscore_ref, dstep_ref,
     rowsum_ref, colsum_ref, turned_ref, dskip_ref, factor_ref, pull_ref, turned_normed_ref, grad_ref,
     w_ref, dproj_ref, tok_ref, seg_ref, weight_sems, sems, load_sems, token_sems) = (
        rest[2 + chunk_count :]
    )
    seg_in = token_copies(places, token_rows, seg_ref, 2 * LANES, 16, token_sems)
    loads = [
        started(source, target, load_sems.at[at])
        for at, (source, target) in enumerate(
            ((proj_in, proj_ref), (mixer_in, mixer_ref), (dgated_in, dgated_ref), (normed_in, normed_ref))
        )
    ]
    weights = in_copies(rank_ref, weight_chunks, w_ref, weight_sems)
    for copy in weights:
        copy.start()
    weights += token_copies(places, token_rows, tok_ref, 0, LANES, token_sems, len(places))
    for copy in seg_in:
        copy.wait()
    spread_marks(seg_ref, masks_ref, vis_ref)
    loads[0].wait()
    tokens, width = proj_ref.shape
    seqs = tokens // LANES
    raw, step, decay = decay_prep(
        proj_ref, heads_ref, inner, head_dim, stepe_ref, cume_ref, cumt_ref
    )
    small_ref[...] = jnp.zeros_like(small_ref)

    def convolve(at, _):
        signal, mixed = conv_block(proj_ref, masks_ref, cw_ref, cb_ref, inner, at)
        act_ref[:, pl.ds(pl.multiple_of(at * LANES, LANES), LANES)] = silu_parts(mixed)[1]
        return 0

    lax.fori_loop(0, act_ref.shape[1] // LANES, convolve, 0)
    for seq in range(seqs):
        rows = slice(seq * LANES, (seq + 1) * LANES)
        keys = act_ref[rows, inner : inner + LANES]
        queries = act_ref[rows, inner + LANES :]
        score_ref[rows, :] = exact_dot(queries, keys, ((1,), (1,)))
    dscore_ref[...] = jnp.zeros_like(dscore_ref)
    dstep_ref[...] = jnp.zeros_like(dstep_ref)
    rowsum_ref[...] = jnp.zeros_like(rowsum_ref)
    turned_ref[...] = jnp.zeros_like(turned_ref)
    dskip_ref[...] = jnp.zeros_like(dskip_ref)
    for seq in range(seqs):
        rows = slice(seq * LANES, (seq + 1) * LANES)
        row = lax.rsqrt(sums_ref[seq : seq + 1, :] / full_inner + epsilon)
        pulled = row * row * row * sums_ref[seqs + seq : seqs + seq + 1, :] / full_inner
        factor_ref[rows, :] = jnp.broadcast_to(row, (LANES, LANES)).T
        pull_ref[rows, :] = jnp.broadcast_to(pulled, (LANES, LANES)).T

    def scan(pair, _):
        lanes = pl.ds(pl.multiple_of(pair * LANES, LANES), LANES)
        skip = skip_ref[:, lanes]
        gain = gain_ref[:, lanes]
        collect = (
            iota((LANES, LANES), 0) // head_dim + 2 * pair == iota((LANES, LANES), 1)
        ).astype(f32)
        dgain = jnp.zeros((1, LANES), f32)
        dskip = jnp.zeros((1, LANES), f32)
        for seq in range(seqs):
            rows = slice(seq * LANES, (seq + 1) * LANES)
            gate = proj_ref[rows, lanes]
            sig, gate_act = silu_parts(gate)
            mixed = mixer_ref[rows, lanes]
            product = mixed * gate_act
            dgated = dgated_ref[rows, lanes]
            factor = factor_ref[rows, :]
            dproduct = factor * gain * dgated - product * pull_ref[rows, :]
            dgain = dgain + jnp.sum(dgated * product * factor, axis=0, keepdims=True)
            dgate = dproduct * mixed * (sig * (1.0 + gate * (1.0 - sig)))
            dproj_ref[rows, lanes] = dgate.astype(bf16)
            dmixed = dproduct * gate_act
            values = act_ref[rows, lanes]
            stepe = stepe_ref[rows, lanes]
            dskip = dskip + jnp.sum(dmixed * values, axis=0, keepdims=True)
            fade_a, fade_b = pair_weights(cume_ref, cumt_ref, vis_ref, rows, lanes, pair, head_dim)
            score = score_ref[rows, :]
            weights_a, weights_b = fade_a * score, fade_b * score
            dsplit = split_heads(dmixed, head_dim)
            dweights = low_dot(dsplit, values * stepe, ((1,), (1,)))
            dweights_a, dweights_b = dweights[:LANES], dweights[LANES:]
            dscore_ref[rows, :] += dweights_a * fade_a + dweights_b * fade_b
            spread_a, spread_b = dweights_a * weights_a, dweights_b * weights_b
            lane = iota((LANES, LANES), 1)
            rowsum_ref[rows, :] += jnp.where(
                lane == 2 * pair,
                jnp.sum(spread_a, axis=1, keepdims=True),
                jnp.where(lane == 2 * pair + 1, jnp.sum(spread_b, axis=1, keepdims=True), 0.0),
            )
            colsum_ref[pair, 0:1, rows] = jnp.sum(spread_a, axis=0, keepdims=True)
            colsum_ref[pair, 1:2, rows] = jnp.sum(spread_b, axis=0, keepdims=True)
            weights = jnp.concatenate([weights_a, weights_b], axis=0)
            dscaled = low_dot(weights, dsplit, ((0,), (0,)))
            dact_ref[rows, lanes] = dscaled * stepe + skip * dmixed
            dstep_ref[rows, :] += exact_dot(dscaled * values, collect)
        small_ref[5:6, lanes] = dgain
        dskip_ref[0:1, lanes] = dskip
        return 0

    for copy in loads[1:]:
        copy.wait()
    lax.fori_loop(0, inner // LANES, scan, 0)
    for pair in range(inner // LANES):
        turned_ref[2 * pair : 2 * pair + 2, :] = colsum_ref[pair, 0:2, :]
    upper = (iota((LANES, LANES), 0) <= iota((LANES, LANES), 1)).astype(f32)
    rate = jnp.exp(heads_ref[1:2, :])
    ddt = jnp.zeros((1, LANES), f32)
    dalog = jnp.zeros((1, LANES), f32)
    for seq in range(seqs):
        rows = slice(seq * LANES, (seq + 1) * LANES)
        keys = act_ref[rows, inner : inner + LANES]
        queries = act_ref[rows, inner + LANES :]
        dscore = dscore_ref[rows, :]
        dact_ref[rows, inner : inner + LANES] = exact_dot(dscore, queries, ((0,), (0,)))
        dact_ref[rows, inner + LANES :] = exact_dot(dscore, keys)
        dcumul = rowsum_ref[rows, :] - turned_ref[:, rows].T
        ddecay = exact_dot(upper, dcumul)
        dalog = dalog + jnp.sum(ddecay * decay[rows], axis=0, keepdims=True)
        dstep = dstep_ref[rows, :] - ddecay * rate
        draw = dstep / (1.0 + jnp.exp(-raw[rows]))
        ddt = ddt + jnp.sum(draw, axis=0, keepdims=True)
        dproj_ref[rows, width - LANES :] = draw.astype(bf16)
    gather = (
        iota((inner, LANES), 0) // head_dim == iota((inner, LANES), 1)
    ).astype(f32)
    dskip_heads = exact_dot(dskip_ref[...], gather)
    small_ref[6:7, 0:LANES] = ddt
    small_ref[6:7, LANES : 2 * LANES] = dalog
    small_ref[6:7, 2 * LANES : 3 * LANES] = dskip_heads[0:1]

    def convolve_back(at, _):
        lanes = pl.ds(pl.multiple_of(at * LANES, LANES), LANES)
        signal, mixed = conv_block(proj_ref, masks_ref, cw_ref, cb_ref, inner, at)
        sig, _unused = silu_parts(mixed)
        dmixed = dact_ref[:, lanes] * (sig * (1.0 + mixed * (1.0 - sig)))
        taps = cw_ref.shape[0]
        small_ref[taps : taps + 1, lanes] = jnp.sum(dmixed, axis=0, keepdims=True)
        small_ref[taps - 1 : taps, lanes] = jnp.sum(dmixed * signal, axis=0, keepdims=True)
        dsignal = cw_ref[taps - 1 : taps, lanes] * dmixed
        for offset in range(1, taps):
            masked = dmixed * masks_ref[offset - 1]
            place = taps - 1 - offset
            small_ref[place : place + 1, lanes] = jnp.sum(
                masked * pltpu.roll(signal, offset, 0), axis=0, keepdims=True
            )
            dsignal = dsignal + cw_ref[place : place + 1, lanes] * pltpu.roll(
                masked, tokens - offset, 0
            )
        dproj_ref[:, pl.ds(pl.multiple_of(inner + at * LANES, LANES), LANES)] = dsignal.astype(bf16)
        return 0

    lax.fori_loop(0, dact_ref.shape[1] // LANES, convolve_back, 0)
    for seq in range(seqs):
        rows = slice(seq * LANES, (seq + 1) * LANES)
        turned_normed_ref[:, rows] = normed_ref[rows, :].astype(f32).T.astype(bf16)
    for start in range(0, width, 512):
        lanes = slice(start, min(start + 512, width))
        grad_ref[:, lanes] = low_dot(turned_normed_ref[...], dproj_ref[:, lanes]).astype(bf16)
    copies = in_grad_copies(rank_ref, chunks, grad_ref, sems)
    for copy in copies:
        copy.start()
    for copy in weights:
        copy.wait()
    model = w_ref.shape[0]
    hidden = tok_ref[...].astype(f32)
    token_factor = lax.rsqrt(jnp.mean(hidden * hidden, axis=-1, keepdims=True) + epsilon)
    conv_width = dact_ref.shape[1]
    part = model // 8
    for start in range(0, model, 256):
        lanes = slice(start, start + 256)
        dnormed = low_dot(dproj_ref[...], w_ref[lanes, :], ((1,), (1,)))
        dnormed_ref[:, lanes] = dnormed
        dgain = jnp.sum(dnormed * hidden[:, lanes] * token_factor, axis=0, keepdims=True)
        for at in range(0, 256, part):
            row = (start + at) // part
            small_ref[row : row + 1, conv_width:] = dgain[:, at : at + part]
    for copy in copies:
        copy.wait()


def tail_kernel(tok_ref, cot_ref, gain_ref, mine_ref, other_ref, dtok_ref):
    hidden = tok_ref[...].astype(f32)
    factor = lax.rsqrt(jnp.mean(hidden * hidden, axis=-1, keepdims=True) + epsilon)
    dnormed = mine_ref[...] + other_ref[...]
    scaled = dnormed * gain_ref[...]
    pull = jnp.mean(scaled * hidden, axis=-1, keepdims=True) * factor * factor * factor
    dtok_ref[...] = cot_ref[...].astype(f32) + scaled * factor - hidden * pull


def after(x, *others):
    return lax.optimization_barrier((x, *others))[0]


class Links:
    first, second = (1, 2), (2, 1)
    slots = (0, 4, 8, 12)

    def __init__(self, reps, chips, paired):
        self.reps, self.chips, self.paired = reps, chips, paired
        self.rep = lax.axis_index("rep")
        self.chip = lax.axis_index("fsdp")
        self.side = self.chip // 4 % 2

    def exchange(self, x, masks):
        if isinstance(masks, int):
            masks = (masks, masks)
        pairs = [
            (core * self.chips + chip, core * self.chips + (chip ^ masks[core]))
            for core in range(self.reps)
            for chip in range(self.chips)
        ]
        return lax.ppermute(x, BOTH, pairs)

    def swap(self, x):
        return lax.ppermute(x, "rep", [(0, 1), (1, 0)])

    def spread(self, block):
        near = self.exchange(block, self.first)
        side = self.exchange(block, self.second)
        return [block, near, side, self.exchange(near, self.second)]

    def gather(self, keep, give):
        across = self.exchange(keep, self.slots[2])
        own = self.spread(keep)
        beside = self.exchange(give, self.slots[1])
        far = self.exchange(after(give, beside), self.slots[3])
        return [own, self.spread(beside), self.spread(across), self.spread(far)]

    def square(self, own, near, send):
        rows = own.shape[0]
        came = self.exchange(send, self.second)
        near = (near.astype(f32) + came[rows:].astype(f32)).astype(bf16)
        last = self.exchange(near, self.first)
        return own.astype(f32) + came[:rows].astype(f32) + last.astype(f32), came, last

    def square_at_once(self, own, near, side, far):
        moved = [self.exchange(near, self.first), self.exchange(side, self.second), self.exchange(far, 3)]
        return sum((x.astype(f32) for x in moved), own.astype(f32)), moved

    def across(self, x):
        return self.exchange(x.astype(bf16), self.slots[2]).astype(f32)

    def beside(self, x):
        return self.exchange(x.astype(bf16), self.slots[1]).astype(f32)

    def scatter(self, chunks, far, out, after_first, meanwhile):
        width = chunks[0].shape[1] // 2
        close, _, _ = self.square(*chunks[:2], after(chunks[2], after_first, out[1]))
        other = self.beside(after(close[:, width:] + far[:, width:], *meanwhile))
        return jnp.concatenate([close[:, :width] + far[:, :width], out[0] + out[1], other], axis=1)

    def sum_chips(self, x):
        for step in (1, 2, 8):
            x = x + self.exchange(x, step)
        return jnp.concatenate([x, self.exchange(x, 4)], axis=1)

    def group_rows(self, x, others):
        other = after(self.exchange(x, self.slots[1]), *others)
        return [x, self.swap(jnp.concatenate([x, other])), other]

    def from_reps(self, x):
        whole = lax.all_gather(x, "rep", axis=0)
        return [whole[at] for at in range(self.reps)]

    def sum_group(self, x):
        if not self.paired:
            return lax.psum(x, "rep")

        def reordered(y, bit):
            return jnp.concatenate([y[at ^ bit : (at ^ bit) + 1] for at in range(y.shape[0])])

        x = x + reordered(self.exchange(x, self.slots[1]), 2)
        return x + reordered(self.swap(x), 1)

    def from_side(self, x):
        return self.exchange(x[x.shape[0] // 2 :].astype(bf16), self.slots[1])

    def own_rows(self, x, came):
        rows = x.shape[0] // 4
        came = came.astype(f32)
        return x[:rows] + came[:rows], self.swap(x[rows : 2 * rows] + came[rows:])

    def scattered(self, x):
        mine = lax.psum_scatter(x, "rep", scatter_dimension=0, tiled=True)
        return mine, jnp.zeros_like(mine)


def per_device(
    reps, chips,
    tokens, segment_ids, norm_gain, in_weight, conv_weight, conv_bias, dt_bias, a_log, skip_gain,
    gate_gain, out_weight, cotangent,
):
    full_inner, full_heads = gate_gain.shape[0], dt_bias.shape[0]
    conv_dim, taps = conv_bias.shape[0], conv_weight.shape[0]
    model = norm_gain.shape[0]
    state = (conv_dim - full_inner) // 2
    head_dim = full_inner // full_heads
    rows_in, rows_out = in_weight.shape[0], out_weight.shape[0]
    paired = (reps, chips, full_heads) == (2, 16, 32) and rows_out == 2 * rows_in == 2 * head_dim
    ranks = 4 if paired else reps
    inner, heads = full_inner // ranks, full_heads // ranks
    links = Links(reps, chips, paired)
    rep, chip = links.rep, links.chip
    conv_local = inner + 2 * state
    width = inner + conv_local + LANES
    own_tokens = tokens.shape[0]
    total = own_tokens * ranks

    def arr(*shape, dtype=f32):
        return jax.ShapeDtypeStruct(shape, dtype)

    def vmem(*shape, dtype=f32):
        return pltpu.VMEM(shape, dtype)

    def own_heads(x, size):
        lead = x.shape[:-1]
        if paired:
            split = x.reshape(lead + (2, 2, 4, 2, size))
            split = lax.dynamic_index_in_dim(split, links.side, split.ndim - 4, False)
        else:
            split = x.reshape(lead + (heads, reps, size))
        split = lax.dynamic_index_in_dim(split, rep, split.ndim - 2, False)
        return split.reshape(lead + (heads * size,))

    def all_heads(parts, size):
        lead = parts[0].shape[:-1]
        if paired:
            split = [part.reshape(lead + (2, 1, 4, 1, size)) for part in parts]
            sides = [jnp.concatenate(split[at : at + 2], axis=-2) for at in (0, 2)]
            whole = jnp.concatenate(sides, axis=-4)
        else:
            whole = jnp.concatenate([part.reshape(lead + (heads, 1, size)) for part in parts], axis=-2)
        return whole.reshape(lead + (full_heads * size,))

    rank = jnp.stack([links.side, rep, chip]).astype(jnp.int32)
    if paired:
        keep, give = pl.pallas_call(
            functools.partial(pack_kernel, inner, state, heads),
            out_shape=[arr(rows_in, width + model, dtype=bf16), arr(rows_in, width, dtype=bf16)],
            in_specs=in_smem(1) + in_vmem(2),
            out_specs=in_vmem(2),
            compiler_params=params(),
            name="pack",
        )(rank, in_weight, out_weight)
        slots = links.gather(keep, give)
        first_rows = slots[1][0]
        conv_w, conv_b, gate_g, norm_g, head_rows, skip = pl.pallas_call(
            functools.partial(prepare_kernel, inner, state, heads, head_dim),
            out_shape=[
                arr(taps, conv_local), arr(1, conv_local), arr(1, inner), arr(1, model), arr(8, LANES),
                arr(1, inner),
            ],
            in_specs=in_smem(1) + in_vmem(7),
            out_specs=in_vmem(6),
            compiler_params=params(),
            name="prepare",
        )(rank, conv_weight, conv_bias.reshape(-1, LANES), gate_gain.reshape(-1, LANES),
          norm_gain.reshape(-1, LANES), dt_bias[None], a_log[None], skip_gain[None])
        in_chunks, out_chunks = sum(slots, []), slots[0] + slots[2]
        in_shapes = [(rows_in, 2 * width), (rows_in, 2 * width), (2 * rows_in, 2 * width)] * 2
        out_shapes = [(2 * rows_in, model)] * 4
    else:
        in_full = lax.all_gather(in_weight, "fsdp", axis=0, tiled=True)
        out_full = lax.all_gather(out_weight, "fsdp", axis=0, tiled=True)
        ends = [full_inner, 2 * full_inner, full_inner + conv_dim]
        gates, signals, shared, step_cols = jnp.split(in_full, ends, axis=1)
        in_chunks = [
            jnp.concatenate(
                [own_heads(gates, head_dim), own_heads(signals, head_dim), shared, own_heads(step_cols, 1),
                 jnp.zeros((model, LANES - heads), bf16)],
                axis=1,
            )
        ]
        out_chunks = [own_heads(out_full.T, head_dim).T]
        def local_conv(x):
            return jnp.concatenate([own_heads(x[:, :full_inner], head_dim), x[:, full_inner:]], axis=1)

        conv_w, conv_b = local_conv(conv_weight), local_conv(conv_bias[None])

        def lane_row(x):
            return jnp.pad(own_heads(x, 1), (0, LANES - heads))

        head_rows = jnp.pad(jnp.stack([lane_row(dt_bias), lane_row(a_log)]), ((0, 6), (0, 0)))
        skip = jnp.repeat(own_heads(skip_gain, 1), head_dim)[None]
        gate_g = own_heads(gate_gain, head_dim)[None]
        norm_g = norm_gain[None]
        in_shapes, out_shapes = [(model, width)], [(inner, model)]
    extra = jnp.pad(segment_ids.astype(bf16), ((0, 15), (0, model - segment_ids.shape[1])))
    own_rows = jnp.concatenate([tokens, cotangent, extra])
    held = own_rows.shape[0]
    if paired:
        own_rows = after(own_rows, first_rows)
        waits = slots[0][3:] + slots[1][1:3] + slots[2][1:3] + slots[3][:1]
        token_rows = links.group_rows(own_rows, waits)
        places = ((0, 0), (1, 0), (2, 0), (1, held))
    else:
        token_rows = links.from_reps(own_rows)
        places = tuple((at, 0) for at in range(reps))
    in_shapes = [arr(*shape, dtype=bf16) for shape in in_shapes]
    out_shapes = [arr(*shape, dtype=bf16) for shape in out_shapes]
    in_count, out_count = len(in_chunks), len(out_chunks)

    w_in, w_out = vmem(model, width, dtype=bf16), vmem(inner, model, dtype=bf16)
    in_sems, out_sems = (pltpu.SemaphoreType.DMA((n,)) for n in (in_count, out_count))
    def sems(n):
        return pltpu.SemaphoreType.DMA((n,))

    kept = [vmem(total, model, dtype=bf16), vmem(total, width), vmem(total, inner), vmem(total, inner)]
    tok, segs = vmem(total, model, dtype=bf16), vmem(16 * len(places), LANES, dtype=bf16)
    conv_masks = [vmem(taps - 1, total, LANES), vmem(total, LANES)]
    sums, normed, projected, mixed, d_gated = pl.pallas_call(
        functools.partial(forward_kernel, places, in_count, out_count, inner, head_dim),
        out_shape=[
            arr(2 * total // LANES, LANES), arr(total, model, dtype=bf16), arr(total, width),
            arr(total, inner), arr(total, inner),
        ],
        in_specs=in_smem(1) + in_vmem(6) + in_hbm(len(token_rows) + in_count + out_count),
        out_specs=in_vmem(1) + in_hbm(4),
        scratch_shapes=kept + [
            w_in, w_out,
            vmem(total, conv_local), vmem(total, inner), vmem(total, inner), vmem(inner // LANES, 8, total),
            vmem(total, LANES), vmem(total, LANES), vmem(total, LANES), *conv_masks,
            tok, tok, segs, in_sems, out_sems, sems(4), sems(3 * len(places)),
        ],
        compiler_params=params(),
        cost_estimate=cost(14),
        name="forward",
    )(rank, norm_g, gate_g, conv_w, conv_b, head_rows, skip, *token_rows, *in_chunks, *out_chunks)
    sums = links.sum_group(sums)
    block_part, *out_grads = pl.pallas_call(
        functools.partial(gated_kernel, places, out_count, len(out_shapes), inner, full_inner),
        out_shape=[arr(total, model)] + out_shapes,
        in_specs=in_smem(1) + in_vmem(2) + in_hbm(2 + len(token_rows) + out_count),
        out_specs=in_vmem(1) + in_hbm(len(out_shapes)),
        scratch_shapes=[
            vmem(total, inner), vmem(total, inner), vmem(total, inner, dtype=bf16), vmem(total, LANES), w_out,
            vmem(inner, model, dtype=bf16), tok, out_sems, out_sems, sems(2), sems(len(places)),
        ],
        compiler_params=params(),
        cost_estimate=cost(6),
        name="gated",
    )(rank, sums, gate_g, projected, mixed, *token_rows, *out_chunks)
    if paired:
        out_sums, moved = links.square_at_once(*out_grads)
        sums = after(sums, out_grads[2])
        block_came = links.from_side(block_part)
    d_normed, small, *in_grads = pl.pallas_call(
        functools.partial(backward_kernel, places, in_count, len(in_shapes), inner, head_dim, full_inner),
        out_shape=[arr(total, model), arr(8, conv_local + model // 8)] + in_shapes,
        in_specs=in_smem(1) + in_vmem(6) + in_hbm(4 + len(token_rows) + in_count),
        out_specs=in_vmem(2) + in_hbm(len(in_shapes)),
        scratch_shapes=kept + conv_masks + [
            vmem(total, conv_local),
            vmem(total, conv_local), vmem(total, inner), vmem(total, inner), vmem(inner // LANES, 8, total),
            vmem(total, LANES), vmem(total, LANES), vmem(total, LANES),
            vmem(total, LANES), vmem(inner // LANES, 8, total), vmem(LANES, total), vmem(8, inner),
            vmem(total, LANES), vmem(total, LANES), vmem(model, total, dtype=bf16), w_in, w_in,
            vmem(total, width, dtype=bf16), tok, segs, in_sems, in_sems, sems(4),
            sems(2 * len(places)),
        ],
        compiler_params=params(),
        cost_estimate=cost(24),
        name="backward",
    )(rank, sums, gate_g, conv_w, conv_b, head_rows, skip, normed, projected, mixed, d_gated, *token_rows,
      *in_chunks)

    if paired:
        far, came, last = links.square(*in_grads[:2], after(in_grads[2], block_came, *moved))
        far = links.across(far)
        out_parts = out_sums[:rows_in], links.across(out_sums[rows_in:])
        small = links.sum_chips(after(small, last))
        small_other = links.swap(small)
        d_normed_parts = links.own_rows(d_normed, after(links.from_side(d_normed), last))
        block_parts = links.own_rows(block_part, block_came)
    else:
        out_sum, in_sum = (
            lax.psum_scatter(grads[0], "fsdp", scatter_dimension=0, tiled=True).astype(f32)
            for grads in (out_grads, in_grads)
        )
        smalls = links.from_reps(lax.psum(small, "fsdp"))
        d_normed_parts, block_parts = links.scattered(d_normed), links.scattered(block_part)
    d_tokens = pl.pallas_call(
        tail_kernel,
        out_shape=arr(own_tokens, model),
        in_specs=in_vmem(5),
        out_specs=in_vmem(1)[0],
        compiler_params=params(),
        cost_estimate=cost(2),
        name="tail",
    )(tokens, cotangent, norm_g, *d_normed_parts)
    block_out = (tokens.astype(f32) + (block_parts[0] + block_parts[1])).astype(bf16)

    if paired:
        grad_sum = links.scatter(
            in_grads[3:], far, out_parts, came, [d_tokens, block_out, small_other]
        )
        d_in_weight, d_out_weight, d_conv_weight, d_conv_bias, d_gate_gain, d_norm_gain, *by_head = pl.pallas_call(
            functools.partial(unpack_kernel, inner, state, heads, model, taps),
            out_shape=[
                arr(*in_weight.shape), arr(*out_weight.shape), arr(taps, conv_dim), arr(conv_dim // LANES, LANES),
                arr(full_inner // LANES, LANES), arr(8, model // 8), *[arr(1, full_heads)] * 3,
            ],
            in_specs=in_smem(1) + in_vmem(4),
            out_specs=in_vmem(9),
            compiler_params=params(),
            name="unpack",
        )(rank, grad_sum, links.swap(grad_sum), small, small_other)
        d_conv_bias, d_gate_gain, d_norm_gain = (x.reshape(-1) for x in (d_conv_bias, d_gate_gain, d_norm_gain))
        d_dt_bias, d_a_log, d_skip_gain = (x.reshape(-1) for x in by_head)
    else:
        parts = [part[:, :inner] for part in smalls]
        shared = sum(part[:, inner:] for part in smalls)
        d_norm_gain = shared[:, 2 * state :].reshape(-1)
        d_conv = jnp.concatenate([all_heads(parts, head_dim), shared[:, : 2 * state]], axis=1)
        d_conv_weight, d_conv_bias = d_conv[:taps], d_conv[taps]
        d_gate_gain = d_conv[taps + 1, :full_inner]
        d_dt_bias, d_a_log, d_skip_gain = (
            all_heads([part[taps + 2, at * LANES : at * LANES + heads] for part in parts], 1) for at in range(3)
        )
        in_parts = links.from_reps(in_sum)
        mid = 2 * inner
        end = mid + 2 * state
        d_in_weight = jnp.concatenate(
            [
                all_heads([part[:, :inner] for part in in_parts], head_dim),
                all_heads([part[:, inner:mid] for part in in_parts], head_dim),
                sum(part[:, mid:end] for part in in_parts),
                all_heads([part[:, end : end + heads] for part in in_parts], 1),
            ],
            axis=1,
        )
        held = links.from_reps(lax.all_gather(out_sum, "fsdp", axis=0, tiled=True))
        whole = all_heads([part.T for part in held], head_dim).T
        d_out_weight = lax.dynamic_slice_in_dim(whole, chip * rows_out, rows_out, 0)
    return (
        block_out, d_tokens, d_norm_gain, d_in_weight, d_conv_weight, d_conv_bias, d_dt_bias, d_a_log,
        d_skip_gain, d_gate_gain, d_out_weight,
    )


def solution(mesh):
    rows = P(("rep", "fsdp"), None)
    in_specs = (
        rows, rows, P(), P("fsdp", None), P(), P(), P(), P(), P(), P(), P("fsdp", None), rows,
    )
    out_specs = (
        rows, rows, P(), P("fsdp", None), P(), P(), P(), P(), P(), P(), P("fsdp", None),
    )
    reps, chips = mesh.shape["rep"], mesh.shape["fsdp"]
    return jax.shard_map(
        functools.partial(per_device, reps, chips),
        mesh=mesh, in_specs=in_specs, out_specs=out_specs, check_vma=False,
    )
```

time: 294 us -> 178 us (0.61)
  starting transfers between devices: 122 us -> 44.9 us
  waiting for transfers between devices: 83.4 us -> 66.1 us
  local copies, waits for them, and re-layouts: 18.5 us -> 5.05 us
  other arithmetic: 12.9 us -> 6.63 us
    ppermute x72 -> x33, starting transfers between devices: 118 us -> 44.7 us  [exchange(): return lax.ppermute(x, BOTH, pairs)]
    ppermute x72 -> x33, waiting for transfers between devices: 75.3 us -> 62.4 us  [exchange(): return lax.ppermute(x, BOTH, pairs)]
    unnamed x138 -> x68, local copies, waits for them, and re-layouts: 8.87 us -> 3.64 us
    ppermute x2 -> x0, waiting for transfers between devices: 5.14 us -> none  [the longest x1 5.14 us: per_device(): came = lax.ppermute(away, BOTH, moves)]
    dynamic_slice x10 -> x0, local copies, waits for them, and re-layouts: 4.62 us -> none  [the longest x2 2.46 us: own_rows(): theirs = lax.dynamic_slice_in_dim(x, (1 - self.rep) * rows, rows, 0)]
    ppermute x2 -> x0, starting transfers between devices: 3.3 us -> none  [the longest x1 2.01 us: per_device(): came = lax.ppermute(away, BOTH, moves)]
    pallas_call x6 -> x7, Pallas kernels: 55 us -> 53 us  [the longest x1 22.9 us: per_device(): pl.pallas_call(functools.partial(backward_kernel, places, in_count, len(i...]
  transfers between devices with their start and end apart: 85 -> 39, of which waited for: 29 -> 18; matrix products, arithmetic and copies ran while one was open for 6% -> 3% of each run, Pallas kernels for 16% -> 15%
where the time goes in v2:
time: 178 us; the launch traced here: 177 us
  waiting for transfers between devices  66.1 us (37%)
  Pallas kernels  53 us (30%)
  starting transfers between devices  44.9 us (25%)
  other arithmetic  6.63 us (4%)
  local copies, waits for them, and re-layouts  5.05 us (3%)
    ppermute x33, waiting for transfers between devices, exchange(): return lax.ppermute(x, BOTH, pairs)  62.4 us
    ppermute x33, starting transfers between devices, exchange(): return lax.ppermute(x, BOTH, pairs)  44.7 us
    pallas_call x1, Pallas kernels, per_device(): pl.pallas_call(functools.partial(backward_kernel, places, in_count, len(i...  22.9 us
    pallas_call x1, Pallas kernels, per_device(): pl.pallas_call(functools.partial(forward_kernel, places, in_count, out_co...  14.1 us
    pallas_call x1, Pallas kernels, per_device(): pl.pallas_call(functools.partial(gated_kernel, places, out_count, len(out...  6.42 us
    ppermute x6, waiting for transfers between devices, swap(): return lax.ppermute(x, 'rep', [(0, 1), (1, 0)])  3.72 us
    unnamed x68, local copies, waits for them, and re-layouts  3.64 us
  transfers between devices with their start and end apart: 39, of which 18 were waited for; matrix products, arithmetic and copies ran while one was open for 3% of the time, Pallas kernels for 15%

profile of v2, /device:TPU:0, one launch (start us, length us, event | category | flops | bytes accessed | tf_op | source)
XLA Modules:
  0.0 177.1 jit_solution(9448645651759960275)
XLA Ops:
  1.3 2.2 %pack.1 = (bf16[64,2432]{1,0:T(8,128)(2,1)}, bf16[64,1408]{1,0:T(8,128)(2,1)}) custom-call(s32[3]{0:T(128)} %pad_add_fusion.rank_ref, bf16[64,4384]{1,0:T(8,128)(2,1)} %in_ref.1, bf16[128,1024]{1,0:T(8,128)(2,1)} %out_ref.1), custom_call_target="tpu_custom_call" | custom-call | tf_op jit(solution)/shard_map/pack/pallas_call | solution.py:836
  3.5 3.0 %collective-permute-start = (bf16[64,1408]{1,0:T(8,128)(2,1)}, bf16[64,1408]{1,0:T(8,128)(2,1)S(1)}, u32[]{:S(2)}, u32[]{:S(2)}) collective-permute-start(bf16[64,1408]{1,0:T(8,128)(2,1)} %get-tuple-element.64), channel_id=1, source_target_pairs={{0,4},{1,5},{2,6},{3,7},{4,0},{5,1},{6,2},{7,3},{8,12},{9,13},{10,... | collective-permute-start | bytes 540680 | tf_op jit(solution)/shard_map/ppermute | solution.py:711
  6.5 1.5 collective-permute-start.2
  8.0 2.6 %collective-permute-start.6 = (bf16[64,2432]{1,0:T(8,128)(2,1)}, bf16[64,2432]{1,0:T(8,128)(2,1)S(1)}, u32[]{:S(2)}, u32[]{:S(2)}) collective-permute-start(bf16[64,2432]{1,0:T(8,128)(2,1)} %get-tuple-element.63.rest_3_.rest_19_), channel_id=1, source_target_pairs={{0,8},{1,9},{2,10},{3,11},{4,12},{5,13},{6,14},{7,15},{8,0},{9,1},... | collective-permute-start | bytes 933896 | tf_op jit(solution)/shard_map/ppermute | solution.py:711
  11.2 1.1 fusion.1.rest_0_
  13.2 1.5 collective-permute-start.4
  14.7 3.2 %collective-permute-start.5 = (bf16[64,1408]{1,0:T(8,128)(2,1)S(1)}, bf16[64,1408]{1,0:T(8,128)(2,1)S(1)}, u32[]{:S(2)}, u32[]{:S(2)}) collective-permute-start(bf16[64,1408]{1,0:T(8,128)(2,1)S(1)} %collective-permute-done.rest_7_), channel_id=1, source_target_pairs={{0,2},{1,3},{2,0},{3,1},{4,6},{5,7},{6,4},{7,5},{8,10},{9,11},{10,... | collective-permute-start | bytes 540680 | tf_op jit(solution)/shard_map/ppermute | solution.py:711
  18.0 6.5 %collective-permute-done.6.rest_11_.rest_23_.rest_7_ = bf16[64,2432]{1,0:T(8,128)(2,1)S(1)} collective-permute-done((bf16[64,2432]{1,0:T(8,128)(2,1)}, bf16[64,2432]{1,0:T(8,128)(2,1)S(1)}, u32[]{:S(2)}, u32[]{:S(2)}) %collective-permute-start.6) | collective-permute-done | bytes 311328 | tf_op jit(solution)/shard_map/ppermute | solution.py:711
  24.5 1.5 collective-permute-start.7
  26.5 2.5 %collective-permute-start.9 = (bf16[64,1408]{1,0:T(8,128)(2,1)}, bf16[64,1408]{1,0:T(8,128)(2,1)S(1)}, u32[]{:S(2)}, u32[]{:S(2)}) collective-permute-start(bf16[64,1408]{1,0:T(8,128)(2,1)} %get-tuple-element.64), channel_id=1, source_target_pairs={{0,12},{1,13},{2,14},{3,15},{4,8},{5,9},{6,10},{7,11},{8,4},{9,5},... | collective-permute-start | bytes 540680 | tf_op jit(solution)/shard_map/ppermute | solution.py:711
  29.0 7.0 %collective-permute-done.9.rest_15_ = bf16[64,1408]{1,0:T(8,128)(2,1)S(1)} collective-permute-done((bf16[64,1408]{1,0:T(8,128)(2,1)}, bf16[64,1408]{1,0:T(8,128)(2,1)S(1)}, u32[]{:S(2)}, u32[]{:S(2)}) %collective-permute-start.9) | collective-permute-done | bytes 180256 | tf_op jit(solution)/shard_map/ppermute | solution.py:711
  36.9 1.5 collective-permute-start.11
  38.4 1.5 collective-permute-start.14
  40.4 1.5 collective-permute-start.12
  41.9 3.8 %collective-permute-done.11.rest_5_.rest_21_ = bf16[64,2432]{1,0:T(8,128)(2,1)S(1)} collective-permute-done((bf16[64,2432]{1,0:T(8,128)(2,1)S(1)}, bf16[64,2432]{1,0:T(8,128)(2,1)S(1)}, u32[]{:S(2)}, u32[]{:S(2)}) %collective-permute-start.11) | collective-permute-done | bytes 311328 | tf_op jit(solution)/shard_map/ppermute | solution.py:711
  45.7 1.5 collective-permute-start.15
  47.7 1.8 prepare.1
  49.5 1.5 collective-permute-done.12.rest_10_
  51.0 1.9 %collective-permute-done.15.rest_17_ = bf16[64,1408]{1,0:T(8,128)(2,1)S(1)} collective-permute-done((bf16[64,1408]{1,0:T(8,128)(2,1)S(1)}, bf16[64,1408]{1,0:T(8,128)(2,1)S(1)}, u32[]{:S(2)}, u32[]{:S(2)}) %collective-permute-start.15) | collective-permute-done | bytes 180256 | tf_op jit(solution)/shard_map/ppermute | solution.py:711
  52.9 1.9 %collective-permute-done.16.rest_18_ = bf16[64,1408]{1,0:T(8,128)(2,1)S(1)} collective-permute-done((bf16[64,1408]{1,0:T(8,128)(2,1)S(1)}, bf16[64,1408]{1,0:T(8,128)(2,1)S(1)}, u32[]{:S(2)}, u32[]{:S(2)}) %collective-permute-start.16) | collective-permute-done | bytes 180256 | tf_op jit(solution)/shard_map/ppermute | solution.py:711
  56.0 14.1 %forward.1 = (f32[8,128]{1,0:T(8,128)}, bf16[512,1024]{1,0:T(8,128)(2,1)}, f32[512,1408]{1,0:T(8,128)}, f32[512,512]{1,0:T(8,128)}, f32[512,512]{1,0:T(8,128)}) custom-call(s32[3]{0:T(128)} %pad_add_fusion.rank_ref, f32[1,1024]{1,0:T(1,128)} %get-tuple-element.55.gain_ref, f32[1,512]{1,0:T(1,128)} %get-tuple-element.56.gate_gain_ref.gain_ref, ...), custom_call_target="tpu_custom_call" | custom-call | bytes 49000000 | tf_op jit(solution)/shard_map/forward/pallas_call | solution.py:910
  70.2 3.8 %collective-permute-done.17 = f32[8,128]{1,0:T(8,128)S(1)} collective-permute-done((f32[8,128]{1,0:T(8,128)}, f32[8,128]{1,0:T(8,128)S(1)}, u32[]{:S(2)}, u32[]{:S(2)}) %collective-permute-start.17) | collective-permute-done | bytes 4128 | tf_op jit(solution)/shard_map/ppermute | solution.py:711
  74.7 1.2 collective-permute-done.18
  76.5 6.4 %gated.1 = (f32[512,1024]{1,0:T(8,128)}, bf16[128,1024]{1,0:T(8,128)(2,1)}, bf16[128,1024]{1,0:T(8,128)(2,1)}, bf16[128,1024]{1,0:T(8,128)(2,1)}, bf16[128,1024]{1,0:T(8,128)(2,1)}) custom-call(s32[3]{0:T(128)} %pad_add_fusion.rank_ref, f32[8,128]{1,0:T(8,128)} %add.78.sums_ref, f32[1,512]{1,0:T(1,128)} %get-tuple-element.56.gate_gain_ref.gain_ref, ...), custom_call_target="tpu_custom_call" | custom-call | bytes 21000000 | tf_op jit(solution)/shard_map/gated/pallas_call | solution.py:929
  82.9 1.3 slice.182
  84.3 1.4 collective-permute-start.22
  85.7 1.5 collective-permute-start.23
  87.9 22.9 %backward.1 = (f32[512,1024]{1,0:T(8,128)}, f32[8,896]{1,0:T(8,128)}, bf16[64,2816]{1,0:T(8,128)(2,1)}, bf16[64,2816]{1,0:T(8,128)(2,1)}, bf16[128,2816]{1,0:T(8...) custom-call(s32[3]{0:T(128)} %pad_add_fusion.rank_ref, ...), custom_call_target="tpu_custom_call" | custom-call | bytes 84000000 | tf_op jit(solution)/shard_map/backward/pallas_call | solution.py:946
  110.8 1.6 collective-permute-start.25
  112.6 3.5 %collective-permute-start.28 = (bf16[64,1024]{1,0:T(8,128)(2,1)S(1)}, bf16[64,1024]{1,0:T(8,128)(2,1)S(1)}, u32[]{:S(2)}, u32[]{:S(2)}) collective-permute-start(bf16[64,1024]{1,0:T(8,128)(2,1)S(1)} %slice.183), channel_id=1, source_target_pairs={{0,8},{1,9},{2,10},{3,11},{4,12},{5,13},{6,14},{7,15},{8,0},{9,1},... | collective-permute-start | bytes 393224 | tf_op jit(solution)/shard_map/ppermute | solution.py:711
  116.1 6.3 %collective-permute-done.25 = bf16[128,2816]{1,0:T(8,128)(2,1)S(1)} collective-permute-done((bf16[128,2816]{1,0:T(8,128)(2,1)}, bf16[128,2816]{1,0:T(8,128)(2,1)S(1)}, u32[]{:S(2)}, u32[]{:S(2)}) %collective-permute-start.25) | collective-permute-done | bytes 720928 | tf_op jit(solution)/shard_map/ppermute | solution.py:711
  122.5 1.4 collective-permute-start.26
  124.0 2.0 %collective-permute-start.21 = (bf16[256,1024]{1,0:T(8,128)(2,1)S(1)}, bf16[256,1024]{1,0:T(8,128)(2,1)S(1)}, u32[]{:S(2)}, u32[]{:S(2)}) collective-permute-start(bf16[256,1024]{1,0:T(8,128)(2,1)S(1)} %slice.181), channel_id=1, source_target_pairs={{0,4},{1,5},{2,6},{3,7},{4,0},{5,1},{6,2},{7,3},{8,12},{9,13},{10,... | collective-permute-start | bytes 1572872 | tf_op jit(solution)/shard_map/ppermute | solution.py:711
  126.1 3.9 %collective-permute-done.26 = bf16[64,2816]{1,0:T(8,128)(2,1)S(1)} collective-permute-done((bf16[64,2816]{1,0:T(8,128)(2,1)S(1)}, bf16[64,2816]{1,0:T(8,128)(2,1)S(1)}, u32[]{:S(2)}, u32[]{:S(2)}) %collective-permute-start.26) | collective-permute-done | bytes 360480 | tf_op jit(solution)/shard_map/ppermute | solution.py:711
  130.0 1.3 collective-permute-start.32
  131.4 1.6 collective-permute-start.29
  133.0 3.3 %collective-permute-done.21 = bf16[256,1024]{1,0:T(8,128)(2,1)S(1)} collective-permute-done((bf16[256,1024]{1,0:T(8,128)(2,1)S(1)}, bf16[256,1024]{1,0:T(8,128)(2,1)S(1)}, u32[]{:S(2)}, u32[]{:S(2)}) %collective-permute-start.21) | collective-permute-done | bytes 524320 | tf_op jit(solution)/shard_map/ppermute | solution.py:711
  137.0 1.0 slice_add_fusion
  137.9 5.5 %collective-permute-done.33 = f32[8,896]{1,0:T(8,128)S(1)} collective-permute-done((f32[8,896]{1,0:T(8,128)S(1)}, f32[8,896]{1,0:T(8,128)S(1)}, u32[]{:S(2)}, u32[]{:S(2)}) %collective-permute-start.33) | collective-permute-done | bytes 28704 | tf_op jit(solution)/shard_map/ppermute | solution.py:711
  143.4 3.4 %collective-permute-start.34 = (f32[8,896]{1,0:T(8,128)S(1)}, f32[8,896]{1,0:T(8,128)S(1)}, u32[]{:S(2)}, u32[]{:S(2)}) collective-permute-start(f32[8,896]{1,0:T(8,128)S(1)} %add.98), channel_id=1, source_target_pairs={{0,8},{1,9},{2,10},{3,11},{4,12},{5,13},{6,14},{7,15},{8,0},{9,1},... | collective-permute-start | bytes 86024 | tf_op jit(solution)/shard_map/ppermute | solution.py:711
  147.1 2.7 %collective-permute-done.34 = f32[8,896]{1,0:T(8,128)S(1)} collective-permute-done((f32[8,896]{1,0:T(8,128)S(1)}, f32[8,896]{1,0:T(8,128)S(1)}, u32[]{:S(2)}, u32[]{:S(2)}) %collective-permute-start.34) | collective-permute-done | bytes 28704 | tf_op jit(solution)/shard_map/ppermute | solution.py:711
  150.2 1.2 collective-permute-start.30
  152.3 1.4 collective-permute-done.35
  153.8 7.2 %collective-permute-done.31 = bf16[64,2816]{1,0:T(8,128)(2,1)S(1)} collective-permute-done((bf16[64,2816]{1,0:T(8,128)(2,1)S(1)}, bf16[64,2816]{1,0:T(8,128)(2,1)S(1)}, u32[]{:S(2)}, u32[]{:S(2)}) %collective-permute-start.31) | collective-permute-done | bytes 360480 | tf_op jit(solution)/shard_map/ppermute | solution.py:711
  161.9 2.4 %tail.1 = f32[128,1024]{1,0:T(8,128)} custom-call(bf16[128,1024]{1,0:T(8,128)(2,1)} %tok_ref.1, bf16[128,1024]{1,0:T(8,128)(2,1)} %cot_ref.1, f32[1,1024]{1,0:T(1,128)} %get-tuple-element.55.gain_ref, f32[128,1024]{1,0:T(8,128)} %get-tuple-element.100.mine_ref, f32[128,1024]{1,0:T(8,128)} %copy-done.24), custom_call_target="tpu_custom_call" | custom-call | bytes 7000000 | tf_op jit(solution)/shard_map/tail/pallas_call | solution.py:981
  164.6 5.4 %collective-permute-done.37 = bf16[64,1408]{1,0:T(8,128)(2,1)S(1)} collective-permute-done((bf16[64,1408]{1,0:T(8,128)(2,1)S(1)}, bf16[64,1408]{1,0:T(8,128)(2,1)S(1)}, u32[]{:S(2)}, u32[]{:S(2)}) %collective-permute-start.37) | collective-permute-done | bytes 180256 | tf_op jit(solution)/shard_map/ppermute | solution.py:711
  170.2 2.6 %collective-permute-done.38.other_ref = f32[64,3840]{1,0:T(8,128)S(1)} collective-permute-done((f32[64,3840]{1,0:T(8,128)S(1)}, f32[64,3840]{1,0:T(8,128)S(1)}, u32[]{:S(2)}, u32[]{:S(2)}) %collective-permute-start.38) | collective-permute-done | bytes 983072 | tf_op jit(solution)/shard_map/ppermute | solution.py:714
  173.7 3.2 %unpack.1 = (f32[64,4384]{1,0:T(8,128)}, f32[128,1024]{1,0:T(8,128)}, f32[4,2304]{1,0:T(4,128)}, f32[18,128]{1,0:T(8,128)}, f32[16,128]{1,0:T(8,128)}, /*index=5...) custom-call(s32[3]{0:T(128)} %pad_add_fusion.rank_ref, f32[64,3840]{1,0:T(8,128)} %copy-done.11, ...), custom_call_target="tpu_custom_call" | custom-call | tf_op jit(solution)/shard_map/unpack/pallas_call | solution.py:996
  (137 shorter events, 13.0 us)
Async XLA Ops:
  3.5 9.2 %collective-permute-start = (bf16[64,1408]{1,0:T(8,128)(2,1)}, bf16[64,1408]{1,0:T(8,128)(2,1)S(1)}, u32[]{:S(2)}, u32[]{:S(2)}) collective-permute-start(bf16[64,1408]{1,0:T(8,128)(2,1)} %get-tuple-element.64), channel_id=1, source_target_pairs={{0,4},{1,5},{2,6},{3,7},{4,0},{5,1},{6,2},{7,3},{8,12},{9,13},{10,... | collective-permute-start | bytes 540680 | tf_op jit(solution)/shard_map/ppermute | solution.py:711
  6.5 11.5 %collective-permute-start.2 = (bf16[64,2432]{1,0:T(8,128)(2,1)}, bf16[64,2432]{1,0:T(8,128)(2,1)S(1)}, u32[]{:S(2)}, u32[]{:S(2)}) collective-permute-start(bf16[64,2432]{1,0:T(8,128)(2,1)} %get-tuple-element.63.rest_3_.rest_19_), channel_id=1, source_target_pairs={{0,1},{1,0},{2,3},{3,2},{4,5},{5,4},{6,7},{7,6},{8,9},{9,8},{10,11... | collective-permute-start | bytes 933896 | tf_op jit(solution)/shard_map/ppermute | solution.py:711
  8.0 16.5 %collective-permute-start.6 = (bf16[64,2432]{1,0:T(8,128)(2,1)}, bf16[64,2432]{1,0:T(8,128)(2,1)S(1)}, u32[]{:S(2)}, u32[]{:S(2)}) collective-permute-start(bf16[64,2432]{1,0:T(8,128)(2,1)} %get-tuple-element.63.rest_3_.rest_19_), channel_id=1, source_target_pairs={{0,8},{1,9},{2,10},{3,11},{4,12},{5,13},{6,14},{7,15},{8,0},{9,1},... | collective-permute-start | bytes 933896 | tf_op jit(solution)/shard_map/ppermute | solution.py:711
  12.3 23.8 %copy-start = (bf16[272,1024]{1,0:T(8,128)(2,1)}, bf16[272,1024]{1,0:T(8,128)(2,1)S(1)}, u32[]{:S(2)}) copy-start(bf16[272,1024]{1,0:T(8,128)(2,1)S(1)} %fusion.1.rest_0_) | copy-start | bytes 1671172
  12.3 24.6 %copy-start.3 = (bf16[64,2432]{1,0:T(8,128)(2,1)S(1)}, bf16[64,2432]{1,0:T(8,128)(2,1)}, u32[]{:S(2)}) copy-start(bf16[64,2432]{1,0:T(8,128)(2,1)} %get-tuple-element.63.rest_3_.rest_19_) | copy-start | bytes 933892
  12.7 23.4 %copy-start.16 = (bf16[64,1408]{1,0:T(8,128)(2,1)}, bf16[64,1408]{1,0:T(8,128)(2,1)S(1)}, u32[]{:S(2)}) copy-start(bf16[64,1408]{1,0:T(8,128)(2,1)S(1)} %collective-permute-done.rest_7_) | copy-start | bytes 540676
  12.7 23.3 %collective-permute-start.1 = (bf16[272,1024]{1,0:T(8,128)(2,1)S(1)}, bf16[272,1024]{1,0:T(8,128)(2,1)S(1)}, u32[]{:S(2)}, u32[]{:S(2)}) collective-permute-start(bf16[272,1024]{1,0:T(8,128)(2,1)S(1)} %fusion.1.rest_0_), channel_id=1, source_target_pairs={{0,4},{1,5},{2,6},{3,7},{4,0},{5,1},{6,2},{7,3},{8,12},{9,13},{10,... | collective-permute-start | bytes 1671176 | tf_op jit(solution)/shard_map/ppermute | solution.py:711
  13.2 12.8 %collective-permute-start.4 = (bf16[64,1408]{1,0:T(8,128)(2,1)S(1)}, bf16[64,1408]{1,0:T(8,128)(2,1)S(1)}, u32[]{:S(2)}, u32[]{:S(2)}) collective-permute-start(bf16[64,1408]{1,0:T(8,128)(2,1)S(1)} %collective-permute-done.rest_7_), channel_id=1, source_target_pairs={{0,1},{1,0},{2,3},{3,2},{4,5},{5,4},{6,7},{7,6},{8,9},{9,8},{10,11... | collective-permute-start | bytes 540680 | tf_op jit(solution)/shard_map/ppermute | solution.py:711
  14.7 11.8 %collective-permute-start.5 = (bf16[64,1408]{1,0:T(8,128)(2,1)S(1)}, bf16[64,1408]{1,0:T(8,128)(2,1)S(1)}, u32[]{:S(2)}, u32[]{:S(2)}) collective-permute-start(bf16[64,1408]{1,0:T(8,128)(2,1)S(1)} %collective-permute-done.rest_7_), channel_id=1, source_target_pairs={{0,2},{1,3},{2,0},{3,1},{4,6},{5,7},{6,4},{7,5},{8,10},{9,11},{10,... | collective-permute-start | bytes 540680 | tf_op jit(solution)/shard_map/ppermute | solution.py:711
  17.9 18.0 %collective-permute-start.3 = (bf16[64,2432]{1,0:T(8,128)(2,1)S(1)}, bf16[64,2432]{1,0:T(8,128)(2,1)S(1)}, u32[]{:S(2)}, u32[]{:S(2)}) collective-permute-start(bf16[64,2432]{1,0:T(8,128)(2,1)S(1)} %collective-permute-done.2.rest_4_.rest_20_), channel_id=1, source_target_pairs={{0,2},{1,3},{2,0},{3,1},{4,6},{5,7},{6,4},{7,5},{8,10},{9,11},{10,... | collective-permute-start | bytes 933896 | tf_op jit(solution)/shard_map/ppermute | solution.py:711
  24.5 11.5 %collective-permute-start.7 = (bf16[64,2432]{1,0:T(8,128)(2,1)S(1)}, bf16[64,2432]{1,0:T(8,128)(2,1)S(1)}, u32[]{:S(2)}, u32[]{:S(2)}) collective-permute-start(bf16[64,2432]{1,0:T(8,128)(2,1)S(1)} %collective-permute-done.6.rest_11_.rest_23_.rest_7_), channel_id=1, source_target_pairs={{0,1},{1,0},{2,3},{3,2},{4,5},{5,4},{6,7},{7,6},{8,9},{9,8},{10,11... | collective-permute-start | bytes 933896 | tf_op jit(solution)/shard_map/ppermute | solution.py:711
  26.0 28.9 %copy-start.17 = (bf16[64,1408]{1,0:T(8,128)(2,1)}, bf16[64,1408]{1,0:T(8,128)(2,1)S(1)}, u32[]{:S(2)}) copy-start(bf16[64,1408]{1,0:T(8,128)(2,1)S(1)} %collective-permute-done.4.rest_8_) | copy-start | bytes 540676
  26.0 10.0 %collective-permute-start.8 = (bf16[64,2432]{1,0:T(8,128)(2,1)S(1)}, bf16[64,2432]{1,0:T(8,128)(2,1)S(1)}, u32[]{:S(2)}, u32[]{:S(2)}) collective-permute-start(bf16[64,2432]{1,0:T(8,128)(2,1)S(1)} %collective-permute-done.6.rest_11_.rest_23_.rest_7_), channel_id=1, source_target_pairs={{0,2},{1,3},{2,0},{3,1},{4,6},{5,7},{6,4},{7,5},{8,10},{9,11},{10,... | collective-permute-start | bytes 933896 | tf_op jit(solution)/shard_map/ppermute | solution.py:711
  26.5 28.4 %copy-start.18 = (bf16[64,1408]{1,0:T(8,128)(2,1)}, bf16[64,1408]{1,0:T(8,128)(2,1)S(1)}, u32[]{:S(2)}) copy-start(bf16[64,1408]{1,0:T(8,128)(2,1)S(1)} %collective-permute-done.5.rest_9_) | copy-start | bytes 540676
  26.5 9.4 %collective-permute-start.9 = (bf16[64,1408]{1,0:T(8,128)(2,1)}, bf16[64,1408]{1,0:T(8,128)(2,1)S(1)}, u32[]{:S(2)}, u32[]{:S(2)}) collective-permute-start(bf16[64,1408]{1,0:T(8,128)(2,1)} %get-tuple-element.64), channel_id=1, source_target_pairs={{0,12},{1,13},{2,14},{3,15},{4,8},{5,9},{6,10},{7,11},{8,4},{9,5},... | collective-permute-start | bytes 540680 | tf_op jit(solution)/shard_map/ppermute | solution.py:711
  35.9 18.9 %copy-start.19 = (bf16[64,1408]{1,0:T(8,128)(2,1)}, bf16[64,1408]{1,0:T(8,128)(2,1)S(1)}, u32[]{:S(2)}) copy-start(bf16[64,1408]{1,0:T(8,128)(2,1)S(1)} %collective-permute-done.9.rest_15_) | copy-start | bytes 540676
  36.0 18.9 %copy-start.7 = (bf16[64,2432]{1,0:T(8,128)(2,1)}, bf16[64,2432]{1,0:T(8,128)(2,1)S(1)}, u32[]{:S(2)}) copy-start(bf16[64,2432]{1,0:T(8,128)(2,1)S(1)} %collective-permute-done.7.rest_12_.rest_24_.rest_8_) | copy-start | bytes 933892
  36.0 18.9 %copy-start.8 = (bf16[64,2432]{1,0:T(8,128)(2,1)}, bf16[64,2432]{1,0:T(8,128)(2,1)S(1)}, u32[]{:S(2)}) copy-start(bf16[64,2432]{1,0:T(8,128)(2,1)S(1)} %collective-permute-done.8.rest_13_.rest_25_.rest_9_) | copy-start | bytes 933892
  36.9 18.0 %collective-permute-start.10 = (bf16[544,1024]{1,0:T(8,128)(2,1)S(1)}, bf16[544,1024]{1,0:T(8,128)(2,1)S(1)}, u32[]{:S(2)}, u32[]{:S(2)}) collective-permute-start(bf16[544,1024]{1,0:T(8,128)(2,1)S(1)} %pad_maximum_fusion), channel_id=1, source_target_pairs={{0,16},{16,0},{1,17},{17,1},{2,18},{18,2},{3,19},{19,3},{4,20},{20... | collective-permute-start | bytes 3342344 | tf_op jit(solution)/shard_map/ppermute | solution.py:714
  36.9 8.8 %collective-permute-start.11 = (bf16[64,2432]{1,0:T(8,128)(2,1)S(1)}, bf16[64,2432]{1,0:T(8,128)(2,1)S(1)}, u32[]{:S(2)}, u32[]{:S(2)}) collective-permute-start(bf16[64,2432]{1,0:T(8,128)(2,1)S(1)} %copy-done.3), channel_id=1, source_target_pairs={{0,2},{1,3},{2,0},{3,1},{4,6},{5,7},{6,4},{7,5},{8,10},{9,11},{10,... | collective-permute-start | bytes 933896 | tf_op jit(solution)/shard_map/ppermute | solution.py:711
  38.4 8.8 %collective-permute-start.14 = (bf16[64,1408]{1,0:T(8,128)(2,1)S(1)}, bf16[64,1408]{1,0:T(8,128)(2,1)S(1)}, u32[]{:S(2)}, u32[]{:S(2)}) collective-permute-start(bf16[64,1408]{1,0:T(8,128)(2,1)S(1)} %collective-permute-done.9.rest_15_), channel_id=1, source_target_pairs={{0,1},{1,0},{2,3},{3,2},{4,5},{5,4},{6,7},{7,6},{8,9},{9,8},{10,11... | collective-permute-start | bytes 540680 | tf_op jit(solution)/shard_map/ppermute | solution.py:711
  39.9 15.0 %collective-permute-start.13 = (bf16[64,2432]{1,0:T(8,128)(2,1)S(1)}, bf16[64,2432]{1,0:T(8,128)(2,1)S(1)}, u32[]{:S(2)}, u32[]{:S(2)}) collective-permute-start(bf16[64,2432]{1,0:T(8,128)(2,1)S(1)} %collective-permute-done.7.rest_12_.rest_24_.rest_8_), channel_id=1, source_target_pairs={{0,2},{1,3},{2,0},{3,1},{4,6},{5,7},{6,4},{7,5},{8,10},{9,11},{10,... | collective-permute-start | bytes 933896 | tf_op jit(solution)/shard_map/ppermute | solution.py:711
  40.4 10.6 %collective-permute-start.12 = (bf16[64,1408]{1,0:T(8,128)(2,1)S(1)}, bf16[64,1408]{1,0:T(8,128)(2,1)S(1)}, u32[]{:S(2)}, u32[]{:S(2)}) collective-permute-start(bf16[64,1408]{1,0:T(8,128)(2,1)S(1)} %collective-permute-done.4.rest_8_), channel_id=1, source_target_pairs={{0,2},{1,3},{2,0},{3,1},{4,6},{5,7},{6,4},{7,5},{8,10},{9,11},{10,... | collective-permute-start | bytes 540680 | tf_op jit(solution)/shard_map/ppermute | solution.py:711
  45.7 7.2 %collective-permute-start.15 = (bf16[64,1408]{1,0:T(8,128)(2,1)S(1)}, bf16[64,1408]{1,0:T(8,128)(2,1)S(1)}, u32[]{:S(2)}, u32[]{:S(2)}) collective-permute-start(bf16[64,1408]{1,0:T(8,128)(2,1)S(1)} %collective-permute-done.9.rest_15_), channel_id=1, source_target_pairs={{0,2},{1,3},{2,0},{3,1},{4,6},{5,7},{6,4},{7,5},{8,10},{9,11},{10,... | collective-permute-start | bytes 540680 | tf_op jit(solution)/shard_map/ppermute | solution.py:711
  47.2 7.6 %collective-permute-start.16 = (bf16[64,1408]{1,0:T(8,128)(2,1)S(1)}, bf16[64,1408]{1,0:T(8,128)(2,1)S(1)}, u32[]{:S(2)}, u32[]{:S(2)}) collective-permute-start(bf16[64,1408]{1,0:T(8,128)(2,1)S(1)} %collective-permute-done.14.rest_16_), channel_id=1, source_target_pairs={{0,2},{1,3},{2,0},{3,1},{4,6},{5,7},{6,4},{7,5},{8,10},{9,11},{10,... | collective-permute-start | bytes 540680 | tf_op jit(solution)/shard_map/ppermute | solution.py:711
  70.1 3.9 %collective-permute-start.17 = (f32[8,128]{1,0:T(8,128)}, f32[8,128]{1,0:T(8,128)S(1)}, u32[]{:S(2)}, u32[]{:S(2)}) collective-permute-start(f32[8,128]{1,0:T(8,128)} %get-tuple-element.66), channel_id=1, source_target_pairs={{0,4},{1,5},{2,6},{3,7},{4,0},{5,1},{6,2},{7,3},{8,12},{9,13},{10,... | collective-permute-start | bytes 12296 | tf_op jit(solution)/shard_map/ppermute | solution.py:711
  74.7 1.2 collective-permute-start.18
  84.2 26.6 %collective-permute-start.19 = (bf16[256,1024]{1,0:T(8,128)(2,1)S(1)}, bf16[256,1024]{1,0:T(8,128)(2,1)S(1)}, u32[]{:S(2)}, u32[]{:S(2)}) collective-permute-start(bf16[256,1024]{1,0:T(8,128)(2,1)S(1)} %slice.182), channel_id=1, source_target_pairs={{0,4},{1,5},{2,6},{3,7},{4,0},{5,1},{6,2},{7,3},{8,12},{9,13},{10,... | collective-permute-start | bytes 1572872 | tf_op jit(solution)/shard_map/ppermute | solution.py:711
  84.3 26.5 %collective-permute-start.22 = (bf16[128,1024]{1,0:T(8,128)(2,1)}, bf16[128,1024]{1,0:T(8,128)(2,1)S(1)}, u32[]{:S(2)}, u32[]{:S(2)}) collective-permute-start(bf16[128,1024]{1,0:T(8,128)(2,1)} %get-tuple-element.77), channel_id=1, source_target_pairs={{0,1},{1,0},{2,3},{3,2},{4,5},{5,4},{6,7},{7,6},{8,9},{9,8},{10,11... | collective-permute-start | bytes 786440 | tf_op jit(solution)/shard_map/ppermute | solution.py:711
  85.7 25.1 %collective-permute-start.23 = (bf16[128,1024]{1,0:T(8,128)(2,1)}, bf16[128,1024]{1,0:T(8,128)(2,1)S(1)}, u32[]{:S(2)}, u32[]{:S(2)}) collective-permute-start(bf16[128,1024]{1,0:T(8,128)(2,1)} %get-tuple-element.70), channel_id=1, source_target_pairs={{0,2},{1,3},{2,0},{3,1},{4,6},{5,7},{6,4},{7,5},{8,10},{9,11},{10,... | collective-permute-start | bytes 786440 | tf_op jit(solution)/shard_map/ppermute | solution.py:711
  87.2 23.6 %collective-permute-start.24 = (bf16[128,1024]{1,0:T(8,128)(2,1)}, bf16[128,1024]{1,0:T(8,128)(2,1)S(1)}, u32[]{:S(2)}, u32[]{:S(2)}) collective-permute-start(bf16[128,1024]{1,0:T(8,128)(2,1)} %get-tuple-element.78), channel_id=1, source_target_pairs={{0,3},{1,2},{2,1},{3,0},{4,7},{5,6},{6,5},{7,4},{8,11},{9,10},{10,... | collective-permute-start | bytes 786440 | tf_op jit(solution)/shard_map/ppermute | solution.py:711
  87.9 24.6 %copy-start.29 = (bf16[128,1024]{1,0:T(8,128)(2,1)S(1)}, bf16[128,1024]{1,0:T(8,128)(2,1)}, u32[]{:S(2)}) copy-start(bf16[128,1024]{1,0:T(8,128)(2,1)} %get-tuple-element.83) | copy-start | bytes 786436
  110.8 11.6 %collective-permute-start.25 = (bf16[128,2816]{1,0:T(8,128)(2,1)}, bf16[128,2816]{1,0:T(8,128)(2,1)S(1)}, u32[]{:S(2)}, u32[]{:S(2)}) collective-permute-start(bf16[128,2816]{1,0:T(8,128)(2,1)} %get-tuple-element.79), channel_id=1, source_target_pairs={{0,2},{1,3},{2,0},{3,1},{4,6},{5,7},{6,4},{7,5},{8,10},{9,11},{10,... | collective-permute-start | bytes 2162696 | tf_op jit(solution)/shard_map/ppermute | solution.py:711
  112.6 13.3 %collective-permute-start.28 = (bf16[64,1024]{1,0:T(8,128)(2,1)S(1)}, bf16[64,1024]{1,0:T(8,128)(2,1)S(1)}, u32[]{:S(2)}, u32[]{:S(2)}) collective-permute-start(bf16[64,1024]{1,0:T(8,128)(2,1)S(1)} %slice.183), channel_id=1, source_target_pairs={{0,8},{1,9},{2,10},{3,11},{4,12},{5,13},{6,14},{7,15},{8,0},{9,1},... | collective-permute-start | bytes 393224 | tf_op jit(solution)/shard_map/ppermute | solution.py:711
  122.5 7.5 %collective-permute-start.26 = (bf16[64,2816]{1,0:T(8,128)(2,1)S(1)}, bf16[64,2816]{1,0:T(8,128)(2,1)S(1)}, u32[]{:S(2)}, u32[]{:S(2)}) collective-permute-start(bf16[64,2816]{1,0:T(8,128)(2,1)S(1)} %add_convert_fusion.2), channel_id=1, source_target_pairs={{0,1},{1,0},{2,3},{3,2},{4,5},{5,4},{6,7},{7,6},{8,9},{9,8},{10,11... | collective-permute-start | bytes 1081352 | tf_op jit(solution)/shard_map/ppermute | solution.py:711
  124.0 12.3 %collective-permute-start.21 = (bf16[256,1024]{1,0:T(8,128)(2,1)S(1)}, bf16[256,1024]{1,0:T(8,128)(2,1)S(1)}, u32[]{:S(2)}, u32[]{:S(2)}) collective-permute-start(bf16[256,1024]{1,0:T(8,128)(2,1)S(1)} %slice.181), channel_id=1, source_target_pairs={{0,4},{1,5},{2,6},{3,7},{4,0},{5,1},{6,2},{7,3},{8,12},{9,13},{10,... | collective-permute-start | bytes 1572872 | tf_op jit(solution)/shard_map/ppermute | solution.py:711
  130.0 6.4 %collective-permute-start.32 = (f32[8,896]{1,0:T(8,128)S(1)}, f32[8,896]{1,0:T(8,128)S(1)}, u32[]{:S(2)}, u32[]{:S(2)}) collective-permute-start(f32[8,896]{1,0:T(8,128)S(1)} %copy-done.32), channel_id=1, source_target_pairs={{0,1},{1,0},{2,3},{3,2},{4,5},{5,4},{6,7},{7,6},{8,9},{9,8},{10,11... | collective-permute-start | bytes 86024 | tf_op jit(solution)/shard_map/ppermute | solution.py:711
  131.3 20.1 %collective-permute-start.20 = (f32[128,1024]{1,0:T(8,128)S(1)}, f32[128,1024]{1,0:T(8,128)S(1)}, u32[]{:S(2)}, u32[]{:S(2)}) collective-permute-start(f32[128,1024]{1,0:T(8,128)S(1)} %slice_add_fusion.2), channel_id=1, source_target_pairs={{0,16},{16,0},{1,17},{17,1},{2,18},{18,2},{3,19},{19,3},{4,20},{20... | collective-permute-start | bytes 1572872 | tf_op jit(solution)/shard_map/ppermute | solution.py:714
  131.4 18.7 %collective-permute-start.29 = (bf16[128,2816]{1,0:T(8,128)(2,1)S(1)}, bf16[128,2816]{1,0:T(8,128)(2,1)S(1)}, u32[]{:S(2)}, u32[]{:S(2)}) collective-permute-start(bf16[128,2816]{1,0:T(8,128)(2,1)S(1)} %copy-done.33), channel_id=1, source_target_pairs={{0,2},{1,3},{2,0},{3,1},{4,6},{5,7},{6,4},{7,5},{8,10},{9,11},{10,... | collective-permute-start | bytes 2162696 | tf_op jit(solution)/shard_map/ppermute | solution.py:711
  136.4 7.0 %collective-permute-start.33 = (f32[8,896]{1,0:T(8,128)S(1)}, f32[8,896]{1,0:T(8,128)S(1)}, u32[]{:S(2)}, u32[]{:S(2)}) collective-permute-start(f32[8,896]{1,0:T(8,128)S(1)} %add.97), channel_id=1, source_target_pairs={{0,2},{1,3},{2,0},{3,1},{4,6},{5,7},{6,4},{7,5},{8,10},{9,11},{10,... | collective-permute-start | bytes 86024 | tf_op jit(solution)/shard_map/ppermute | solution.py:711
  137.9 23.1 %collective-permute-start.27 = (f32[128,1024]{1,0:T(8,128)S(1)}, f32[128,1024]{1,0:T(8,128)S(1)}, u32[]{:S(2)}, u32[]{:S(2)}) collective-permute-start(f32[128,1024]{1,0:T(8,128)S(1)} %get-tuple-element.99), channel_id=1, source_target_pairs={{0,16},{16,0},{1,17},{17,1},{2,18},{18,2},{3,19},{19,3},{4,20},{20... | collective-permute-start | bytes 1572872 | tf_op jit(solution)/shard_map/ppermute | solution.py:714
  143.4 6.4 %collective-permute-start.34 = (f32[8,896]{1,0:T(8,128)S(1)}, f32[8,896]{1,0:T(8,128)S(1)}, u32[]{:S(2)}, u32[]{:S(2)}) collective-permute-start(f32[8,896]{1,0:T(8,128)S(1)} %add.98), channel_id=1, source_target_pairs={{0,8},{1,9},{2,10},{3,11},{4,12},{5,13},{6,14},{7,15},{8,0},{9,1},... | collective-permute-start | bytes 86024 | tf_op jit(solution)/shard_map/ppermute | solution.py:711
  147.0 14.0 %collective-permute-start.31 = (bf16[64,2816]{1,0:T(8,128)(2,1)S(1)}, bf16[64,2816]{1,0:T(8,128)(2,1)S(1)}, u32[]{:S(2)}, u32[]{:S(2)}) collective-permute-start(bf16[64,2816]{1,0:T(8,128)(2,1)S(1)} %add_convert_fusion), channel_id=1, source_target_pairs={{0,8},{1,9},{2,10},{3,11},{4,12},{5,13},{6,14},{7,15},{8,0},{9,1},... | collective-permute-start | bytes 1081352 | tf_op jit(solution)/shard_map/ppermute | solution.py:711
  149.8 3.9 %collective-permute-start.35 = (f32[8,896]{1,0:T(8,128)S(1)}, f32[8,896]{1,0:T(8,128)S(1)}, u32[]{:S(2)}, u32[]{:S(2)}) collective-permute-start(f32[8,896]{1,0:T(8,128)S(1)} %add.99), channel_id=1, source_target_pairs={{0,4},{1,5},{2,6},{3,7},{4,0},{5,1},{6,2},{7,3},{8,12},{9,13},{10,... | collective-permute-start | bytes 86024 | tf_op jit(solution)/shard_map/ppermute | solution.py:711
  150.2 14.0 %collective-permute-start.30 = (bf16[64,2816]{1,0:T(8,128)(2,1)S(1)}, bf16[64,2816]{1,0:T(8,128)(2,1)S(1)}, u32[]{:S(2)}, u32[]{:S(2)}) collective-permute-start(bf16[64,2816]{1,0:T(8,128)(2,1)S(1)} %add_convert_fusion.1), channel_id=1, source_target_pairs={{0,1},{1,0},{2,3},{3,2},{4,5},{5,4},{6,7},{7,6},{8,9},{9,8},{10,11... | collective-permute-start | bytes 1081352 | tf_op jit(solution)/shard_map/ppermute | solution.py:711
  153.7 10.8 %collective-permute-start.36 = (f32[8,1792]{1,0:T(8,128)S(1)}, f32[8,1792]{1,0:T(8,128)S(1)}, u32[]{:S(2)}, u32[]{:S(2)}) collective-permute-start(f32[8,1792]{1,0:T(8,128)S(1)} %pad_maximum_fusion.2.small_mine_ref), channel_id=1, source_target_pairs={{0,16},{16,0},{1,17},{17,1},{2,18},{18,2},{3,19},{19,3},{4,20},{20... | collective-permute-start | bytes 172040 | tf_op jit(solution)/shard_map/ppermute | solution.py:714
  164.5 5.6 %collective-permute-start.37 = (bf16[64,1408]{1,0:T(8,128)(2,1)S(1)}, bf16[64,1408]{1,0:T(8,128)(2,1)S(1)}, u32[]{:S(2)}, u32[]{:S(2)}) collective-permute-start(bf16[64,1408]{1,0:T(8,128)(2,1)S(1)} %slice_add_fusion.4), channel_id=1, source_target_pairs={{0,4},{1,5},{2,6},{3,7},{4,0},{5,1},{6,2},{7,3},{8,12},{9,13},{10,... | collective-permute-start | bytes 540680 | tf_op jit(solution)/shard_map/ppermute | solution.py:711
  170.1 2.6 %collective-permute-start.38 = (f32[64,3840]{1,0:T(8,128)S(1)}, f32[64,3840]{1,0:T(8,128)S(1)}, u32[]{:S(2)}, u32[]{:S(2)}) collective-permute-start(f32[64,3840]{1,0:T(8,128)S(1)} %pad_maximum_fusion.1.mine_ref), channel_id=1, source_target_pairs={{0,16},{16,0},{1,17},{17,1},{2,18},{18,2},{3,19},{19,3},{4,20},{20... | collective-permute-start | bytes 2949128 | tf_op jit(solution)/shard_map/ppermute | solution.py:714
  (25 other events, 149.7 us)

commit v3 on v2

--- a/solution.py
+++ b/solution.py
@@ -447,11 +447,11 @@
     token_count = 1 + max(ref for ref, _ in places)
     token_rows, rest = rest[:token_count], rest[token_count:]
     chunks = rest[:chunk_count]
-    block_ref = rest[chunk_count]
-    grads = rest[chunk_count + 1 : chunk_count + 1 + grad_count]
+    close_ref, away_ref = rest[chunk_count : chunk_count + 2]
+    grads = rest[chunk_count + 2 : chunk_count + 2 + grad_count]
     (proj_ref, mixer_ref, gated_ref, factor_ref, w_out_ref, grad_ref, cot_ref, sems, grad_sems, load_sems,
      token_sems) = (
-        rest[chunk_count + 1 + grad_count :]
+        rest[chunk_count + 2 + grad_count :]
     )
     loads = [
         started(proj_in.at[:, pl.ds(0, inner)], proj_ref, load_sems.at[0]),
@@ -480,7 +480,10 @@
         copy.start()
     for copy in weights:
         copy.wait()
-    block_ref[...] = jnp.dot(gated_ref[...], w_out_ref[...], preferred_element_type=f32)
+    half = tokens // 2
+    close_ref[...] = jnp.dot(gated_ref[:half, :], w_out_ref[...], preferred_element_type=f32)
+    away = jnp.dot(gated_ref[half:, :], w_out_ref[...], preferred_element_type=f32)
+    away_ref[...] = away.astype(bf16)
     for copy in copies:
         copy.wait()
 
@@ -494,13 +497,13 @@
     token_rows, rest = rest[:token_count], rest[token_count:]
     weight_chunks = rest[:weight_count]
     rest = rest[weight_count:]
-    dnormed_ref, small_ref = rest[:2]
-    chunks = rest[2 : 2 + chunk_count]
+    close_ref, away_ref, small_ref, coded_ref = rest[:4]
+    chunks = rest[4 : 4 + chunk_count]
     (normed_ref, proj_ref, mixer_ref, dgated_ref, masks_ref, vis_ref, dact_ref,
      act_ref, stepe_ref, cume_ref, cumt_ref, score_ref, dscore_ref, dstep_ref,
      rowsum_ref, colsum_ref, turned_ref, dskip_ref, factor_ref, pull_ref, turned_normed_ref, grad_ref,
-     w_ref, dproj_ref, tok_ref, seg_ref, weight_sems, sems, load_sems, token_sems) = (
-        rest[2 + chunk_count :]
+     w_ref, dproj_ref, tok_ref, seg_ref, carried_ref, weight_sems, sems, load_sems, token_sems) = (
+        rest[4 + chunk_count :]
     )
     seg_in = token_copies(places, token_rows, seg_ref, 2 * LANES, 16, token_sems)
     loads = [
@@ -668,11 +671,21 @@
     for start in range(0, model, 256):
         lanes = slice(start, start + 256)
         dnormed = low_dot(dproj_ref[...], w_ref[lanes, :], ((1,), (1,)))
-        dnormed_ref[:, lanes] = dnormed
+        half = tokens // 2
+        close_ref[:, lanes] = dnormed[:half]
+        away_ref[:, lanes] = dnormed[half:].astype(bf16)
         dgain = jnp.sum(dnormed * hidden[:, lanes] * token_factor, axis=0, keepdims=True)
         for at in range(0, 256, part):
             row = (start + at) // part
             small_ref[row : row + 1, conv_width:] = dgain[:, at : at + part]
+    high = small_ref[...].astype(bf16)
+    low = small_ref[...] - high.astype(f32)
+    coded_ref[...] = jnp.concatenate([high.astype(f32), low], axis=0).astype(bf16)
+    if chunk_count > 1:
+        carried_ref[...] = jnp.zeros_like(carried_ref)
+        carried_ref[:, : coded_ref.shape[1]] = coded_ref[...]
+        held = chunks[2].at[pl.ds(chunks[2].shape[0] - 16, 16)]
+        copies.append(started(carried_ref, held, token_sems.at[2 * len(places)]))
     for copy in copies:
         copy.wait()
 
@@ -719,39 +732,49 @@
         return [block, near, side, self.exchange(near, self.second)]
 
     def gather(self, keep, give):
-        across = self.exchange(keep, self.slots[2])
-        own = self.spread(keep)
-        beside = self.exchange(give, self.slots[1])
+        beside, across = self.exchange(give, self.slots[1]), self.exchange(keep, self.slots[2])
+        own, near = self.spread(keep), self.spread(beside)
         far = self.exchange(after(give, beside), self.slots[3])
-        return [own, self.spread(beside), self.spread(across), self.spread(far)]
-
-    def square(self, own, near, send):
-        rows = own.shape[0]
+        return [own, near, self.spread(after(across, *own[2:], near[2])), self.spread(after(far, near[3]))]
+
+    def square_with(self, own, near, send, small, earlier):
+        rows, width = own.shape
+        count = small.shape[0] // 2
+
+        def decoded(x):
+            x = x[-2 * count :, : small.shape[1]].astype(f32)
+            return x[:count] + x[count:]
+
         came = self.exchange(send, self.second)
-        near = (near.astype(f32) + came[rows:].astype(f32)).astype(bf16)
-        last = self.exchange(near, self.first)
-        return own.astype(f32) + came[:rows].astype(f32) + last.astype(f32), came, last
+        near = (near.astype(f32) + came[rows : 2 * rows].astype(f32)).astype(bf16)
+        near = after(near, earlier)
+        total = decoded(small) + decoded(came)
+        high = lax.reduce_precision(total, 8, 7)
+        coded = jnp.concatenate([high, total - high]).astype(bf16)
+        ride = jnp.pad(coded, ((0, 0), (0, width - small.shape[1])))
+        last = self.exchange(jnp.concatenate([near, ride]), self.first)
+        total = decoded(coded) + decoded(last)
+        return own.astype(f32) + came[:rows].astype(f32) + last[:rows].astype(f32), total, came
 
     def square_at_once(self, own, near, side, far):
         moved = [self.exchange(near, self.first), self.exchange(side, self.second), self.exchange(far, 3)]
         return sum((x.astype(f32) for x in moved), own.astype(f32)), moved
 
     def across(self, x):
-        return self.exchange(x.astype(bf16), self.slots[2]).astype(f32)
+        return self.exchange(x.astype(bf16), self.slots[2])
 
     def beside(self, x):
         return self.exchange(x.astype(bf16), self.slots[1]).astype(f32)
 
-    def scatter(self, chunks, far, out, after_first, meanwhile):
-        width = chunks[0].shape[1] // 2
-        close, _, _ = self.square(*chunks[:2], after(chunks[2], after_first, out[1]))
-        other = self.beside(after(close[:, width:] + far[:, width:], *meanwhile))
-        return jnp.concatenate([close[:, :width] + far[:, :width], out[0] + out[1], other], axis=1)
-
-    def sum_chips(self, x):
-        for step in (1, 2, 8):
-            x = x + self.exchange(x, step)
-        return jnp.concatenate([x, self.exchange(x, 4)], axis=1)
+    def square_second(self, own, near, came, meanwhile):
+        rows = own.shape[0]
+        near = (near.astype(f32) + came[rows:].astype(f32)).astype(bf16)
+        near = self.exchange(after(near, *meanwhile), self.first)
+        return own.astype(f32) + came[:rows].astype(f32) + near.astype(f32)
+
+    def sum_lines(self, x):
+        same, beside, other = (self.exchange(x, slot) for slot in (8, 4, 12))
+        return jnp.concatenate([x + same, beside + other], axis=1)
 
     def group_rows(self, x, others):
         other = after(self.exchange(x, self.slots[1]), *others)
@@ -772,14 +795,15 @@
         return x + reordered(self.swap(x), 1)
 
     def from_side(self, x):
-        return self.exchange(x[x.shape[0] // 2 :].astype(bf16), self.slots[1])
+        return self.exchange(x, self.slots[1])
 
     def own_rows(self, x, came):
-        rows = x.shape[0] // 4
+        rows = x.shape[0] // 2
         came = came.astype(f32)
-        return x[:rows] + came[:rows], self.swap(x[rows : 2 * rows] + came[rows:])
-
-    def scattered(self, x):
+        return x[:rows] + came[:rows], self.swap(x[rows:] + came[rows:])
+
+    def scattered(self, close, away):
+        x = jnp.concatenate([close, away.astype(f32)])
         mine = lax.psum_scatter(x, "rep", scatter_dimension=0, tiled=True)
         return mine, jnp.zeros_like(mine)
 
@@ -857,6 +881,7 @@
           norm_gain.reshape(-1, LANES), dt_bias[None], a_log[None], skip_gain[None])
         in_chunks, out_chunks = sum(slots, []), slots[0] + slots[2]
         in_shapes = [(rows_in, 2 * width), (rows_in, 2 * width), (2 * rows_in, 2 * width)] * 2
+        in_shapes[2] = (2 * rows_in + 16, 2 * width)
         out_shapes = [(2 * rows_in, model)] * 4
     else:
         in_full = lax.all_gather(in_weight, "fsdp", axis=0, tiled=True)
@@ -926,11 +951,11 @@
         name="forward",
     )(rank, norm_g, gate_g, conv_w, conv_b, head_rows, skip, *token_rows, *in_chunks, *out_chunks)
     sums = links.sum_group(sums)
-    block_part, *out_grads = pl.pallas_call(
+    block_close, block_away, *out_grads = pl.pallas_call(
         functools.partial(gated_kernel, places, out_count, len(out_shapes), inner, full_inner),
-        out_shape=[arr(total, model)] + out_shapes,
+        out_shape=[arr(total // 2, model), arr(total // 2, model, dtype=bf16)] + out_shapes,
         in_specs=in_smem(1) + in_vmem(2) + in_hbm(2 + len(token_rows) + out_count),
-        out_specs=in_vmem(1) + in_hbm(len(out_shapes)),
+        out_specs=in_vmem(2) + in_hbm(len(out_shapes)),
         scratch_shapes=[
             vmem(total, inner), vmem(total, inner), vmem(total, inner, dtype=bf16), vmem(total, LANES), w_out,
             vmem(inner, model, dtype=bf16), tok, out_sems, out_sems, sems(2), sems(len(places)),
@@ -942,20 +967,23 @@
     if paired:
         out_sums, moved = links.square_at_once(*out_grads)
         sums = after(sums, out_grads[2])
-        block_came = links.from_side(block_part)
-    d_normed, small, *in_grads = pl.pallas_call(
+        block_came = links.from_side(block_away)
+    d_normed_close, d_normed_away, small, coded, *in_grads = pl.pallas_call(
         functools.partial(backward_kernel, places, in_count, len(in_shapes), inner, head_dim, full_inner),
-        out_shape=[arr(total, model), arr(8, conv_local + model // 8)] + in_shapes,
+        out_shape=[
+            arr(total // 2, model), arr(total // 2, model, dtype=bf16),
+            arr(8, conv_local + model // 8), arr(16, conv_local + model // 8, dtype=bf16),
+        ] + in_shapes,
         in_specs=in_smem(1) + in_vmem(6) + in_hbm(4 + len(token_rows) + in_count),
-        out_specs=in_vmem(2) + in_hbm(len(in_shapes)),
+        out_specs=in_vmem(4) + in_hbm(len(in_shapes)),
         scratch_shapes=kept + conv_masks + [
             vmem(total, conv_local),
             vmem(total, conv_local), vmem(total, inner), vmem(total, inner), vmem(inner // LANES, 8, total),
             vmem(total, LANES), vmem(total, LANES), vmem(total, LANES),
             vmem(total, LANES), vmem(inner // LANES, 8, total), vmem(LANES, total), vmem(8, inner),
             vmem(total, LANES), vmem(total, LANES), vmem(model, total, dtype=bf16), w_in, w_in,
-            vmem(total, width, dtype=bf16), tok, segs, in_sems, in_sems, sems(4),
-            sems(2 * len(places)),
+            vmem(total, width, dtype=bf16), tok, segs, vmem(16, 2 * width, dtype=bf16), in_sems, in_sems, sems(4),
+            sems(2 * len(places) + 1),
         ],
         compiler_params=params(),
         cost_estimate=cost(24),
@@ -964,20 +992,24 @@
       *in_chunks)
 
     if paired:
-        far, came, last = links.square(*in_grads[:2], after(in_grads[2], block_came, *moved))
-        far = links.across(far)
-        out_parts = out_sums[:rows_in], links.across(out_sums[rows_in:])
-        small = links.sum_chips(after(small, last))
+        out_across = links.across(out_sums[rows_in:])
+        far, small, came = links.square_with(
+            *in_grads[:2], after(in_grads[2], block_came, *moved), coded, out_across
+        )
+        came = links.exchange(after(in_grads[5], came), links.second)
+        far = links.across(far).astype(f32)
+        small = links.sum_lines(after(small, came))
         small_other = links.swap(small)
-        d_normed_parts = links.own_rows(d_normed, after(links.from_side(d_normed), last))
-        block_parts = links.own_rows(block_part, block_came)
+        d_normed_parts = links.own_rows(d_normed_close, after(links.from_side(d_normed_away), came))
+        block_parts = links.own_rows(block_close, block_came)
     else:
         out_sum, in_sum = (
             lax.psum_scatter(grads[0], "fsdp", scatter_dimension=0, tiled=True).astype(f32)
             for grads in (out_grads, in_grads)
         )
         smalls = links.from_reps(lax.psum(small, "fsdp"))
-        d_normed_parts, block_parts = links.scattered(d_normed), links.scattered(block_part)
+        d_normed_parts = links.scattered(d_normed_close, d_normed_away)
+        block_parts = links.scattered(block_close, block_away)
     d_tokens = pl.pallas_call(
         tail_kernel,
         out_shape=arr(own_tokens, model),
@@ -990,9 +1022,10 @@
     block_out = (tokens.astype(f32) + (block_parts[0] + block_parts[1])).astype(bf16)
 
     if paired:
-        grad_sum = links.scatter(
-            in_grads[3:], far, out_parts, came, [d_tokens, block_out, small_other]
-        )
+        close = links.square_second(*in_grads[3:5], came, [d_tokens, block_out])
+        other = links.beside(after(close[:, width:] + far[:, width:], small_other))
+        out_sum = out_sums[:rows_in] + out_across.astype(f32)
+        grad_sum = jnp.concatenate([close[:, :width] + far[:, :width], out_sum, other], axis=1)
         d_in_weight, d_out_weight, d_conv_weight, d_conv_bias, d_gate_gain, d_norm_gain, *by_head = pl.pallas_call(
             functools.partial(unpack_kernel, inner, state, heads, model, taps),
             out_shape=[

time: 178 us -> 167 us (0.938)
  waiting for transfers between devices: 66.1 us -> 57.6 us
  local copies, waits for them, and re-layouts: 5.05 us -> 2.98 us
    ppermute x33 -> x32, waiting for transfers between devices: 62.4 us -> 52 us  [exchange(): return lax.ppermute(x, BOTH, pairs)]
    ppermute x6, waiting for transfers between devices: 3.72 us -> 5.52 us  [swap(): return lax.ppermute(x, 'rep', [(0, 1), (1, 0)])]
    ppermute x33 -> x32, starting transfers between devices: 44.7 us -> 42.9 us  [exchange(): return lax.ppermute(x, BOTH, pairs)]
    unnamed x68 -> x66, local copies, waits for them, and re-layouts: 3.64 us -> 2.92 us
  transfers between devices with their start and end apart: 39 -> 38, of which waited for: 18 -> 18; matrix products, arithmetic and copies ran while one was open for 3% -> 3% of each run, Pallas kernels for 15% -> 17%
where the time goes in v3:
time: 167 us
  waiting for transfers between devices  57.6 us (34%)
  Pallas kernels  53.4 us (32%)
  starting transfers between devices  43.6 us (26%)
  other arithmetic  7.5 us (4%)
  local copies, waits for them, and re-layouts  2.98 us (2%)
    ppermute x32, waiting for transfers between devices, exchange(): return lax.ppermute(x, BOTH, pairs)  52 us
    ppermute x32, starting transfers between devices, exchange(): return lax.ppermute(x, BOTH, pairs)  42.9 us
    pallas_call x1, Pallas kernels, per_device(): pl.pallas_call(functools.partial(backward_kernel, places, in_count, len(i...  23.4 us
    pallas_call x1, Pallas kernels, per_device(): pl.pallas_call(functools.partial(forward_kernel, places, in_count, out_co...  14.2 us
    pallas_call x1, Pallas kernels, per_device(): pl.pallas_call(functools.partial(gated_kernel, places, out_count, len(out...  6.23 us
    ppermute x6, waiting for transfers between devices, swap(): return lax.ppermute(x, 'rep', [(0, 1), (1, 0)])  5.52 us
  transfers between devices with their start and end apart: 38, of which 18 were waited for; matrix products, arithmetic and copies ran while one was open for 3% of the time, Pallas kernels for 17%

profile of v3, /device:TPU:0, one launch (start us, length us, event | category | flops | bytes accessed | tf_op | source)
XLA Modules:
  0.0 166.5 jit_solution(9767494295204803984)
XLA Ops:
  1.3 2.2 %pack.1 = (bf16[64,2432]{1,0:T(8,128)(2,1)}, bf16[64,1408]{1,0:T(8,128)(2,1)}) custom-call(s32[3]{0:T(128)} %pad_add_fusion.rank_ref, bf16[64,4384]{1,0:T(8,128)(2,1)} %in_ref.1, bf16[128,1024]{1,0:T(8,128)(2,1)} %out_ref.1), custom_call_target="tpu_custom_call" | custom-call | tf_op jit(solution)/shard_map/pack/pallas_call | solution.py:860
  3.5 2.9 %collective-permute-start.2 = (bf16[64,2432]{1,0:T(8,128)(2,1)}, bf16[64,2432]{1,0:T(8,128)(2,1)S(1)}, u32[]{:S(2)}, u32[]{:S(2)}) collective-permute-start(bf16[64,2432]{1,0:T(8,128)(2,1)} %get-tuple-element.69.rest_3_.rest_19_), channel_id=1, source_target_pairs={{0,1},{1,0},{2,3},{3,2},{4,5},{5,4},{6,7},{7,6},{8,9},{9,8},{10,11... | collective-permute-start | bytes 933896 | tf_op jit(solution)/shard_map/ppermute | solution.py:724
  6.4 1.6 collective-permute-start
  8.0 2.6 %collective-permute-start.6 = (bf16[64,2432]{1,0:T(8,128)(2,1)}, bf16[64,2432]{1,0:T(8,128)(2,1)S(1)}, u32[]{:S(2)}, u32[]{:S(2)}) collective-permute-start(bf16[64,2432]{1,0:T(8,128)(2,1)} %get-tuple-element.69.rest_3_.rest_19_), channel_id=1, source_target_pairs={{0,8},{1,9},{2,10},{3,11},{4,12},{5,13},{6,14},{7,15},{8,0},{9,1},... | collective-permute-start | bytes 933896 | tf_op jit(solution)/shard_map/ppermute | solution.py:724
  10.6 1.5 collective-permute-start.7
  12.8 1.4 collective-permute-start.3
  14.1 1.1 fusion.2.rest_0_
  15.2 1.2 collective-permute-done.rest_7_
  16.4 1.6 collective-permute-start.1
  18.1 6.4 %collective-permute-done.6.rest_11_.rest_23_.rest_7_ = bf16[64,2432]{1,0:T(8,128)(2,1)S(1)} collective-permute-done((bf16[64,2432]{1,0:T(8,128)(2,1)}, bf16[64,2432]{1,0:T(8,128)(2,1)S(1)}, u32[]{:S(2)}, u32[]{:S(2)}) %collective-permute-start.6) | collective-permute-done | bytes 311328 | tf_op jit(solution)/shard_map/ppermute | solution.py:724
  24.5 1.5 collective-permute-start.4
  27.1 3.3 %collective-permute-start.10 = (bf16[64,1408]{1,0:T(8,128)(2,1)}, bf16[64,1408]{1,0:T(8,128)(2,1)S(1)}, u32[]{:S(2)}, u32[]{:S(2)}) collective-permute-start(bf16[64,1408]{1,0:T(8,128)(2,1)} %get-tuple-element.71), channel_id=1, source_target_pairs={{0,12},{1,13},{2,14},{3,15},{4,8},{5,9},{6,10},{7,11},{8,4},{9,5},... | collective-permute-start | bytes 540680 | tf_op jit(solution)/shard_map/ppermute | solution.py:724
  30.4 1.5 collective-permute-done.4.rest_8_
  32.3 5.0 %collective-permute-done.10.rest_15_ = bf16[64,1408]{1,0:T(8,128)(2,1)S(1)} collective-permute-done((bf16[64,1408]{1,0:T(8,128)(2,1)}, bf16[64,1408]{1,0:T(8,128)(2,1)S(1)}, u32[]{:S(2)}, u32[]{:S(2)}) %collective-permute-start.10) | collective-permute-done | bytes 180256 | tf_op jit(solution)/shard_map/ppermute | solution.py:724
  37.4 0.9 collective-permute-done.8.rest_12_.rest_24_.rest_8_
  39.0 2.0 %collective-permute-start.14 = (bf16[64,1408]{1,0:T(8,128)(2,1)S(1)}, bf16[64,1408]{1,0:T(8,128)(2,1)S(1)}, u32[]{:S(2)}, u32[]{:S(2)}) collective-permute-start(bf16[64,1408]{1,0:T(8,128)(2,1)S(1)} %collective-permute-done.10.rest_15_), channel_id=1, source_target_pairs={{0,1},{1,0},{2,3},{3,2},{4,5},{5,4},{6,7},{7,6},{8,9},{9,8},{10,11... | collective-permute-start | bytes 540680 | tf_op jit(solution)/shard_map/ppermute | solution.py:724
  41.3 1.8 %collective-permute-start.15 = (bf16[64,1408]{1,0:T(8,128)(2,1)S(1)}, bf16[64,1408]{1,0:T(8,128)(2,1)S(1)}, u32[]{:S(2)}, u32[]{:S(2)}) collective-permute-start(bf16[64,1408]{1,0:T(8,128)(2,1)S(1)} %collective-permute-done.10.rest_15_), channel_id=1, source_target_pairs={{0,2},{1,3},{2,0},{3,1},{4,6},{5,7},{6,4},{7,5},{8,10},{9,11},{10,... | collective-permute-start | bytes 540680 | tf_op jit(solution)/shard_map/ppermute | solution.py:724
  43.1 3.4 %collective-permute-done.14.rest_16_ = bf16[64,1408]{1,0:T(8,128)(2,1)S(1)} collective-permute-done((bf16[64,1408]{1,0:T(8,128)(2,1)S(1)}, bf16[64,1408]{1,0:T(8,128)(2,1)S(1)}, u32[]{:S(2)}, u32[]{:S(2)}) %collective-permute-start.14) | collective-permute-done | bytes 180256 | tf_op jit(solution)/shard_map/ppermute | solution.py:724
  46.4 1.8 %prepare.1 = (f32[4,768]{1,0:T(4,128)}, f32[1,768]{1,0:T(1,128)}, f32[1,512]{1,0:T(1,128)}, f32[1,1024]{1,0:T(1,128)}, f32[8,128]{1,0:T(8,128)}, /*index=5*/f32[1,512]{1,0:T(1,128)}) custom-call(s32[3]{0:T(128)} %pad_add_fusion.rank_ref, f32[4,2304]{1,0:T(4,128)} %cw_in.1, f32[18,128]{1,0:T(8,128)} %bitcast.15, f32[16,128]{1,0:T(8,128)} %bitcast.16, ...), custom_call_target="tpu_custom_call" | custom-call | tf_op jit(solution)/shard_map/prepare/pallas_call | solution.py:870
  48.2 1.6 collective-permute-done.15.rest_17_
  49.9 2.1 %collective-permute-done.16.rest_18_ = bf16[64,1408]{1,0:T(8,128)(2,1)S(1)} collective-permute-done((bf16[64,1408]{1,0:T(8,128)(2,1)S(1)}, bf16[64,1408]{1,0:T(8,128)(2,1)S(1)}, u32[]{:S(2)}, u32[]{:S(2)}) %collective-permute-start.16) | collective-permute-done | bytes 180256 | tf_op jit(solution)/shard_map/ppermute | solution.py:724
  53.1 14.2 %forward.1 = (f32[8,128]{1,0:T(8,128)}, bf16[512,1024]{1,0:T(8,128)(2,1)}, f32[512,1408]{1,0:T(8,128)}, f32[512,512]{1,0:T(8,128)}, f32[512,512]{1,0:T(8,128)}) custom-call(s32[3]{0:T(128)} %pad_add_fusion.rank_ref, f32[1,1024]{1,0:T(1,128)} %get-tuple-element.61.gain_ref, f32[1,512]{1,0:T(1,128)} %get-tuple-element.62.gate_gain_ref.gain_ref, ...), custom_call_target="tpu_custom_call" | custom-call | bytes 49000000 | tf_op jit(solution)/shard_map/forward/pallas_call | solution.py:935
  67.8 3.4 %collective-permute-done.17 = f32[8,128]{1,0:T(8,128)S(1)} collective-permute-done((f32[8,128]{1,0:T(8,128)}, f32[8,128]{1,0:T(8,128)S(1)}, u32[]{:S(2)}, u32[]{:S(2)}) %collective-permute-start.17) | collective-permute-done | bytes 4128 | tf_op jit(solution)/shard_map/ppermute | solution.py:724
  71.8 1.2 collective-permute-done.18
  73.6 6.2 %gated.1 = (f32[256,1024]{1,0:T(8,128)}, bf16[256,1024]{1,0:T(8,128)(2,1)}, bf16[128,1024]{1,0:T(8,128)(2,1)}, bf16[128,1024]{1,0:T(8,128)(2,1)}, bf16[128,1024]{1,0:T(8,128)(2,1)}, /*index=5*/bf16[128,1024]{1,0:T(8,128)(2,1)}) custom-call(s32[3]{0:T(128)} %pad_add_fusion.rank_ref, f32[8,128]{1,0:T(8,128)} %add.95.sums_ref, ...), custom_call_target="tpu_custom_call" | custom-call | bytes 21000000 | tf_op jit(solution)/shard_map/gated/pallas_call | solution.py:954
  80.4 1.7 %collective-permute-start.22 = (bf16[128,1024]{1,0:T(8,128)(2,1)}, bf16[128,1024]{1,0:T(8,128)(2,1)S(1)}, u32[]{:S(2)}, u32[]{:S(2)}) collective-permute-start(bf16[128,1024]{1,0:T(8,128)(2,1)} %get-tuple-element.87), channel_id=1, source_target_pairs={{0,1},{1,0},{2,3},{3,2},{4,5},{5,4},{6,7},{7,6},{8,9},{9,8},{10,11... | collective-permute-start | bytes 786440 | tf_op jit(solution)/shard_map/ppermute | solution.py:724
  82.1 1.8 %collective-permute-start.24 = (bf16[128,1024]{1,0:T(8,128)(2,1)}, bf16[128,1024]{1,0:T(8,128)(2,1)S(1)}, u32[]{:S(2)}, u32[]{:S(2)}) collective-permute-start(bf16[128,1024]{1,0:T(8,128)(2,1)} %get-tuple-element.88), channel_id=1, source_target_pairs={{0,3},{1,2},{2,1},{3,0},{4,7},{5,6},{6,5},{7,4},{8,11},{9,10},{10,... | collective-permute-start | bytes 786440 | tf_op jit(solution)/shard_map/ppermute | solution.py:724
  83.9 23.4 %backward.1 = (f32[256,1024]{1,0:T(8,128)}, bf16[256,1024]{1,0:T(8,128)(2,1)}, f32[8,896]{1,0:T(8,128)}, bf16[16,896]{1,0:T(8,128)(2,1)}, bf16[64,2816]{1,0:T(8,...) custom-call(s32[3]{0:T(128)} %pad_add_fusion.rank_ref, ...), custom_call_target="tpu_custom_call" | custom-call | bytes 84000000 | tf_op jit(solution)/shard_map/backward/pallas_call | solution.py:971
  108.6 2.9 %collective-permute-start.29 = (bf16[64,1024]{1,0:T(8,128)(2,1)S(1)}, bf16[64,1024]{1,0:T(8,128)(2,1)S(1)}, u32[]{:S(2)}, u32[]{:S(2)}) collective-permute-start(bf16[64,1024]{1,0:T(8,128)(2,1)S(1)} %slice.241), channel_id=1, source_target_pairs={{0,8},{1,9},{2,10},{3,11},{4,12},{5,13},{6,14},{7,15},{8,0},{9,1},... | collective-permute-start | bytes 393224 | tf_op jit(solution)/shard_map/ppermute | solution.py:724
  111.8 8.1 %collective-permute-done.25 = bf16[144,2816]{1,0:T(8,128)(2,1)S(1)} collective-permute-done((bf16[144,2816]{1,0:T(8,128)(2,1)}, bf16[144,2816]{1,0:T(8,128)(2,1)S(1)}, u32[]{:S(2)}, u32[]{:S(2)}) %collective-permute-start.25) | collective-permute-done | bytes 811040 | tf_op jit(solution)/shard_map/ppermute | solution.py:724
  120.1 1.8 %collective-permute-start.30 = (bf16[80,2816]{1,0:T(8,128)(2,1)S(1)}, bf16[80,2816]{1,0:T(8,128)(2,1)S(1)}, u32[]{:S(2)}, u32[]{:S(2)}) collective-permute-start(bf16[80,2816]{1,0:T(8,128)(2,1)S(1)} %fusion.6), channel_id=1, source_target_pairs={{0,1},{1,0},{2,3},{3,2},{4,5},{5,4},{6,7},{7,6},{8,9},{9,8},{10,11... | collective-permute-start | bytes 1351688 | tf_op jit(solution)/shard_map/ppermute | solution.py:724
  121.9 1.9 %collective-permute-start.21 = (bf16[256,1024]{1,0:T(8,128)(2,1)S(1)}, bf16[256,1024]{1,0:T(8,128)(2,1)S(1)}, u32[]{:S(2)}, u32[]{:S(2)}) collective-permute-start(bf16[256,1024]{1,0:T(8,128)(2,1)S(1)} %copy-done.32), channel_id=1, source_target_pairs={{0,4},{1,5},{2,6},{3,7},{4,0},{5,1},{6,2},{7,3},{8,12},{9,13},{10,... | collective-permute-start | bytes 1572872 | tf_op jit(solution)/shard_map/ppermute | solution.py:724
  123.8 0.9 fusion.5
  124.6 8.4 %collective-permute-done.30 = bf16[80,2816]{1,0:T(8,128)(2,1)S(1)} collective-permute-done((bf16[80,2816]{1,0:T(8,128)(2,1)S(1)}, bf16[80,2816]{1,0:T(8,128)(2,1)S(1)}, u32[]{:S(2)}, u32[]{:S(2)}) %collective-permute-start.30) | collective-permute-done | bytes 450592 | tf_op jit(solution)/shard_map/ppermute | solution.py:724
  133.2 3.0 %collective-permute-start.31 = (bf16[64,2816]{1,0:T(8,128)(2,1)S(1)}, bf16[64,2816]{1,0:T(8,128)(2,1)S(1)}, u32[]{:S(2)}, u32[]{:S(2)}) collective-permute-start(bf16[64,2816]{1,0:T(8,128)(2,1)S(1)} %add_convert_fusion), channel_id=1, source_target_pairs={{0,8},{1,9},{2,10},{3,11},{4,12},{5,13},{6,14},{7,15},{8,0},{9,1},... | collective-permute-start | bytes 1081352 | tf_op jit(solution)/shard_map/ppermute | solution.py:724
  136.4 2.0 %collective-permute-start.34 = (f32[8,896]{1,0:T(8,128)S(1)}, f32[8,896]{1,0:T(8,128)S(1)}, u32[]{:S(2)}, u32[]{:S(2)}) collective-permute-start(f32[8,896]{1,0:T(8,128)S(1)} %fusion.8), channel_id=1, source_target_pairs={{0,12},{1,13},{2,14},{3,15},{4,8},{5,9},{6,10},{7,11},{8,4},{9,5},... | collective-permute-start | bytes 86024 | tf_op jit(solution)/shard_map/ppermute | solution.py:724
  138.4 1.4 collective-permute-start.32
  139.9 1.0 slice_add_fusion
  141.0 1.8 %collective-permute-done.27.other_ref = f32[128,1024]{1,0:T(8,128)S(1)} collective-permute-done((f32[128,1024]{1,0:T(8,128)S(1)}, f32[128,1024]{1,0:T(8,128)S(1)}, u32[]{:S(2)}, u32[]{:S(2)}) %collective-permute-start.27) | collective-permute-done | bytes 524320 | tf_op jit(solution)/shard_map/ppermute | solution.py:727
  142.8 0.8 copy-done.23
  143.6 2.4 %tail.1 = f32[128,1024]{1,0:T(8,128)} custom-call(bf16[128,1024]{1,0:T(8,128)(2,1)} %tok_ref.1, bf16[128,1024]{1,0:T(8,128)(2,1)} %cot_ref.1, f32[1,1024]{1,0:T(1,128)} %get-tuple-element.61.gain_ref, f32[128,1024]{1,0:T(8,128)} %get-tuple-element.114.mine_ref, f32[128,1024]{1,0:T(8,128)} %copy-done.23), custom_call_target="tpu_custom_call" | custom-call | bytes 7000000 | tf_op jit(solution)/shard_map/tail/pallas_call | solution.py:1013
  146.0 1.9 %collective-permute-start.28 = (bf16[64,2816]{1,0:T(8,128)(2,1)S(1)}, bf16[64,2816]{1,0:T(8,128)(2,1)S(1)}, u32[]{:S(2)}, u32[]{:S(2)}) collective-permute-start(bf16[64,2816]{1,0:T(8,128)(2,1)S(1)} %add_convert_fusion.2), channel_id=1, source_target_pairs={{0,1},{1,0},{2,3},{3,2},{4,5},{5,4},{6,7},{7,6},{8,9},{9,8},{10,11... | collective-permute-start | bytes 1081352 | tf_op jit(solution)/shard_map/ppermute | solution.py:724
  148.8 4.6 %collective-permute-done.28 = bf16[64,2816]{1,0:T(8,128)(2,1)S(1)} collective-permute-done((bf16[64,2816]{1,0:T(8,128)(2,1)S(1)}, bf16[64,2816]{1,0:T(8,128)(2,1)S(1)}, u32[]{:S(2)}, u32[]{:S(2)}) %collective-permute-start.28) | collective-permute-done | bytes 360480 | tf_op jit(solution)/shard_map/ppermute | solution.py:724
  153.6 1.1 collective-permute-start.36
  154.7 4.7 %collective-permute-done.36 = bf16[64,1408]{1,0:T(8,128)(2,1)S(1)} collective-permute-done((bf16[64,1408]{1,0:T(8,128)(2,1)S(1)}, bf16[64,1408]{1,0:T(8,128)(2,1)S(1)}, u32[]{:S(2)}, u32[]{:S(2)}) %collective-permute-start.36) | collective-permute-done | bytes 180256 | tf_op jit(solution)/shard_map/ppermute | solution.py:724
  159.6 2.6 %collective-permute-done.37.other_ref = f32[64,3840]{1,0:T(8,128)S(1)} collective-permute-done((f32[64,3840]{1,0:T(8,128)S(1)}, f32[64,3840]{1,0:T(8,128)S(1)}, u32[]{:S(2)}, u32[]{:S(2)}) %collective-permute-start.37) | collective-permute-done | bytes 983072 | tf_op jit(solution)/shard_map/ppermute | solution.py:727
  162.2 0.9 copy-done.14
  163.1 3.2 %unpack.1 = (f32[64,4384]{1,0:T(8,128)}, f32[128,1024]{1,0:T(8,128)}, f32[4,2304]{1,0:T(4,128)}, f32[18,128]{1,0:T(8,128)}, f32[16,128]{1,0:T(8,128)}, /*index=5...) custom-call(s32[3]{0:T(128)} %pad_add_fusion.rank_ref, f32[64,3840]{1,0:T(8,128)} %copy-done.10, ...), custom_call_target="tpu_custom_call" | custom-call | tf_op jit(solution)/shard_map/unpack/pallas_call | solution.py:1029
  (138 shorter events, 10.7 us)
Async XLA Ops:
  3.5 9.3 %collective-permute-start.2 = (bf16[64,2432]{1,0:T(8,128)(2,1)}, bf16[64,2432]{1,0:T(8,128)(2,1)S(1)}, u32[]{:S(2)}, u32[]{:S(2)}) collective-permute-start(bf16[64,2432]{1,0:T(8,128)(2,1)} %get-tuple-element.69.rest_3_.rest_19_), channel_id=1, source_target_pairs={{0,1},{1,0},{2,3},{3,2},{4,5},{5,4},{6,7},{7,6},{8,9},{9,8},{10,11... | collective-permute-start | bytes 933896 | tf_op jit(solution)/shard_map/ppermute | solution.py:724
  6.4 10.0 %collective-permute-start = (bf16[64,1408]{1,0:T(8,128)(2,1)}, bf16[64,1408]{1,0:T(8,128)(2,1)S(1)}, u32[]{:S(2)}, u32[]{:S(2)}) collective-permute-start(bf16[64,1408]{1,0:T(8,128)(2,1)} %get-tuple-element.71), channel_id=1, source_target_pairs={{0,4},{1,5},{2,6},{3,7},{4,0},{5,1},{6,2},{7,3},{8,12},{9,13},{10,... | collective-permute-start | bytes 540680 | tf_op jit(solution)/shard_map/ppermute | solution.py:724
  8.0 16.5 %collective-permute-start.6 = (bf16[64,2432]{1,0:T(8,128)(2,1)}, bf16[64,2432]{1,0:T(8,128)(2,1)S(1)}, u32[]{:S(2)}, u32[]{:S(2)}) collective-permute-start(bf16[64,2432]{1,0:T(8,128)(2,1)} %get-tuple-element.69.rest_3_.rest_19_), channel_id=1, source_target_pairs={{0,8},{1,9},{2,10},{3,11},{4,12},{5,13},{6,14},{7,15},{8,0},{9,1},... | collective-permute-start | bytes 933896 | tf_op jit(solution)/shard_map/ppermute | solution.py:724
  10.6 15.4 %collective-permute-start.7 = (bf16[64,2432]{1,0:T(8,128)(2,1)}, bf16[64,2432]{1,0:T(8,128)(2,1)S(1)}, u32[]{:S(2)}, u32[]{:S(2)}) collective-permute-start(bf16[64,2432]{1,0:T(8,128)(2,1)} %get-tuple-element.69.rest_3_.rest_19_), channel_id=1, source_target_pairs={{0,2},{1,3},{2,0},{3,1},{4,6},{5,7},{6,4},{7,5},{8,10},{9,11},{10,... | collective-permute-start | bytes 933896 | tf_op jit(solution)/shard_map/ppermute | solution.py:724
  12.8 25.7 %copy-start.3 = (bf16[64,2432]{1,0:T(8,128)(2,1)}, bf16[64,2432]{1,0:T(8,128)(2,1)S(1)}, u32[]{:S(2)}) copy-start(bf16[64,2432]{1,0:T(8,128)(2,1)S(1)} %collective-permute-done.2.rest_4_.rest_20_) | copy-start | bytes 933892
  12.8 13.2 %collective-permute-start.3 = (bf16[64,2432]{1,0:T(8,128)(2,1)S(1)}, bf16[64,2432]{1,0:T(8,128)(2,1)S(1)}, u32[]{:S(2)}, u32[]{:S(2)}) collective-permute-start(bf16[64,2432]{1,0:T(8,128)(2,1)S(1)} %collective-permute-done.2.rest_4_.rest_20_), channel_id=1, source_target_pairs={{0,2},{1,3},{2,0},{3,1},{4,6},{5,7},{6,4},{7,5},{8,10},{9,11},{10,... | collective-permute-start | bytes 933896 | tf_op jit(solution)/shard_map/ppermute | solution.py:724
  15.2 23.2 %copy-start = (bf16[272,1024]{1,0:T(8,128)(2,1)}, bf16[272,1024]{1,0:T(8,128)(2,1)S(1)}, u32[]{:S(2)}) copy-start(bf16[272,1024]{1,0:T(8,128)(2,1)S(1)} %fusion.2.rest_0_) | copy-start | bytes 1671172
  16.4 22.0 %copy-start.15 = (bf16[64,1408]{1,0:T(8,128)(2,1)}, bf16[64,1408]{1,0:T(8,128)(2,1)S(1)}, u32[]{:S(2)}) copy-start(bf16[64,1408]{1,0:T(8,128)(2,1)S(1)} %collective-permute-done.rest_7_) | copy-start | bytes 540676
  16.4 21.0 %collective-permute-start.1 = (bf16[272,1024]{1,0:T(8,128)(2,1)S(1)}, bf16[272,1024]{1,0:T(8,128)(2,1)S(1)}, u32[]{:S(2)}, u32[]{:S(2)}) collective-permute-start(bf16[272,1024]{1,0:T(8,128)(2,1)S(1)} %fusion.2.rest_0_), channel_id=1, source_target_pairs={{0,4},{1,5},{2,6},{3,7},{4,0},{5,1},{6,2},{7,3},{8,12},{9,13},{10,... | collective-permute-start | bytes 1671176 | tf_op jit(solution)/shard_map/ppermute | solution.py:724
  18.0 8.0 %collective-permute-start.5 = (bf16[64,1408]{1,0:T(8,128)(2,1)S(1)}, bf16[64,1408]{1,0:T(8,128)(2,1)S(1)}, u32[]{:S(2)}, u32[]{:S(2)}) collective-permute-start(bf16[64,1408]{1,0:T(8,128)(2,1)S(1)} %collective-permute-done.rest_7_), channel_id=1, source_target_pairs={{0,2},{1,3},{2,0},{3,1},{4,6},{5,7},{6,4},{7,5},{8,10},{9,11},{10,... | collective-permute-start | bytes 540680 | tf_op jit(solution)/shard_map/ppermute | solution.py:724
  24.5 14.0 %copy-start.4 = (bf16[64,2432]{1,0:T(8,128)(2,1)}, bf16[64,2432]{1,0:T(8,128)(2,1)S(1)}, u32[]{:S(2)}) copy-start(bf16[64,2432]{1,0:T(8,128)(2,1)S(1)} %collective-permute-done.6.rest_11_.rest_23_.rest_7_) | copy-start | bytes 933892
  24.5 7.4 %collective-permute-start.4 = (bf16[64,1408]{1,0:T(8,128)(2,1)S(1)}, bf16[64,1408]{1,0:T(8,128)(2,1)S(1)}, u32[]{:S(2)}, u32[]{:S(2)}) collective-permute-start(bf16[64,1408]{1,0:T(8,128)(2,1)S(1)} %collective-permute-done.rest_7_), channel_id=1, source_target_pairs={{0,1},{1,0},{2,3},{3,2},{4,5},{5,4},{6,7},{7,6},{8,9},{9,8},{10,11... | collective-permute-start | bytes 540680 | tf_op jit(solution)/shard_map/ppermute | solution.py:724
  26.0 25.9 %copy-start.16 = (bf16[64,1408]{1,0:T(8,128)(2,1)}, bf16[64,1408]{1,0:T(8,128)(2,1)S(1)}, u32[]{:S(2)}) copy-start(bf16[64,1408]{1,0:T(8,128)(2,1)S(1)} %collective-permute-done.5.rest_9_) | copy-start | bytes 540676
  26.1 12.3 %collective-permute-start.8 = (bf16[64,2432]{1,0:T(8,128)(2,1)S(1)}, bf16[64,2432]{1,0:T(8,128)(2,1)S(1)}, u32[]{:S(2)}, u32[]{:S(2)}) collective-permute-start(bf16[64,2432]{1,0:T(8,128)(2,1)S(1)} %collective-permute-done.6.rest_11_.rest_23_.rest_7_), channel_id=1, source_target_pairs={{0,1},{1,0},{2,3},{3,2},{4,5},{5,4},{6,7},{7,6},{8,9},{9,8},{10,11... | collective-permute-start | bytes 933896 | tf_op jit(solution)/shard_map/ppermute | solution.py:724
  26.7 11.7 %collective-permute-start.9 = (bf16[64,2432]{1,0:T(8,128)(2,1)S(1)}, bf16[64,2432]{1,0:T(8,128)(2,1)S(1)}, u32[]{:S(2)}, u32[]{:S(2)}) collective-permute-start(bf16[64,2432]{1,0:T(8,128)(2,1)S(1)} %collective-permute-done.6.rest_11_.rest_23_.rest_7_), channel_id=1, source_target_pairs={{0,2},{1,3},{2,0},{3,1},{4,6},{5,7},{6,4},{7,5},{8,10},{9,11},{10,... | collective-permute-start | bytes 933896 | tf_op jit(solution)/shard_map/ppermute | solution.py:724
  27.1 10.2 %collective-permute-start.10 = (bf16[64,1408]{1,0:T(8,128)(2,1)}, bf16[64,1408]{1,0:T(8,128)(2,1)S(1)}, u32[]{:S(2)}, u32[]{:S(2)}) collective-permute-start(bf16[64,1408]{1,0:T(8,128)(2,1)} %get-tuple-element.71), channel_id=1, source_target_pairs={{0,12},{1,13},{2,14},{3,15},{4,8},{5,9},{6,10},{7,11},{8,4},{9,5},... | collective-permute-start | bytes 540680 | tf_op jit(solution)/shard_map/ppermute | solution.py:724
  31.9 20.0 %copy-start.17 = (bf16[64,1408]{1,0:T(8,128)(2,1)}, bf16[64,1408]{1,0:T(8,128)(2,1)S(1)}, u32[]{:S(2)}) copy-start(bf16[64,1408]{1,0:T(8,128)(2,1)S(1)} %collective-permute-done.4.rest_8_) | copy-start | bytes 540676
  31.9 5.5 %collective-permute-start.11 = (bf16[64,1408]{1,0:T(8,128)(2,1)S(1)}, bf16[64,1408]{1,0:T(8,128)(2,1)S(1)}, u32[]{:S(2)}, u32[]{:S(2)}) collective-permute-start(bf16[64,1408]{1,0:T(8,128)(2,1)S(1)} %collective-permute-done.4.rest_8_), channel_id=1, source_target_pairs={{0,2},{1,3},{2,0},{3,1},{4,6},{5,7},{6,4},{7,5},{8,10},{9,11},{10,... | collective-permute-start | bytes 540680 | tf_op jit(solution)/shard_map/ppermute | solution.py:724
  37.3 14.6 %copy-start.18 = (bf16[64,1408]{1,0:T(8,128)(2,1)}, bf16[64,1408]{1,0:T(8,128)(2,1)S(1)}, u32[]{:S(2)}) copy-start(bf16[64,1408]{1,0:T(8,128)(2,1)S(1)} %collective-permute-done.10.rest_15_) | copy-start | bytes 540676
  37.4 14.5 %copy-start.19 = (bf16[64,1408]{1,0:T(8,128)(2,1)}, bf16[64,1408]{1,0:T(8,128)(2,1)S(1)}, u32[]{:S(2)}) copy-start(bf16[64,1408]{1,0:T(8,128)(2,1)S(1)} %collective-permute-done.11.rest_10_) | copy-start | bytes 540676
  38.4 13.6 %copy-start.8 = (bf16[64,2432]{1,0:T(8,128)(2,1)}, bf16[64,2432]{1,0:T(8,128)(2,1)S(1)}, u32[]{:S(2)}) copy-start(bf16[64,2432]{1,0:T(8,128)(2,1)S(1)} %collective-permute-done.9.rest_13_.rest_25_.rest_9_) | copy-start | bytes 933892
  38.5 13.4 %collective-permute-start.12 = (bf16[544,1024]{1,0:T(8,128)(2,1)S(1)}, bf16[544,1024]{1,0:T(8,128)(2,1)S(1)}, u32[]{:S(2)}, u32[]{:S(2)}) collective-permute-start(bf16[544,1024]{1,0:T(8,128)(2,1)S(1)} %pad_maximum_fusion), channel_id=1, source_target_pairs={{0,16},{16,0},{1,17},{17,1},{2,18},{18,2},{3,19},{19,3},{4,20},{20... | collective-permute-start | bytes 3342344 | tf_op jit(solution)/shard_map/ppermute | solution.py:727
  39.0 7.4 %collective-permute-start.14 = (bf16[64,1408]{1,0:T(8,128)(2,1)S(1)}, bf16[64,1408]{1,0:T(8,128)(2,1)S(1)}, u32[]{:S(2)}, u32[]{:S(2)}) collective-permute-start(bf16[64,1408]{1,0:T(8,128)(2,1)S(1)} %collective-permute-done.10.rest_15_), channel_id=1, source_target_pairs={{0,1},{1,0},{2,3},{3,2},{4,5},{5,4},{6,7},{7,6},{8,9},{9,8},{10,11... | collective-permute-start | bytes 540680 | tf_op jit(solution)/shard_map/ppermute | solution.py:724
  41.0 10.9 %collective-permute-start.13 = (bf16[64,2432]{1,0:T(8,128)(2,1)S(1)}, bf16[64,2432]{1,0:T(8,128)(2,1)S(1)}, u32[]{:S(2)}, u32[]{:S(2)}) collective-permute-start(bf16[64,2432]{1,0:T(8,128)(2,1)S(1)} %collective-permute-done.8.rest_12_.rest_24_.rest_8_), channel_id=1, source_target_pairs={{0,2},{1,3},{2,0},{3,1},{4,6},{5,7},{6,4},{7,5},{8,10},{9,11},{10,... | collective-permute-start | bytes 933896 | tf_op jit(solution)/shard_map/ppermute | solution.py:724
  41.3 8.6 %collective-permute-start.15 = (bf16[64,1408]{1,0:T(8,128)(2,1)S(1)}, bf16[64,1408]{1,0:T(8,128)(2,1)S(1)}, u32[]{:S(2)}, u32[]{:S(2)}) collective-permute-start(bf16[64,1408]{1,0:T(8,128)(2,1)S(1)} %collective-permute-done.10.rest_15_), channel_id=1, source_target_pairs={{0,2},{1,3},{2,0},{3,1},{4,6},{5,7},{6,4},{7,5},{8,10},{9,11},{10,... | collective-permute-start | bytes 540680 | tf_op jit(solution)/shard_map/ppermute | solution.py:724
  46.4 5.5 %collective-permute-start.16 = (bf16[64,1408]{1,0:T(8,128)(2,1)S(1)}, bf16[64,1408]{1,0:T(8,128)(2,1)S(1)}, u32[]{:S(2)}, u32[]{:S(2)}) collective-permute-start(bf16[64,1408]{1,0:T(8,128)(2,1)S(1)} %collective-permute-done.14.rest_16_), channel_id=1, source_target_pairs={{0,2},{1,3},{2,0},{3,1},{4,6},{5,7},{6,4},{7,5},{8,10},{9,11},{10,... | collective-permute-start | bytes 540680 | tf_op jit(solution)/shard_map/ppermute | solution.py:724
  67.2 3.9 %collective-permute-start.17 = (f32[8,128]{1,0:T(8,128)}, f32[8,128]{1,0:T(8,128)S(1)}, u32[]{:S(2)}, u32[]{:S(2)}) collective-permute-start(f32[8,128]{1,0:T(8,128)} %get-tuple-element.74), channel_id=1, source_target_pairs={{0,4},{1,5},{2,6},{3,7},{4,0},{5,1},{6,2},{7,3},{8,12},{9,13},{10,... | collective-permute-start | bytes 12296 | tf_op jit(solution)/shard_map/ppermute | solution.py:724
  71.8 1.2 collective-permute-start.18
  79.9 27.4 %collective-permute-start.19 = (bf16[256,1024]{1,0:T(8,128)(2,1)}, bf16[256,1024]{1,0:T(8,128)(2,1)S(1)}, u32[]{:S(2)}, u32[]{:S(2)}) collective-permute-start(bf16[256,1024]{1,0:T(8,128)(2,1)} %get-tuple-element.78), channel_id=1, source_target_pairs={{0,4},{1,5},{2,6},{3,7},{4,0},{5,1},{6,2},{7,3},{8,12},{9,13},{10,... | collective-permute-start | bytes 1572872 | tf_op jit(solution)/shard_map/ppermute | solution.py:724
  80.4 26.9 %collective-permute-start.22 = (bf16[128,1024]{1,0:T(8,128)(2,1)}, bf16[128,1024]{1,0:T(8,128)(2,1)S(1)}, u32[]{:S(2)}, u32[]{:S(2)}) collective-permute-start(bf16[128,1024]{1,0:T(8,128)(2,1)} %get-tuple-element.87), channel_id=1, source_target_pairs={{0,1},{1,0},{2,3},{3,2},{4,5},{5,4},{6,7},{7,6},{8,9},{9,8},{10,11... | collective-permute-start | bytes 786440 | tf_op jit(solution)/shard_map/ppermute | solution.py:724
  82.1 25.2 %collective-permute-start.23 = (bf16[128,1024]{1,0:T(8,128)(2,1)}, bf16[128,1024]{1,0:T(8,128)(2,1)S(1)}, u32[]{:S(2)}, u32[]{:S(2)}) collective-permute-start(bf16[128,1024]{1,0:T(8,128)(2,1)} %get-tuple-element.79), channel_id=1, source_target_pairs={{0,2},{1,3},{2,0},{3,1},{4,6},{5,7},{6,4},{7,5},{8,10},{9,11},{10,... | collective-permute-start | bytes 786440 | tf_op jit(solution)/shard_map/ppermute | solution.py:724
  82.1 25.2 %collective-permute-start.24 = (bf16[128,1024]{1,0:T(8,128)(2,1)}, bf16[128,1024]{1,0:T(8,128)(2,1)S(1)}, u32[]{:S(2)}, u32[]{:S(2)}) collective-permute-start(bf16[128,1024]{1,0:T(8,128)(2,1)} %get-tuple-element.88), channel_id=1, source_target_pairs={{0,3},{1,2},{2,1},{3,0},{4,7},{5,6},{6,5},{7,4},{8,11},{9,10},{10,... | collective-permute-start | bytes 786440 | tf_op jit(solution)/shard_map/ppermute | solution.py:724
  83.9 24.5 %copy-start.28 = (bf16[128,1024]{1,0:T(8,128)(2,1)S(1)}, bf16[128,1024]{1,0:T(8,128)(2,1)}, u32[]{:S(2)}) copy-start(bf16[128,1024]{1,0:T(8,128)(2,1)} %get-tuple-element.97) | copy-start | bytes 786436
  107.3 12.5 %collective-permute-start.25 = (bf16[144,2816]{1,0:T(8,128)(2,1)}, bf16[144,2816]{1,0:T(8,128)(2,1)S(1)}, u32[]{:S(2)}, u32[]{:S(2)}) collective-permute-start(bf16[144,2816]{1,0:T(8,128)(2,1)} %get-tuple-element.89), channel_id=1, source_target_pairs={{0,2},{1,3},{2,0},{3,1},{4,6},{5,7},{6,4},{7,5},{8,10},{9,11},{10,... | collective-permute-start | bytes 2433032 | tf_op jit(solution)/shard_map/ppermute | solution.py:724
  108.6 11.4 %collective-permute-start.29 = (bf16[64,1024]{1,0:T(8,128)(2,1)S(1)}, bf16[64,1024]{1,0:T(8,128)(2,1)S(1)}, u32[]{:S(2)}, u32[]{:S(2)}) collective-permute-start(bf16[64,1024]{1,0:T(8,128)(2,1)S(1)} %slice.241), channel_id=1, source_target_pairs={{0,8},{1,9},{2,10},{3,11},{4,12},{5,13},{6,14},{7,15},{8,0},{9,1},... | collective-permute-start | bytes 393224 | tf_op jit(solution)/shard_map/ppermute | solution.py:724
  111.7 12.1 %collective-permute-start.20 = (f32[128,1024]{1,0:T(8,128)S(1)}, f32[128,1024]{1,0:T(8,128)S(1)}, u32[]{:S(2)}, u32[]{:S(2)}) collective-permute-start(f32[128,1024]{1,0:T(8,128)S(1)} %slice_add_fusion.2), channel_id=1, source_target_pairs={{0,16},{16,0},{1,17},{17,1},{2,18},{18,2},{3,19},{19,3},{4,20},{20... | collective-permute-start | bytes 1572872 | tf_op jit(solution)/shard_map/ppermute | solution.py:727
  120.1 13.0 %collective-permute-start.30 = (bf16[80,2816]{1,0:T(8,128)(2,1)S(1)}, bf16[80,2816]{1,0:T(8,128)(2,1)S(1)}, u32[]{:S(2)}, u32[]{:S(2)}) collective-permute-start(bf16[80,2816]{1,0:T(8,128)(2,1)S(1)} %fusion.6), channel_id=1, source_target_pairs={{0,1},{1,0},{2,3},{3,2},{4,5},{5,4},{6,7},{7,6},{8,9},{9,8},{10,11... | collective-permute-start | bytes 1351688 | tf_op jit(solution)/shard_map/ppermute | solution.py:724
  121.9 17.9 %collective-permute-start.21 = (bf16[256,1024]{1,0:T(8,128)(2,1)S(1)}, bf16[256,1024]{1,0:T(8,128)(2,1)S(1)}, u32[]{:S(2)}, u32[]{:S(2)}) collective-permute-start(bf16[256,1024]{1,0:T(8,128)(2,1)S(1)} %copy-done.32), channel_id=1, source_target_pairs={{0,4},{1,5},{2,6},{3,7},{4,0},{5,1},{6,2},{7,3},{8,12},{9,13},{10,... | collective-permute-start | bytes 1572872 | tf_op jit(solution)/shard_map/ppermute | solution.py:724
  124.6 11.6 %collective-permute-start.26 = (bf16[128,2816]{1,0:T(8,128)(2,1)S(1)}, bf16[128,2816]{1,0:T(8,128)(2,1)S(1)}, u32[]{:S(2)}, u32[]{:S(2)}) collective-permute-start(bf16[128,2816]{1,0:T(8,128)(2,1)S(1)} %copy-done.31), channel_id=1, source_target_pairs={{0,2},{1,3},{2,0},{3,1},{4,6},{5,7},{6,4},{7,5},{8,10},{9,11},{10,... | collective-permute-start | bytes 2162696 | tf_op jit(solution)/shard_map/ppermute | solution.py:724
  133.2 15.5 %collective-permute-start.31 = (bf16[64,2816]{1,0:T(8,128)(2,1)S(1)}, bf16[64,2816]{1,0:T(8,128)(2,1)S(1)}, u32[]{:S(2)}, u32[]{:S(2)}) collective-permute-start(bf16[64,2816]{1,0:T(8,128)(2,1)S(1)} %add_convert_fusion), channel_id=1, source_target_pairs={{0,8},{1,9},{2,10},{3,11},{4,12},{5,13},{6,14},{7,15},{8,0},{9,1},... | collective-permute-start | bytes 1081352 | tf_op jit(solution)/shard_map/ppermute | solution.py:724
  136.2 12.4 %collective-permute-start.33 = (f32[8,896]{1,0:T(8,128)S(1)}, f32[8,896]{1,0:T(8,128)S(1)}, u32[]{:S(2)}, u32[]{:S(2)}) collective-permute-start(f32[8,896]{1,0:T(8,128)S(1)} %fusion.8), channel_id=1, source_target_pairs={{0,4},{1,5},{2,6},{3,7},{4,0},{5,1},{6,2},{7,3},{8,12},{9,13},{10,... | collective-permute-start | bytes 86024 | tf_op jit(solution)/shard_map/ppermute | solution.py:724
  136.4 12.2 %collective-permute-start.34 = (f32[8,896]{1,0:T(8,128)S(1)}, f32[8,896]{1,0:T(8,128)S(1)}, u32[]{:S(2)}, u32[]{:S(2)}) collective-permute-start(f32[8,896]{1,0:T(8,128)S(1)} %fusion.8), channel_id=1, source_target_pairs={{0,12},{1,13},{2,14},{3,15},{4,8},{5,9},{6,10},{7,11},{8,4},{9,5},... | collective-permute-start | bytes 86024 | tf_op jit(solution)/shard_map/ppermute | solution.py:724
  138.4 10.2 %collective-permute-start.32 = (f32[8,896]{1,0:T(8,128)S(1)}, f32[8,896]{1,0:T(8,128)S(1)}, u32[]{:S(2)}, u32[]{:S(2)}) collective-permute-start(f32[8,896]{1,0:T(8,128)S(1)} %fusion.8), channel_id=1, source_target_pairs={{0,8},{1,9},{2,10},{3,11},{4,12},{5,13},{6,14},{7,15},{8,0},{9,1},... | collective-permute-start | bytes 86024 | tf_op jit(solution)/shard_map/ppermute | solution.py:724
  140.9 1.9 %collective-permute-start.27 = (f32[128,1024]{1,0:T(8,128)S(1)}, f32[128,1024]{1,0:T(8,128)S(1)}, u32[]{:S(2)}, u32[]{:S(2)}) collective-permute-start(f32[128,1024]{1,0:T(8,128)S(1)} %get-tuple-element.113), channel_id=1, source_target_pairs={{0,16},{16,0},{1,17},{17,1},{2,18},{18,2},{3,19},{19,3},{4,20},{20... | collective-permute-start | bytes 1572872 | tf_op jit(solution)/shard_map/ppermute | solution.py:727
  146.0 7.4 %collective-permute-start.28 = (bf16[64,2816]{1,0:T(8,128)(2,1)S(1)}, bf16[64,2816]{1,0:T(8,128)(2,1)S(1)}, u32[]{:S(2)}, u32[]{:S(2)}) collective-permute-start(bf16[64,2816]{1,0:T(8,128)(2,1)S(1)} %add_convert_fusion.2), channel_id=1, source_target_pairs={{0,1},{1,0},{2,3},{3,2},{4,5},{5,4},{6,7},{7,6},{8,9},{9,8},{10,11... | collective-permute-start | bytes 1081352 | tf_op jit(solution)/shard_map/ppermute | solution.py:724
  148.6 5.0 %collective-permute-start.35 = (f32[8,1792]{1,0:T(8,128)S(1)}, f32[8,1792]{1,0:T(8,128)S(1)}, u32[]{:S(2)}, u32[]{:S(2)}) collective-permute-start(f32[8,1792]{1,0:T(8,128)S(1)} %pad_maximum_fusion.2.small_mine_ref), channel_id=1, source_target_pairs={{0,16},{16,0},{1,17},{17,1},{2,18},{18,2},{3,19},{19,3},{4,20},{20... | collective-permute-start | bytes 172040 | tf_op jit(solution)/shard_map/ppermute | solution.py:727
  153.6 5.8 %collective-permute-start.36 = (bf16[64,1408]{1,0:T(8,128)(2,1)S(1)}, bf16[64,1408]{1,0:T(8,128)(2,1)S(1)}, u32[]{:S(2)}, u32[]{:S(2)}) collective-permute-start(bf16[64,1408]{1,0:T(8,128)(2,1)S(1)} %slice_add_fusion.4), channel_id=1, source_target_pairs={{0,4},{1,5},{2,6},{3,7},{4,0},{5,1},{6,2},{7,3},{8,12},{9,13},{10,... | collective-permute-start | bytes 540680 | tf_op jit(solution)/shard_map/ppermute | solution.py:724
  159.5 2.6 %collective-permute-start.37 = (f32[64,3840]{1,0:T(8,128)S(1)}, f32[64,3840]{1,0:T(8,128)S(1)}, u32[]{:S(2)}, u32[]{:S(2)}) collective-permute-start(f32[64,3840]{1,0:T(8,128)S(1)} %pad_maximum_fusion.1.mine_ref), channel_id=1, source_target_pairs={{0,16},{16,0},{1,17},{17,1},{2,18},{18,2},{3,19},{19,3},{4,20},{20... | collective-permute-start | bytes 2949128 | tf_op jit(solution)/shard_map/ppermute | solution.py:727
  (23 other events, 115.1 us)

commit v4 on v3

--- a/solution.py
+++ b/solution.py
@@ -34,8 +34,8 @@
     return pl.CostEstimate(flops=0, transcendentals=0, bytes_accessed=microseconds * 3500000)
 
 
-def params():
-    return pltpu.CompilerParams(vmem_limit_bytes=56 * MIB)
+def params(mebibytes=56):
+    return pltpu.CompilerParams(vmem_limit_bytes=mebibytes * MIB)
 
 
 def in_vmem(n):
@@ -1015,7 +1015,7 @@
         out_shape=arr(own_tokens, model),
         in_specs=in_vmem(5),
         out_specs=in_vmem(1)[0],
-        compiler_params=params(),
+        compiler_params=params(8),
         cost_estimate=cost(2),
         name="tail",
     )(tokens, cotangent, norm_g, *d_normed_parts)
@@ -1034,7 +1034,7 @@
             ],
             in_specs=in_smem(1) + in_vmem(4),
             out_specs=in_vmem(9),
-            compiler_params=params(),
+            compiler_params=params(8),
             name="unpack",
         )(rank, grad_sum, links.swap(grad_sum), small, small_other)
         d_conv_bias, d_gate_gain, d_norm_gain = (x.reshape(-1) for x in (d_conv_bias, d_gate_gain, d_norm_gain))

time: 167 us -> 162 us (0.970)
  Pallas kernels: 53.4 us -> 51.1 us
  transfers between devices with their start and end apart: 38 -> 38, of which waited for: 18 -> 18; matrix products, arithmetic and copies ran while one was open for 3% -> 3% of each run, Pallas kernels for 17% -> 16%
where the time goes in v4:
time: 162 us
  waiting for transfers between devices  56.8 us (35%)
  Pallas kernels  51.1 us (32%)
  starting transfers between devices  43.8 us (27%)
  other arithmetic  6.76 us (4%)
  local copies, waits for them, and re-layouts  1.92 us (1%)
    ppermute x32, waiting for transfers between devices, exchange(): return lax.ppermute(x, BOTH, pairs)  51.9 us
    ppermute x32, starting transfers between devices, exchange(): return lax.ppermute(x, BOTH, pairs)  43 us
    pallas_call x1, Pallas kernels, per_device(): pl.pallas_call(functools.partial(backward_kernel, places, in_count, len(i...  23.4 us
    pallas_call x1, Pallas kernels, per_device(): pl.pallas_call(functools.partial(forward_kernel, places, in_count, out_co...  14.2 us
    pallas_call x1, Pallas kernels, per_device(): pl.pallas_call(functools.partial(gated_kernel, places, out_count, len(out...  6.24 us
    ppermute x6, waiting for transfers between devices, swap(): return lax.ppermute(x, 'rep', [(0, 1), (1, 0)])  4.83 us
  transfers between devices with their start and end apart: 38, of which 18 were waited for; matrix products, arithmetic and copies ran while one was open for 3% of the time, Pallas kernels for 16%

profile of v4, /device:TPU:0, one launch (start us, length us, event | category | flops | bytes accessed | tf_op | source)
XLA Modules:
  0.0 161.6 jit_solution(6883717274987034352)
XLA Ops:
  1.3 2.2 %pack.1 = (bf16[64,2432]{1,0:T(8,128)(2,1)}, bf16[64,1408]{1,0:T(8,128)(2,1)}) custom-call(s32[3]{0:T(128)} %pad_add_fusion.rank_ref, bf16[64,4384]{1,0:T(8,128)(2,1)} %in_ref.1, bf16[128,1024]{1,0:T(8,128)(2,1)} %out_ref.1), custom_call_target="tpu_custom_call" | custom-call | tf_op jit(solution)/shard_map/pack/pallas_call | solution.py:860
  3.5 2.9 %collective-permute-start.2 = (bf16[64,2432]{1,0:T(8,128)(2,1)}, bf16[64,2432]{1,0:T(8,128)(2,1)S(1)}, u32[]{:S(2)}, u32[]{:S(2)}) collective-permute-start(bf16[64,2432]{1,0:T(8,128)(2,1)} %get-tuple-element.69.rest_3_.rest_19_), channel_id=1, source_target_pairs={{0,1},{1,0},{2,3},{3,2},{4,5},{5,4},{6,7},{7,6},{8,9},{9,8},{10,11... | collective-permute-start | bytes 933896 | tf_op jit(solution)/shard_map/ppermute | solution.py:724
  6.4 1.6 collective-permute-start
  8.0 2.6 %collective-permute-start.6 = (bf16[64,2432]{1,0:T(8,128)(2,1)}, bf16[64,2432]{1,0:T(8,128)(2,1)S(1)}, u32[]{:S(2)}, u32[]{:S(2)}) collective-permute-start(bf16[64,2432]{1,0:T(8,128)(2,1)} %get-tuple-element.69.rest_3_.rest_19_), channel_id=1, source_target_pairs={{0,8},{1,9},{2,10},{3,11},{4,12},{5,13},{6,14},{7,15},{8,0},{9,1},... | collective-permute-start | bytes 933896 | tf_op jit(solution)/shard_map/ppermute | solution.py:724
  10.6 1.5 collective-permute-start.7
  12.8 1.4 collective-permute-start.3
  14.1 1.1 fusion.2.rest_0_
  15.2 1.2 collective-permute-done.rest_7_
  16.4 1.6 collective-permute-start.1
  18.1 6.4 %collective-permute-done.6.rest_11_.rest_23_.rest_7_ = bf16[64,2432]{1,0:T(8,128)(2,1)S(1)} collective-permute-done((bf16[64,2432]{1,0:T(8,128)(2,1)}, bf16[64,2432]{1,0:T(8,128)(2,1)S(1)}, u32[]{:S(2)}, u32[]{:S(2)}) %collective-permute-start.6) | collective-permute-done | bytes 311328 | tf_op jit(solution)/shard_map/ppermute | solution.py:724
  24.5 1.5 collective-permute-start.4
  27.1 3.3 %collective-permute-start.10 = (bf16[64,1408]{1,0:T(8,128)(2,1)}, bf16[64,1408]{1,0:T(8,128)(2,1)S(1)}, u32[]{:S(2)}, u32[]{:S(2)}) collective-permute-start(bf16[64,1408]{1,0:T(8,128)(2,1)} %get-tuple-element.71), channel_id=1, source_target_pairs={{0,12},{1,13},{2,14},{3,15},{4,8},{5,9},{6,10},{7,11},{8,4},{9,5},... | collective-permute-start | bytes 540680 | tf_op jit(solution)/shard_map/ppermute | solution.py:724
  30.4 1.5 collective-permute-done.4.rest_8_
  32.3 5.0 %collective-permute-done.10.rest_15_ = bf16[64,1408]{1,0:T(8,128)(2,1)S(1)} collective-permute-done((bf16[64,1408]{1,0:T(8,128)(2,1)}, bf16[64,1408]{1,0:T(8,128)(2,1)S(1)}, u32[]{:S(2)}, u32[]{:S(2)}) %collective-permute-start.10) | collective-permute-done | bytes 180256 | tf_op jit(solution)/shard_map/ppermute | solution.py:724
  37.4 0.9 collective-permute-done.8.rest_12_.rest_24_.rest_8_
  39.0 2.0 %collective-permute-start.14 = (bf16[64,1408]{1,0:T(8,128)(2,1)S(1)}, bf16[64,1408]{1,0:T(8,128)(2,1)S(1)}, u32[]{:S(2)}, u32[]{:S(2)}) collective-permute-start(bf16[64,1408]{1,0:T(8,128)(2,1)S(1)} %collective-permute-done.10.rest_15_), channel_id=1, source_target_pairs={{0,1},{1,0},{2,3},{3,2},{4,5},{5,4},{6,7},{7,6},{8,9},{9,8},{10,11... | collective-permute-start | bytes 540680 | tf_op jit(solution)/shard_map/ppermute | solution.py:724
  41.2 1.8 %collective-permute-start.15 = (bf16[64,1408]{1,0:T(8,128)(2,1)S(1)}, bf16[64,1408]{1,0:T(8,128)(2,1)S(1)}, u32[]{:S(2)}, u32[]{:S(2)}) collective-permute-start(bf16[64,1408]{1,0:T(8,128)(2,1)S(1)} %collective-permute-done.10.rest_15_), channel_id=1, source_target_pairs={{0,2},{1,3},{2,0},{3,1},{4,6},{5,7},{6,4},{7,5},{8,10},{9,11},{10,... | collective-permute-start | bytes 540680 | tf_op jit(solution)/shard_map/ppermute | solution.py:724
  43.1 3.4 %collective-permute-done.14.rest_16_ = bf16[64,1408]{1,0:T(8,128)(2,1)S(1)} collective-permute-done((bf16[64,1408]{1,0:T(8,128)(2,1)S(1)}, bf16[64,1408]{1,0:T(8,128)(2,1)S(1)}, u32[]{:S(2)}, u32[]{:S(2)}) %collective-permute-start.14) | collective-permute-done | bytes 180256 | tf_op jit(solution)/shard_map/ppermute | solution.py:724
  46.4 1.8 %prepare.1 = (f32[4,768]{1,0:T(4,128)}, f32[1,768]{1,0:T(1,128)}, f32[1,512]{1,0:T(1,128)}, f32[1,1024]{1,0:T(1,128)}, f32[8,128]{1,0:T(8,128)}, /*index=5*/f32[1,512]{1,0:T(1,128)}) custom-call(s32[3]{0:T(128)} %pad_add_fusion.rank_ref, f32[4,2304]{1,0:T(4,128)} %cw_in.1, f32[18,128]{1,0:T(8,128)} %bitcast.15, f32[16,128]{1,0:T(8,128)} %bitcast.16, ...), custom_call_target="tpu_custom_call" | custom-call | tf_op jit(solution)/shard_map/prepare/pallas_call | solution.py:870
  48.2 1.6 %collective-permute-done.15.rest_17_ = bf16[64,1408]{1,0:T(8,128)(2,1)S(1)} collective-permute-done((bf16[64,1408]{1,0:T(8,128)(2,1)S(1)}, bf16[64,1408]{1,0:T(8,128)(2,1)S(1)}, u32[]{:S(2)}, u32[]{:S(2)}) %collective-permute-start.15) | collective-permute-done | bytes 180256 | tf_op jit(solution)/shard_map/ppermute | solution.py:724
  49.9 2.1 %collective-permute-done.16.rest_18_ = bf16[64,1408]{1,0:T(8,128)(2,1)S(1)} collective-permute-done((bf16[64,1408]{1,0:T(8,128)(2,1)S(1)}, bf16[64,1408]{1,0:T(8,128)(2,1)S(1)}, u32[]{:S(2)}, u32[]{:S(2)}) %collective-permute-start.16) | collective-permute-done | bytes 180256 | tf_op jit(solution)/shard_map/ppermute | solution.py:724
  53.1 14.2 %forward.1 = (f32[8,128]{1,0:T(8,128)}, bf16[512,1024]{1,0:T(8,128)(2,1)}, f32[512,1408]{1,0:T(8,128)}, f32[512,512]{1,0:T(8,128)}, f32[512,512]{1,0:T(8,128)}) custom-call(s32[3]{0:T(128)} %pad_add_fusion.rank_ref, f32[1,1024]{1,0:T(1,128)} %get-tuple-element.61.gain_ref, f32[1,512]{1,0:T(1,128)} %get-tuple-element.62.gate_gain_ref.gain_ref, ...), custom_call_target="tpu_custom_call" | custom-call | bytes 49000000 | tf_op jit(solution)/shard_map/forward/pallas_call | solution.py:935
  67.8 3.4 %collective-permute-done.17 = f32[8,128]{1,0:T(8,128)S(1)} collective-permute-done((f32[8,128]{1,0:T(8,128)}, f32[8,128]{1,0:T(8,128)S(1)}, u32[]{:S(2)}, u32[]{:S(2)}) %collective-permute-start.17) | collective-permute-done | bytes 4128 | tf_op jit(solution)/shard_map/ppermute | solution.py:724
  71.8 1.2 collective-permute-done.18
  73.6 6.2 %gated.1 = (f32[256,1024]{1,0:T(8,128)}, bf16[256,1024]{1,0:T(8,128)(2,1)}, bf16[128,1024]{1,0:T(8,128)(2,1)}, bf16[128,1024]{1,0:T(8,128)(2,1)}, bf16[128,1024]{1,0:T(8,128)(2,1)}, /*index=5*/bf16[128,1024]{1,0:T(8,128)(2,1)}) custom-call(s32[3]{0:T(128)} %pad_add_fusion.rank_ref, f32[8,128]{1,0:T(8,128)} %add.95.sums_ref, ...), custom_call_target="tpu_custom_call" | custom-call | bytes 21000000 | tf_op jit(solution)/shard_map/gated/pallas_call | solution.py:954
  80.4 1.7 %collective-permute-start.22 = (bf16[128,1024]{1,0:T(8,128)(2,1)}, bf16[128,1024]{1,0:T(8,128)(2,1)S(1)}, u32[]{:S(2)}, u32[]{:S(2)}) collective-permute-start(bf16[128,1024]{1,0:T(8,128)(2,1)} %get-tuple-element.87), channel_id=1, source_target_pairs={{0,1},{1,0},{2,3},{3,2},{4,5},{5,4},{6,7},{7,6},{8,9},{9,8},{10,11... | collective-permute-start | bytes 786440 | tf_op jit(solution)/shard_map/ppermute | solution.py:724
  82.1 1.8 %collective-permute-start.24 = (bf16[128,1024]{1,0:T(8,128)(2,1)}, bf16[128,1024]{1,0:T(8,128)(2,1)S(1)}, u32[]{:S(2)}, u32[]{:S(2)}) collective-permute-start(bf16[128,1024]{1,0:T(8,128)(2,1)} %get-tuple-element.88), channel_id=1, source_target_pairs={{0,3},{1,2},{2,1},{3,0},{4,7},{5,6},{6,5},{7,4},{8,11},{9,10},{10,... | collective-permute-start | bytes 786440 | tf_op jit(solution)/shard_map/ppermute | solution.py:724
  83.9 23.4 %backward.1 = (f32[256,1024]{1,0:T(8,128)}, bf16[256,1024]{1,0:T(8,128)(2,1)}, f32[8,896]{1,0:T(8,128)}, bf16[16,896]{1,0:T(8,128)(2,1)}, bf16[64,2816]{1,0:T(8,...) custom-call(s32[3]{0:T(128)} %pad_add_fusion.rank_ref, ...), custom_call_target="tpu_custom_call" | custom-call | bytes 84000000 | tf_op jit(solution)/shard_map/backward/pallas_call | solution.py:971
  107.7 0.8 convert_element_type.116
  108.6 2.9 %collective-permute-start.29 = (bf16[64,1024]{1,0:T(8,128)(2,1)S(1)}, bf16[64,1024]{1,0:T(8,128)(2,1)S(1)}, u32[]{:S(2)}, u32[]{:S(2)}) collective-permute-start(bf16[64,1024]{1,0:T(8,128)(2,1)S(1)} %slice.241), channel_id=1, source_target_pairs={{0,8},{1,9},{2,10},{3,11},{4,12},{5,13},{6,14},{7,15},{8,0},{9,1},... | collective-permute-start | bytes 393224 | tf_op jit(solution)/shard_map/ppermute | solution.py:724
  111.8 8.1 %collective-permute-done.25 = bf16[144,2816]{1,0:T(8,128)(2,1)S(1)} collective-permute-done((bf16[144,2816]{1,0:T(8,128)(2,1)}, bf16[144,2816]{1,0:T(8,128)(2,1)S(1)}, u32[]{:S(2)}, u32[]{:S(2)}) %collective-permute-start.25) | collective-permute-done | bytes 811040 | tf_op jit(solution)/shard_map/ppermute | solution.py:724
  120.1 1.8 %collective-permute-start.30 = (bf16[80,2816]{1,0:T(8,128)(2,1)S(1)}, bf16[80,2816]{1,0:T(8,128)(2,1)S(1)}, u32[]{:S(2)}, u32[]{:S(2)}) collective-permute-start(bf16[80,2816]{1,0:T(8,128)(2,1)S(1)} %fusion.6), channel_id=1, source_target_pairs={{0,1},{1,0},{2,3},{3,2},{4,5},{5,4},{6,7},{7,6},{8,9},{9,8},{10,11... | collective-permute-start | bytes 1351688 | tf_op jit(solution)/shard_map/ppermute | solution.py:724
  121.9 1.9 %collective-permute-start.21 = (bf16[256,1024]{1,0:T(8,128)(2,1)S(1)}, bf16[256,1024]{1,0:T(8,128)(2,1)S(1)}, u32[]{:S(2)}, u32[]{:S(2)}) collective-permute-start(bf16[256,1024]{1,0:T(8,128)(2,1)S(1)} %copy-done.30), channel_id=1, source_target_pairs={{0,4},{1,5},{2,6},{3,7},{4,0},{5,1},{6,2},{7,3},{8,12},{9,13},{10,... | collective-permute-start | bytes 1572872 | tf_op jit(solution)/shard_map/ppermute | solution.py:724
  123.8 0.9 fusion.5
  124.7 8.4 %collective-permute-done.30 = bf16[80,2816]{1,0:T(8,128)(2,1)S(1)} collective-permute-done((bf16[80,2816]{1,0:T(8,128)(2,1)S(1)}, bf16[80,2816]{1,0:T(8,128)(2,1)S(1)}, u32[]{:S(2)}, u32[]{:S(2)}) %collective-permute-start.30) | collective-permute-done | bytes 450592 | tf_op jit(solution)/shard_map/ppermute | solution.py:724
  133.2 3.0 %collective-permute-start.31 = (bf16[64,2816]{1,0:T(8,128)(2,1)S(1)}, bf16[64,2816]{1,0:T(8,128)(2,1)S(1)}, u32[]{:S(2)}, u32[]{:S(2)}) collective-permute-start(bf16[64,2816]{1,0:T(8,128)(2,1)S(1)} %add_convert_fusion), channel_id=1, source_target_pairs={{0,8},{1,9},{2,10},{3,11},{4,12},{5,13},{6,14},{7,15},{8,0},{9,1},... | collective-permute-start | bytes 1081352 | tf_op jit(solution)/shard_map/ppermute | solution.py:724
  136.4 2.0 %collective-permute-start.34 = (f32[8,896]{1,0:T(8,128)S(1)}, f32[8,896]{1,0:T(8,128)S(1)}, u32[]{:S(2)}, u32[]{:S(2)}) collective-permute-start(f32[8,896]{1,0:T(8,128)S(1)} %fusion.8), channel_id=1, source_target_pairs={{0,12},{1,13},{2,14},{3,15},{4,8},{5,9},{6,10},{7,11},{8,4},{9,5},... | collective-permute-start | bytes 86024 | tf_op jit(solution)/shard_map/ppermute | solution.py:724
  138.5 1.4 collective-permute-start.32
  140.2 0.7 copy-done.25
  141.0 1.1 collective-permute-done.27.other_ref
  142.1 1.1 tail.1
  143.2 1.9 %collective-permute-start.28 = (bf16[64,2816]{1,0:T(8,128)(2,1)S(1)}, bf16[64,2816]{1,0:T(8,128)(2,1)S(1)}, u32[]{:S(2)}, u32[]{:S(2)}) collective-permute-start(bf16[64,2816]{1,0:T(8,128)(2,1)S(1)} %add_convert_fusion.2), channel_id=1, source_target_pairs={{0,1},{1,0},{2,3},{3,2},{4,5},{5,4},{6,7},{7,6},{8,9},{9,8},{10,11... | collective-permute-start | bytes 1081352 | tf_op jit(solution)/shard_map/ppermute | solution.py:724
  145.2 3.4 %collective-permute-done.32 = f32[8,896]{1,0:T(8,128)S(1)} collective-permute-done((f32[8,896]{1,0:T(8,128)S(1)}, f32[8,896]{1,0:T(8,128)S(1)}, u32[]{:S(2)}, u32[]{:S(2)}) %collective-permute-start.32) | collective-permute-done | bytes 28704 | tf_op jit(solution)/shard_map/ppermute | solution.py:724
  148.8 1.8 %collective-permute-done.28 = bf16[64,2816]{1,0:T(8,128)(2,1)S(1)} collective-permute-done((bf16[64,2816]{1,0:T(8,128)(2,1)S(1)}, bf16[64,2816]{1,0:T(8,128)(2,1)S(1)}, u32[]{:S(2)}, u32[]{:S(2)}) %collective-permute-start.28) | collective-permute-done | bytes 360480 | tf_op jit(solution)/shard_map/ppermute | solution.py:724
  150.8 1.1 collective-permute-start.36
  151.9 4.7 %collective-permute-done.36 = bf16[64,1408]{1,0:T(8,128)(2,1)S(1)} collective-permute-done((bf16[64,1408]{1,0:T(8,128)(2,1)S(1)}, bf16[64,1408]{1,0:T(8,128)(2,1)S(1)}, u32[]{:S(2)}, u32[]{:S(2)}) %collective-permute-start.36) | collective-permute-done | bytes 180256 | tf_op jit(solution)/shard_map/ppermute | solution.py:724
  156.8 2.6 %collective-permute-done.37.other_ref = f32[64,3840]{1,0:T(8,128)S(1)} collective-permute-done((f32[64,3840]{1,0:T(8,128)S(1)}, f32[64,3840]{1,0:T(8,128)S(1)}, u32[]{:S(2)}, u32[]{:S(2)}) %collective-permute-start.37) | collective-permute-done | bytes 983072 | tf_op jit(solution)/shard_map/ppermute | solution.py:727
  159.4 2.3 %unpack.1 = (f32[64,4384]{1,0:T(8,128)}, f32[128,1024]{1,0:T(8,128)}, f32[4,2304]{1,0:T(4,128)}, f32[18,128]{1,0:T(8,128)}, f32[16,128]{1,0:T(8,128)}, /*index=5...) custom-call(s32[3]{0:T(128)S(1)} %copy-done.2, f32[64,3840]{1,0:T(8,128)S(1)} %pad_maximum_fusion.1.mine_ref, ...), custom_call_target="tpu_custom_call" | custom-call | tf_op jit(solution)/shard_map/unpack/pallas_call | solution.py:1029
  (134 shorter events, 9.5 us)
Async XLA Ops:
  3.5 9.3 %collective-permute-start.2 = (bf16[64,2432]{1,0:T(8,128)(2,1)}, bf16[64,2432]{1,0:T(8,128)(2,1)S(1)}, u32[]{:S(2)}, u32[]{:S(2)}) collective-permute-start(bf16[64,2432]{1,0:T(8,128)(2,1)} %get-tuple-element.69.rest_3_.rest_19_), channel_id=1, source_target_pairs={{0,1},{1,0},{2,3},{3,2},{4,5},{5,4},{6,7},{7,6},{8,9},{9,8},{10,11... | collective-permute-start | bytes 933896 | tf_op jit(solution)/shard_map/ppermute | solution.py:724
  6.4 10.0 %collective-permute-start = (bf16[64,1408]{1,0:T(8,128)(2,1)}, bf16[64,1408]{1,0:T(8,128)(2,1)S(1)}, u32[]{:S(2)}, u32[]{:S(2)}) collective-permute-start(bf16[64,1408]{1,0:T(8,128)(2,1)} %get-tuple-element.71), channel_id=1, source_target_pairs={{0,4},{1,5},{2,6},{3,7},{4,0},{5,1},{6,2},{7,3},{8,12},{9,13},{10,... | collective-permute-start | bytes 540680 | tf_op jit(solution)/shard_map/ppermute | solution.py:724
  8.0 16.5 %collective-permute-start.6 = (bf16[64,2432]{1,0:T(8,128)(2,1)}, bf16[64,2432]{1,0:T(8,128)(2,1)S(1)}, u32[]{:S(2)}, u32[]{:S(2)}) collective-permute-start(bf16[64,2432]{1,0:T(8,128)(2,1)} %get-tuple-element.69.rest_3_.rest_19_), channel_id=1, source_target_pairs={{0,8},{1,9},{2,10},{3,11},{4,12},{5,13},{6,14},{7,15},{8,0},{9,1},... | collective-permute-start | bytes 933896 | tf_op jit(solution)/shard_map/ppermute | solution.py:724
  10.6 15.4 %collective-permute-start.7 = (bf16[64,2432]{1,0:T(8,128)(2,1)}, bf16[64,2432]{1,0:T(8,128)(2,1)S(1)}, u32[]{:S(2)}, u32[]{:S(2)}) collective-permute-start(bf16[64,2432]{1,0:T(8,128)(2,1)} %get-tuple-element.69.rest_3_.rest_19_), channel_id=1, source_target_pairs={{0,2},{1,3},{2,0},{3,1},{4,6},{5,7},{6,4},{7,5},{8,10},{9,11},{10,... | collective-permute-start | bytes 933896 | tf_op jit(solution)/shard_map/ppermute | solution.py:724
  12.8 25.7 %copy-start.7 = (bf16[64,2432]{1,0:T(8,128)(2,1)}, bf16[64,2432]{1,0:T(8,128)(2,1)S(1)}, u32[]{:S(2)}) copy-start(bf16[64,2432]{1,0:T(8,128)(2,1)S(1)} %collective-permute-done.2.rest_4_.rest_20_) | copy-start | bytes 933892
  12.8 13.2 %collective-permute-start.3 = (bf16[64,2432]{1,0:T(8,128)(2,1)S(1)}, bf16[64,2432]{1,0:T(8,128)(2,1)S(1)}, u32[]{:S(2)}, u32[]{:S(2)}) collective-permute-start(bf16[64,2432]{1,0:T(8,128)(2,1)S(1)} %collective-permute-done.2.rest_4_.rest_20_), channel_id=1, source_target_pairs={{0,2},{1,3},{2,0},{3,1},{4,6},{5,7},{6,4},{7,5},{8,10},{9,11},{10,... | collective-permute-start | bytes 933896 | tf_op jit(solution)/shard_map/ppermute | solution.py:724
  15.2 23.2 %copy-start.4 = (bf16[272,1024]{1,0:T(8,128)(2,1)}, bf16[272,1024]{1,0:T(8,128)(2,1)S(1)}, u32[]{:S(2)}) copy-start(bf16[272,1024]{1,0:T(8,128)(2,1)S(1)} %fusion.2.rest_0_) | copy-start | bytes 1671172
  16.4 22.0 %copy-start.16 = (bf16[64,1408]{1,0:T(8,128)(2,1)}, bf16[64,1408]{1,0:T(8,128)(2,1)S(1)}, u32[]{:S(2)}) copy-start(bf16[64,1408]{1,0:T(8,128)(2,1)S(1)} %collective-permute-done.rest_7_) | copy-start | bytes 540676
  16.4 21.0 %collective-permute-start.1 = (bf16[272,1024]{1,0:T(8,128)(2,1)S(1)}, bf16[272,1024]{1,0:T(8,128)(2,1)S(1)}, u32[]{:S(2)}, u32[]{:S(2)}) collective-permute-start(bf16[272,1024]{1,0:T(8,128)(2,1)S(1)} %fusion.2.rest_0_), channel_id=1, source_target_pairs={{0,4},{1,5},{2,6},{3,7},{4,0},{5,1},{6,2},{7,3},{8,12},{9,13},{10,... | collective-permute-start | bytes 1671176 | tf_op jit(solution)/shard_map/ppermute | solution.py:724
  18.0 8.0 %collective-permute-start.5 = (bf16[64,1408]{1,0:T(8,128)(2,1)S(1)}, bf16[64,1408]{1,0:T(8,128)(2,1)S(1)}, u32[]{:S(2)}, u32[]{:S(2)}) collective-permute-start(bf16[64,1408]{1,0:T(8,128)(2,1)S(1)} %collective-permute-done.rest_7_), channel_id=1, source_target_pairs={{0,2},{1,3},{2,0},{3,1},{4,6},{5,7},{6,4},{7,5},{8,10},{9,11},{10,... | collective-permute-start | bytes 540680 | tf_op jit(solution)/shard_map/ppermute | solution.py:724
  24.5 14.0 %copy-start.8 = (bf16[64,2432]{1,0:T(8,128)(2,1)}, bf16[64,2432]{1,0:T(8,128)(2,1)S(1)}, u32[]{:S(2)}) copy-start(bf16[64,2432]{1,0:T(8,128)(2,1)S(1)} %collective-permute-done.6.rest_11_.rest_23_.rest_7_) | copy-start | bytes 933892
  24.5 7.4 %collective-permute-start.4 = (bf16[64,1408]{1,0:T(8,128)(2,1)S(1)}, bf16[64,1408]{1,0:T(8,128)(2,1)S(1)}, u32[]{:S(2)}, u32[]{:S(2)}) collective-permute-start(bf16[64,1408]{1,0:T(8,128)(2,1)S(1)} %collective-permute-done.rest_7_), channel_id=1, source_target_pairs={{0,1},{1,0},{2,3},{3,2},{4,5},{5,4},{6,7},{7,6},{8,9},{9,8},{10,11... | collective-permute-start | bytes 540680 | tf_op jit(solution)/shard_map/ppermute | solution.py:724
  26.0 25.9 %copy-start.17 = (bf16[64,1408]{1,0:T(8,128)(2,1)}, bf16[64,1408]{1,0:T(8,128)(2,1)S(1)}, u32[]{:S(2)}) copy-start(bf16[64,1408]{1,0:T(8,128)(2,1)S(1)} %collective-permute-done.5.rest_9_) | copy-start | bytes 540676
  26.0 12.3 %collective-permute-start.8 = (bf16[64,2432]{1,0:T(8,128)(2,1)S(1)}, bf16[64,2432]{1,0:T(8,128)(2,1)S(1)}, u32[]{:S(2)}, u32[]{:S(2)}) collective-permute-start(bf16[64,2432]{1,0:T(8,128)(2,1)S(1)} %collective-permute-done.6.rest_11_.rest_23_.rest_7_), channel_id=1, source_target_pairs={{0,1},{1,0},{2,3},{3,2},{4,5},{5,4},{6,7},{7,6},{8,9},{9,8},{10,11... | collective-permute-start | bytes 933896 | tf_op jit(solution)/shard_map/ppermute | solution.py:724
  26.6 11.7 %collective-permute-start.9 = (bf16[64,2432]{1,0:T(8,128)(2,1)S(1)}, bf16[64,2432]{1,0:T(8,128)(2,1)S(1)}, u32[]{:S(2)}, u32[]{:S(2)}) collective-permute-start(bf16[64,2432]{1,0:T(8,128)(2,1)S(1)} %collective-permute-done.6.rest_11_.rest_23_.rest_7_), channel_id=1, source_target_pairs={{0,2},{1,3},{2,0},{3,1},{4,6},{5,7},{6,4},{7,5},{8,10},{9,11},{10,... | collective-permute-start | bytes 933896 | tf_op jit(solution)/shard_map/ppermute | solution.py:724
  27.1 10.2 %collective-permute-start.10 = (bf16[64,1408]{1,0:T(8,128)(2,1)}, bf16[64,1408]{1,0:T(8,128)(2,1)S(1)}, u32[]{:S(2)}, u32[]{:S(2)}) collective-permute-start(bf16[64,1408]{1,0:T(8,128)(2,1)} %get-tuple-element.71), channel_id=1, source_target_pairs={{0,12},{1,13},{2,14},{3,15},{4,8},{5,9},{6,10},{7,11},{8,4},{9,5},... | collective-permute-start | bytes 540680 | tf_op jit(solution)/shard_map/ppermute | solution.py:724
  31.9 20.0 %copy-start.18 = (bf16[64,1408]{1,0:T(8,128)(2,1)}, bf16[64,1408]{1,0:T(8,128)(2,1)S(1)}, u32[]{:S(2)}) copy-start(bf16[64,1408]{1,0:T(8,128)(2,1)S(1)} %collective-permute-done.4.rest_8_) | copy-start | bytes 540676
  31.9 5.5 %collective-permute-start.11 = (bf16[64,1408]{1,0:T(8,128)(2,1)S(1)}, bf16[64,1408]{1,0:T(8,128)(2,1)S(1)}, u32[]{:S(2)}, u32[]{:S(2)}) collective-permute-start(bf16[64,1408]{1,0:T(8,128)(2,1)S(1)} %collective-permute-done.4.rest_8_), channel_id=1, source_target_pairs={{0,2},{1,3},{2,0},{3,1},{4,6},{5,7},{6,4},{7,5},{8,10},{9,11},{10,... | collective-permute-start | bytes 540680 | tf_op jit(solution)/shard_map/ppermute | solution.py:724
  37.3 14.6 %copy-start.19 = (bf16[64,1408]{1,0:T(8,128)(2,1)}, bf16[64,1408]{1,0:T(8,128)(2,1)S(1)}, u32[]{:S(2)}) copy-start(bf16[64,1408]{1,0:T(8,128)(2,1)S(1)} %collective-permute-done.10.rest_15_) | copy-start | bytes 540676
  37.4 14.5 %copy-start.20 = (bf16[64,1408]{1,0:T(8,128)(2,1)}, bf16[64,1408]{1,0:T(8,128)(2,1)S(1)}, u32[]{:S(2)}) copy-start(bf16[64,1408]{1,0:T(8,128)(2,1)S(1)} %collective-permute-done.11.rest_10_) | copy-start | bytes 540676
  38.4 13.6 %copy-start.12 = (bf16[64,2432]{1,0:T(8,128)(2,1)}, bf16[64,2432]{1,0:T(8,128)(2,1)S(1)}, u32[]{:S(2)}) copy-start(bf16[64,2432]{1,0:T(8,128)(2,1)S(1)} %collective-permute-done.9.rest_13_.rest_25_.rest_9_) | copy-start | bytes 933892
  38.5 13.4 %collective-permute-start.12 = (bf16[544,1024]{1,0:T(8,128)(2,1)S(1)}, bf16[544,1024]{1,0:T(8,128)(2,1)S(1)}, u32[]{:S(2)}, u32[]{:S(2)}) collective-permute-start(bf16[544,1024]{1,0:T(8,128)(2,1)S(1)} %pad_maximum_fusion), channel_id=1, source_target_pairs={{0,16},{16,0},{1,17},{17,1},{2,18},{18,2},{3,19},{19,3},{4,20},{20... | collective-permute-start | bytes 3342344 | tf_op jit(solution)/shard_map/ppermute | solution.py:727
  39.0 7.4 %collective-permute-start.14 = (bf16[64,1408]{1,0:T(8,128)(2,1)S(1)}, bf16[64,1408]{1,0:T(8,128)(2,1)S(1)}, u32[]{:S(2)}, u32[]{:S(2)}) collective-permute-start(bf16[64,1408]{1,0:T(8,128)(2,1)S(1)} %collective-permute-done.10.rest_15_), channel_id=1, source_target_pairs={{0,1},{1,0},{2,3},{3,2},{4,5},{5,4},{6,7},{7,6},{8,9},{9,8},{10,11... | collective-permute-start | bytes 540680 | tf_op jit(solution)/shard_map/ppermute | solution.py:724
  41.0 10.9 %collective-permute-start.13 = (bf16[64,2432]{1,0:T(8,128)(2,1)S(1)}, bf16[64,2432]{1,0:T(8,128)(2,1)S(1)}, u32[]{:S(2)}, u32[]{:S(2)}) collective-permute-start(bf16[64,2432]{1,0:T(8,128)(2,1)S(1)} %collective-permute-done.8.rest_12_.rest_24_.rest_8_), channel_id=1, source_target_pairs={{0,2},{1,3},{2,0},{3,1},{4,6},{5,7},{6,4},{7,5},{8,10},{9,11},{10,... | collective-permute-start | bytes 933896 | tf_op jit(solution)/shard_map/ppermute | solution.py:724
  41.2 8.6 %collective-permute-start.15 = (bf16[64,1408]{1,0:T(8,128)(2,1)S(1)}, bf16[64,1408]{1,0:T(8,128)(2,1)S(1)}, u32[]{:S(2)}, u32[]{:S(2)}) collective-permute-start(bf16[64,1408]{1,0:T(8,128)(2,1)S(1)} %collective-permute-done.10.rest_15_), channel_id=1, source_target_pairs={{0,2},{1,3},{2,0},{3,1},{4,6},{5,7},{6,4},{7,5},{8,10},{9,11},{10,... | collective-permute-start | bytes 540680 | tf_op jit(solution)/shard_map/ppermute | solution.py:724
  46.4 5.5 %collective-permute-start.16 = (bf16[64,1408]{1,0:T(8,128)(2,1)S(1)}, bf16[64,1408]{1,0:T(8,128)(2,1)S(1)}, u32[]{:S(2)}, u32[]{:S(2)}) collective-permute-start(bf16[64,1408]{1,0:T(8,128)(2,1)S(1)} %collective-permute-done.14.rest_16_), channel_id=1, source_target_pairs={{0,2},{1,3},{2,0},{3,1},{4,6},{5,7},{6,4},{7,5},{8,10},{9,11},{10,... | collective-permute-start | bytes 540680 | tf_op jit(solution)/shard_map/ppermute | solution.py:724
  67.2 3.9 %collective-permute-start.17 = (f32[8,128]{1,0:T(8,128)}, f32[8,128]{1,0:T(8,128)S(1)}, u32[]{:S(2)}, u32[]{:S(2)}) collective-permute-start(f32[8,128]{1,0:T(8,128)} %get-tuple-element.74), channel_id=1, source_target_pairs={{0,4},{1,5},{2,6},{3,7},{4,0},{5,1},{6,2},{7,3},{8,12},{9,13},{10,... | collective-permute-start | bytes 12296 | tf_op jit(solution)/shard_map/ppermute | solution.py:724
  71.8 1.2 collective-permute-start.18
  79.9 27.4 %collective-permute-start.19 = (bf16[256,1024]{1,0:T(8,128)(2,1)}, bf16[256,1024]{1,0:T(8,128)(2,1)S(1)}, u32[]{:S(2)}, u32[]{:S(2)}) collective-permute-start(bf16[256,1024]{1,0:T(8,128)(2,1)} %get-tuple-element.78), channel_id=1, source_target_pairs={{0,4},{1,5},{2,6},{3,7},{4,0},{5,1},{6,2},{7,3},{8,12},{9,13},{10,... | collective-permute-start | bytes 1572872 | tf_op jit(solution)/shard_map/ppermute | solution.py:724
  80.4 26.9 %collective-permute-start.22 = (bf16[128,1024]{1,0:T(8,128)(2,1)}, bf16[128,1024]{1,0:T(8,128)(2,1)S(1)}, u32[]{:S(2)}, u32[]{:S(2)}) collective-permute-start(bf16[128,1024]{1,0:T(8,128)(2,1)} %get-tuple-element.87), channel_id=1, source_target_pairs={{0,1},{1,0},{2,3},{3,2},{4,5},{5,4},{6,7},{7,6},{8,9},{9,8},{10,11... | collective-permute-start | bytes 786440 | tf_op jit(solution)/shard_map/ppermute | solution.py:724
  82.1 25.2 %collective-permute-start.23 = (bf16[128,1024]{1,0:T(8,128)(2,1)}, bf16[128,1024]{1,0:T(8,128)(2,1)S(1)}, u32[]{:S(2)}, u32[]{:S(2)}) collective-permute-start(bf16[128,1024]{1,0:T(8,128)(2,1)} %get-tuple-element.79), channel_id=1, source_target_pairs={{0,2},{1,3},{2,0},{3,1},{4,6},{5,7},{6,4},{7,5},{8,10},{9,11},{10,... | collective-permute-start | bytes 786440 | tf_op jit(solution)/shard_map/ppermute | solution.py:724
  82.1 25.2 %collective-permute-start.24 = (bf16[128,1024]{1,0:T(8,128)(2,1)}, bf16[128,1024]{1,0:T(8,128)(2,1)S(1)}, u32[]{:S(2)}, u32[]{:S(2)}) collective-permute-start(bf16[128,1024]{1,0:T(8,128)(2,1)} %get-tuple-element.88), channel_id=1, source_target_pairs={{0,3},{1,2},{2,1},{3,0},{4,7},{5,6},{6,5},{7,4},{8,11},{9,10},{10,... | collective-permute-start | bytes 786440 | tf_op jit(solution)/shard_map/ppermute | solution.py:724
  83.9 24.5 %copy-start.28 = (bf16[128,1024]{1,0:T(8,128)(2,1)S(1)}, bf16[128,1024]{1,0:T(8,128)(2,1)}, u32[]{:S(2)}) copy-start(bf16[128,1024]{1,0:T(8,128)(2,1)} %get-tuple-element.97) | copy-start | bytes 786436
  107.3 12.5 %collective-permute-start.25 = (bf16[144,2816]{1,0:T(8,128)(2,1)}, bf16[144,2816]{1,0:T(8,128)(2,1)S(1)}, u32[]{:S(2)}, u32[]{:S(2)}) collective-permute-start(bf16[144,2816]{1,0:T(8,128)(2,1)} %get-tuple-element.89), channel_id=1, source_target_pairs={{0,2},{1,3},{2,0},{3,1},{4,6},{5,7},{6,4},{7,5},{8,10},{9,11},{10,... | collective-permute-start | bytes 2433032 | tf_op jit(solution)/shard_map/ppermute | solution.py:724
  108.6 11.4 %collective-permute-start.29 = (bf16[64,1024]{1,0:T(8,128)(2,1)S(1)}, bf16[64,1024]{1,0:T(8,128)(2,1)S(1)}, u32[]{:S(2)}, u32[]{:S(2)}) collective-permute-start(bf16[64,1024]{1,0:T(8,128)(2,1)S(1)} %slice.241), channel_id=1, source_target_pairs={{0,8},{1,9},{2,10},{3,11},{4,12},{5,13},{6,14},{7,15},{8,0},{9,1},... | collective-permute-start | bytes 393224 | tf_op jit(solution)/shard_map/ppermute | solution.py:724
  111.7 12.1 %collective-permute-start.20 = (f32[128,1024]{1,0:T(8,128)S(1)}, f32[128,1024]{1,0:T(8,128)S(1)}, u32[]{:S(2)}, u32[]{:S(2)}) collective-permute-start(f32[128,1024]{1,0:T(8,128)S(1)} %slice_add_fusion.2), channel_id=1, source_target_pairs={{0,16},{16,0},{1,17},{17,1},{2,18},{18,2},{3,19},{19,3},{4,20},{20... | collective-permute-start | bytes 1572872 | tf_op jit(solution)/shard_map/ppermute | solution.py:727
  120.1 12.9 %collective-permute-start.30 = (bf16[80,2816]{1,0:T(8,128)(2,1)S(1)}, bf16[80,2816]{1,0:T(8,128)(2,1)S(1)}, u32[]{:S(2)}, u32[]{:S(2)}) collective-permute-start(bf16[80,2816]{1,0:T(8,128)(2,1)S(1)} %fusion.6), channel_id=1, source_target_pairs={{0,1},{1,0},{2,3},{3,2},{4,5},{5,4},{6,7},{7,6},{8,9},{9,8},{10,11... | collective-permute-start | bytes 1351688 | tf_op jit(solution)/shard_map/ppermute | solution.py:724
  121.9 17.9 %collective-permute-start.21 = (bf16[256,1024]{1,0:T(8,128)(2,1)S(1)}, bf16[256,1024]{1,0:T(8,128)(2,1)S(1)}, u32[]{:S(2)}, u32[]{:S(2)}) collective-permute-start(bf16[256,1024]{1,0:T(8,128)(2,1)S(1)} %copy-done.30), channel_id=1, source_target_pairs={{0,4},{1,5},{2,6},{3,7},{4,0},{5,1},{6,2},{7,3},{8,12},{9,13},{10,... | collective-permute-start | bytes 1572872 | tf_op jit(solution)/shard_map/ppermute | solution.py:724
  124.7 11.6 %collective-permute-start.26 = (bf16[128,2816]{1,0:T(8,128)(2,1)S(1)}, bf16[128,2816]{1,0:T(8,128)(2,1)S(1)}, u32[]{:S(2)}, u32[]{:S(2)}) collective-permute-start(bf16[128,2816]{1,0:T(8,128)(2,1)S(1)} %copy-done.29), channel_id=1, source_target_pairs={{0,2},{1,3},{2,0},{3,1},{4,6},{5,7},{6,4},{7,5},{8,10},{9,11},{10,... | collective-permute-start | bytes 2162696 | tf_op jit(solution)/shard_map/ppermute | solution.py:724
  133.2 15.6 %collective-permute-start.31 = (bf16[64,2816]{1,0:T(8,128)(2,1)S(1)}, bf16[64,2816]{1,0:T(8,128)(2,1)S(1)}, u32[]{:S(2)}, u32[]{:S(2)}) collective-permute-start(bf16[64,2816]{1,0:T(8,128)(2,1)S(1)} %add_convert_fusion), channel_id=1, source_target_pairs={{0,8},{1,9},{2,10},{3,11},{4,12},{5,13},{6,14},{7,15},{8,0},{9,1},... | collective-permute-start | bytes 1081352 | tf_op jit(solution)/shard_map/ppermute | solution.py:724
  136.3 12.4 %collective-permute-start.33 = (f32[8,896]{1,0:T(8,128)S(1)}, f32[8,896]{1,0:T(8,128)S(1)}, u32[]{:S(2)}, u32[]{:S(2)}) collective-permute-start(f32[8,896]{1,0:T(8,128)S(1)} %fusion.8), channel_id=1, source_target_pairs={{0,4},{1,5},{2,6},{3,7},{4,0},{5,1},{6,2},{7,3},{8,12},{9,13},{10,... | collective-permute-start | bytes 86024 | tf_op jit(solution)/shard_map/ppermute | solution.py:724
  136.4 12.2 %collective-permute-start.34 = (f32[8,896]{1,0:T(8,128)S(1)}, f32[8,896]{1,0:T(8,128)S(1)}, u32[]{:S(2)}, u32[]{:S(2)}) collective-permute-start(f32[8,896]{1,0:T(8,128)S(1)} %fusion.8), channel_id=1, source_target_pairs={{0,12},{1,13},{2,14},{3,15},{4,8},{5,9},{6,10},{7,11},{8,4},{9,5},... | collective-permute-start | bytes 86024 | tf_op jit(solution)/shard_map/ppermute | solution.py:724
  138.5 10.2 %collective-permute-start.32 = (f32[8,896]{1,0:T(8,128)S(1)}, f32[8,896]{1,0:T(8,128)S(1)}, u32[]{:S(2)}, u32[]{:S(2)}) collective-permute-start(f32[8,896]{1,0:T(8,128)S(1)} %fusion.8), channel_id=1, source_target_pairs={{0,8},{1,9},{2,10},{3,11},{4,12},{5,13},{6,14},{7,15},{8,0},{9,1},... | collective-permute-start | bytes 86024 | tf_op jit(solution)/shard_map/ppermute | solution.py:724
  140.2 2.0 %collective-permute-start.27 = (f32[128,1024]{1,0:T(8,128)S(1)}, f32[128,1024]{1,0:T(8,128)S(1)}, u32[]{:S(2)}, u32[]{:S(2)}) collective-permute-start(f32[128,1024]{1,0:T(8,128)S(1)} %get-tuple-element.113), channel_id=1, source_target_pairs={{0,16},{16,0},{1,17},{17,1},{2,18},{18,2},{3,19},{19,3},{4,20},{20... | collective-permute-start | bytes 1572872 | tf_op jit(solution)/shard_map/ppermute | solution.py:727
  143.2 7.4 %collective-permute-start.28 = (bf16[64,2816]{1,0:T(8,128)(2,1)S(1)}, bf16[64,2816]{1,0:T(8,128)(2,1)S(1)}, u32[]{:S(2)}, u32[]{:S(2)}) collective-permute-start(bf16[64,2816]{1,0:T(8,128)(2,1)S(1)} %add_convert_fusion.2), channel_id=1, source_target_pairs={{0,1},{1,0},{2,3},{3,2},{4,5},{5,4},{6,7},{7,6},{8,9},{9,8},{10,11... | collective-permute-start | bytes 1081352 | tf_op jit(solution)/shard_map/ppermute | solution.py:724
  148.7 2.1 %collective-permute-start.35 = (f32[8,1792]{1,0:T(8,128)S(1)}, f32[8,1792]{1,0:T(8,128)S(1)}, u32[]{:S(2)}, u32[]{:S(2)}) collective-permute-start(f32[8,1792]{1,0:T(8,128)S(1)} %pad_maximum_fusion.2.small_mine_ref), channel_id=1, source_target_pairs={{0,16},{16,0},{1,17},{17,1},{2,18},{18,2},{3,19},{19,3},{4,20},{20... | collective-permute-start | bytes 172040 | tf_op jit(solution)/shard_map/ppermute | solution.py:727
  150.8 5.8 %collective-permute-start.36 = (bf16[64,1408]{1,0:T(8,128)(2,1)S(1)}, bf16[64,1408]{1,0:T(8,128)(2,1)S(1)}, u32[]{:S(2)}, u32[]{:S(2)}) collective-permute-start(bf16[64,1408]{1,0:T(8,128)(2,1)S(1)} %slice_add_fusion.4), channel_id=1, source_target_pairs={{0,4},{1,5},{2,6},{3,7},{4,0},{5,1},{6,2},{7,3},{8,12},{9,13},{10,... | collective-permute-start | bytes 540680 | tf_op jit(solution)/shard_map/ppermute | solution.py:724
  156.7 2.6 %collective-permute-start.37 = (f32[64,3840]{1,0:T(8,128)S(1)}, f32[64,3840]{1,0:T(8,128)S(1)}, u32[]{:S(2)}, u32[]{:S(2)}) collective-permute-start(f32[64,3840]{1,0:T(8,128)S(1)} %pad_maximum_fusion.1.mine_ref), channel_id=1, source_target_pairs={{0,16},{16,0},{1,17},{17,1},{2,18},{18,2},{3,19},{19,3},{4,20},{20... | collective-permute-start | bytes 2949128 | tf_op jit(solution)/shard_map/ppermute | solution.py:727
  (21 other events, 106.8 us)
